TPU v7x, 32 devices: a whole 2x2x4 slice. The times are simulated.
32 devices in a mesh: space: 8 (over z, x), sample: 4 (over y, core).
Axes of the slice: x: 2, y: 2, z: 4, core: 2. Of those that a mesh axis runs over, the one named last changes fastest.
Arguments:
- state_hat: float32 [20, 3, 64, 32, 128], P('sample', None, 'space'), may hold values from -2.4 to 2.4
- adjoint_hat: float32 [20, 3, 64, 32, 128], P('sample', None, 'space'), may hold values from -2.4 to 2.4
- objective_hat: float32 [20, 3, 64, 32, 128], P('sample', None, 'space'), may hold values from -6 to 6
- density: float32 [64, 32, 128], P('space'), may hold values from 0.05 to 1
- region: int32 [64, 32, 128], P('space'), may hold values from 0 to 3
Outputs:
- adjoint_residual: float32 [20, 3, 64, 32, 128], P('sample', None, 'space')
- density_gradient: float32 [64, 32, 128], P('space', 'sample')
All inputs are finite; a program needn't handle non-finite values.
Results may differ from a plain program's by a relative error of at most 0.00026.
Values sent between devices are 32-bit elements; how exact they have to be, the bound alone decides.
No kernel may reach another device: no remote copies, remote signals or barrier semaphores. Data moves between devices by JAX's collectives and lax.ppermute only.
A program may use at most 128 MiB of HBM per device.

v0:
```python
import math

import jax
import jax.numpy as jnp
from jax import lax
from jax.sharding import PartitionSpec as P

NCOEF = 20
NT = 40


magnet_reluct = 0.95
iron_floor = 0.05
saturation = 1.0


def passed_along(array, axis, by):
    size = lax.axis_size(axis)
    pairs = [(i, i + by) for i in range(size) if 0 <= i + by < size]
    return lax.ppermute(array, axis, pairs)


def harmonic_table():
    sample_steps = jnp.arange(NT, dtype=jnp.int32).astype(jnp.float32)
    orders = (jnp.arange(NCOEF // 2, dtype=jnp.int32) + 1).astype(jnp.float32)
    angles = 2.0 * math.pi / NT * sample_steps[:, None] * orders[None, :]
    return jnp.stack([jnp.cos(angles), jnp.sin(angles)], axis=2).reshape(NT, NCOEF)


def forward_diff(potential, along):
    length = potential.shape[along]
    widths = [(0, 0)] * potential.ndim
    widths[along] = (0, 1)
    padded = jnp.pad(potential, widths)
    return lax.slice_in_dim(padded, 1, length + 1, axis=along) - potential


def backward_diff(potential, along):
    length = potential.shape[along]
    widths = [(0, 0)] * potential.ndim
    widths[along] = (1, 0)
    padded = jnp.pad(potential, widths)
    return lax.slice_in_dim(padded, 0, length, axis=along) - potential


def curl_quarter(potential, x_upper, y_upper):
    x_step = jnp.concatenate([potential[:, :, 1:], x_upper], axis=2) - potential
    y_step = jnp.concatenate([potential[:, :, :, 1:], y_upper], axis=3) - potential
    part_one, part_two = (potential[:, 0], potential[:, 1])
    flux_one = y_step[:, 2] - forward_diff(part_two, 3)
    flux_two = forward_diff(part_one, 3) - x_step[:, 2]
    flux_three = x_step[:, 1] - y_step[:, 0]
    return jnp.stack([flux_one, flux_two, flux_three], axis=1)


def curl_back_quarter(field_h, x_lower, y_lower):
    x_step = jnp.concatenate([x_lower, field_h[:, 1:3, :-1]], axis=2) - field_h[:, 1:3]
    y_parts = jnp.stack([field_h[:, 0], field_h[:, 2]], axis=1)
    y_step = jnp.concatenate([y_lower, y_parts[:, :, :, :-1]], axis=3) - y_parts
    back_one = backward_diff(field_h[:, 1], 3) - y_step[:, 1]
    back_two = x_step[:, 1] - backward_diff(field_h[:, 0], 3)
    back_three = y_step[:, 0] - x_step[:, 0]
    return jnp.stack([back_one, back_two, back_three], axis=1)


def material(density, region):
    iron_share = jnp.where(region == 0, density**3, jnp.zeros_like(density))
    iron_slope = jnp.where(region == 0, 3.0 * density**2, jnp.zeros_like(density))
    base_reluct = jnp.where(
        region == 1, magnet_reluct * jnp.ones_like(density), jnp.ones_like(density)
    )
    return (iron_share, iron_slope, base_reluct)


def reluctivity(state_flux, adjoint_flux, base_reluct, iron_share):
    flux_square = jnp.sum(state_flux * state_flux, axis=1)
    flux_inner = jnp.sum(state_flux * adjoint_flux, axis=1)
    iron_curve = iron_floor + (1.0 - iron_floor) * flux_square / (flux_square + saturation)
    curve_slope = (1.0 - iron_floor) * saturation / (flux_square + saturation) ** 2
    reluct_now = base_reluct + iron_share * (iron_curve - 1.0)
    reluct_slope = iron_share * curve_slope
    field_h = (
        reluct_now[:, None] * adjoint_flux + (2.0 * reluct_slope * flux_inner)[:, None] * state_flux
    )
    return (field_h, iron_curve, flux_inner)


def local(state_hat, adjoint_hat, objective_hat, density, region):
    harm_table = harmonic_table()
    groups = lax.axis_size("sample")
    planes = state_hat.shape[2]
    iron_share, iron_slope, base_reluct = material(density, region)
    quarter = density.shape[1] // groups
    first_row = lax.axis_index("sample") * quarter
    share_q = lax.dynamic_slice_in_dim(iron_share, first_row, quarter, 1)
    slope_q = lax.dynamic_slice_in_dim(iron_slope, first_row, quarter, 1)
    base_q = lax.dynamic_slice_in_dim(base_reluct, first_row, quarter, 1)
    state_cells, adjoint_cells = (
        lax.all_to_all(state_hat, "sample", split_axis=3, concat_axis=0, tiled=True),
        lax.all_to_all(adjoint_hat, "sample", split_axis=3, concat_axis=0, tiled=True),
    )
    state_time = jnp.tensordot(harm_table, state_cells, axes=1, precision=lax.Precision.HIGHEST)
    adjoint_time = jnp.tensordot(harm_table, adjoint_cells, axes=1, precision=lax.Precision.HIGHEST)
    both_time = jnp.concatenate([state_time, adjoint_time], axis=1)
    x_upper = passed_along(both_time[:, :, :1], "space", -1)
    y_upper = passed_along(both_time[:, :, :, :1], "sample", -1)
    state_flux = curl_quarter(state_time, x_upper[:, :3], y_upper[:, :3])
    adjoint_flux = curl_quarter(adjoint_time, x_upper[:, 3:], y_upper[:, 3:])
    field_h, iron_curve, flux_inner = reluctivity(state_flux, adjoint_flux, base_q, share_q)
    x_lower = passed_along(field_h[:, 1:3, planes - 1 :], "space", 1)
    last_rows = jnp.stack(
        [field_h[:, 0, :, quarter - 1 :], field_h[:, 2, :, quarter - 1 :]], axis=1
    )
    y_lower = passed_along(last_rows, "sample", 1)
    back_field = curl_back_quarter(field_h, x_lower, y_lower)
    coef_values = (
        2.0 / NT * jnp.tensordot(harm_table.T, back_field, axes=1, precision=lax.Precision.HIGHEST)
    )
    summed = lax.all_to_all(coef_values, "sample", split_axis=0, concat_axis=3, tiled=True)
    adjoint_residual = objective_hat - summed
    density_gradient = -(1.0 / NT) * jnp.sum(slope_q * (iron_curve - 1.0) * flux_inner, axis=0)
    return (adjoint_residual, density_gradient)


def solution(mesh):
    in_specs = (
        P("sample", None, "space", None, None),
        P("sample", None, "space", None, None),
        P("sample", None, "space", None, None),
        P("space", None, None),
        P("space", None, None),
    )
    out_specs = (P("sample", None, "space", None, None), P("space", "sample", None))
    return jax.shard_map(local, mesh=mesh, in_specs=in_specs, out_specs=out_specs, check_vma=False)
```

profile of v0, /device:TPU:0, one launch (start us, length us, event | category | flops | bytes accessed | tf_op | source)
XLA Modules:
  0.0 166.3 jit_solution(3846367425839377877)
XLA Ops:
  0.6 4.0 %copy.19 = f32[5,3,8,32,128]{4,2,1,0,3:T(8,128)} copy(f32[5,3,8,32,128]{4,3,2,1,0:T(8,128)} %param.5) | data formatting | bytes 3932160 | tf_op args[0]
  4.6 4.2 %all-to-all-start = ((f32[5,3,8,32,128]{4,2,1,0,3:T(8,128)}), f32[5,3,8,32,128]{4,2,1,0,3:T(8,128)S(1)}, u32[]{:S(2)}, u32[]{:S(2)}) async-start(f32[5,3,8,32,128]{4,2,1,0,3:T(8,128)} %copy.19), calls=%async_computation | async-start | bytes 3932160 | tf_op jit(solution)/shard_map/all_to_all | solution.py:99
  8.8 4.0 %copy.23 = f32[5,3,8,32,128]{4,2,1,0,3:T(8,128)} copy(f32[5,3,8,32,128]{4,3,2,1,0:T(8,128)} %param.6) | data formatting | bytes 3932160 | tf_op args[1]
  12.8 20.3 %all-to-all-done = f32[5,3,8,32,128]{4,2,1,0,3:T(8,128)S(1)} async-done(((f32[5,3,8,32,128]{4,2,1,0,3:T(8,128)}), f32[5,3,8,32,128]{4,2,1,0,3:T(8,128)S(1)}, u32[]{:S(2)}, u32[]{:S(2)}) %all-to-all-start) | async-done | bytes 1966112 | tf_op jit(solution)/shard_map/all_to_all | solution.py:99
  33.1 4.6 %all-to-all-start.1 = ((f32[5,3,8,32,128]{4,2,1,0,3:T(8,128)}), f32[5,3,8,32,128]{4,2,1,0,3:T(8,128)}, u32[]{:S(2)}, u32[]{:S(2)}) async-start(f32[5,3,8,32,128]{4,2,1,0,3:T(8,128)} %copy.23), calls=%async_computation.1 | async-start | bytes 3932160 | tf_op jit(solution)/shard_map/all_to_all | solution.py:100
  37.8 0.2 multiply_cosine_fusion
  38.0 2.0 %copy.21 = f32[4,5,3,8,8,128]{5,4,3,2,1,0:T(8,128)S(1)} copy(f32[4,5,3,8,8,128]{5,3,2,1,4,0:T(8,128)} %bitcast.72) | data formatting | bytes 3932160 | tf_op jit(solution)/shard_map/all_to_all | solution.py:99
  40.0 21.9 %all-to-all-done.1 = f32[5,3,8,32,128]{4,2,1,0,3:T(8,128)} async-done(((f32[5,3,8,32,128]{4,2,1,0,3:T(8,128)}), f32[5,3,8,32,128]{4,2,1,0,3:T(8,128)}, u32[]{:S(2)}, u32[]{:S(2)}) %all-to-all-start.1) | async-done | bytes 1966112 | tf_op jit(solution)/shard_map/all_to_all | solution.py:100
  61.9 2.0 %copy.25 = f32[4,5,3,8,8,128]{5,4,3,2,1,0:T(8,128)S(1)} copy(f32[4,5,3,8,8,128]{5,3,2,1,4,0:T(8,128)} %bitcast.7) | data formatting | bytes 3932160 | tf_op jit(solution)/shard_map/all_to_all | solution.py:100
  63.9 4.6 %fusion.9 = f32[40,3,8,8,128]{4,0,3,2,1:T(8,128)S(1)} fusion(f32[20,3,8,8,128]{4,3,2,1,0:T(8,128)S(1)} %bitcast.70, f32[40,20,1,1,1]{0,1,2,3,4:T(8,128)S(1)} %reshape.128), kind=kOutput, calls=%fused_computation.28 | convolution fusion | flops 235929600 | bytes 5901440 | tf_op jit(solution)/shard_map/dot_general | solution.py:102
  68.5 4.6 %fusion.7 = f32[40,3,8,8,128]{4,0,3,2,1:T(8,128)S(1)} fusion(f32[20,3,8,8,128]{4,3,2,1,0:T(8,128)S(1)} %bitcast.71, f32[40,20,1,1,1]{0,1,2,3,4:T(8,128)S(1)} %reshape.128), kind=kOutput, calls=%fused_computation.26 | convolution fusion | flops 235929600 | bytes 5901440 | tf_op jit(solution)/shard_map/dot_general | solution.py:103
  73.2 1.8 %copy-done.3 = f32[40,3,8,8,128]{4,0,3,2,1:T(8,128)} copy-done((f32[40,3,8,8,128]{4,0,3,2,1:T(8,128)}, f32[40,3,8,8,128]{4,0,3,2,1:T(8,128)S(1)}, u32[]{:S(2)}) %copy-start.3) | copy-done | bytes 3932184
  75.0 1.3 collective-permute-start.1
  76.4 1.3 pad_maximum_fusion.4
  77.6 1.5 collective-permute-start
  79.2 0.6 multiply_select_fusion
  79.8 2.1 %copy-done.4 = f32[40,3,8,8,128]{4,0,3,2,1:T(8,128)S(1)} copy-done((f32[40,3,8,8,128]{4,0,3,2,1:T(8,128)S(1)}, f32[40,3,8,8,128]{4,0,3,2,1:T(8,128)}, u32[]{:S(2)}) %copy-start.4) | copy-done | bytes 3932184
  81.9 1.7 %slice_bitcast_fusion.5 = (f32[40,8,8,128]{3,0,2,1:T(8,128)}, f32[40,8,8,128]{3,0,2,1:T(8,128)}) fusion(f32[40,3,8,8,128]{4,0,3,2,1:T(8,128)S(1)} %copy-done.4), kind=kLoop, calls=%fused_computation.58 | loop fusion | bytes 5242880 | tf_op jit(solution)/shard_map/squeeze | solution.py:49
  83.6 2.2 %copy-done.1 = f32[40,3,8,8,128]{4,0,3,2,1:T(8,128)S(1)} copy-done((f32[40,3,8,8,128]{4,0,3,2,1:T(8,128)S(1)}, f32[40,3,8,8,128]{4,0,3,2,1:T(8,128)}, u32[]{:S(2)}) %copy-start.1) | copy-done | bytes 3932184
  85.8 1.8 %slice_bitcast_fusion.9 = (f32[40,8,8,128]{3,0,2,1:T(8,128)}, f32[40,8,8,128]{3,0,2,1:T(8,128)}) fusion(f32[40,3,8,8,128]{4,0,3,2,1:T(8,128)S(1)} %copy-done.1), kind=kLoop, calls=%fused_computation.63 | loop fusion | bytes 5242880 | tf_op jit(solution)/shard_map/squeeze | solution.py:49
  87.5 13.2 %collective-permute-done.1 = f32[40,6,1,8,128]{4,0,3,2,1:T(8,128)S(1)} collective-permute-done((f32[40,6,1,8,128]{4,0,3,2,1:T(8,128)S(1)}, f32[40,6,1,8,128]{4,0,3,2,1:T(8,128)S(1)}, u32[]{:S(2)}, u32[]{:S(2)}) %collective-permute-start.1) | collective-permute-done | bytes 983072 | tf_op jit(solution)/shard_map/ppermute | solution.py:20
  100.8 1.1 fusion.41
  101.9 5.1 %maximum_subtract_fusion.1 = (f32[40,3,8,8,128]{4,0,3,2,1:T(8,128)S(1)}, f32[40,3,8,8,128]{4,0,3,2,1:T(8,128)S(1)}, f32[40,3,8,8,128]{4,0,3,2,1:T(8,128)}, f32[40,3,8,8,128]{4,0,3,2,1:T(8,128)}) fusion(f32[40,3,8,8,128]{4,0,3,2,1:T(8,128)S(1)} %copy-done.2, f32[40,3,1,8,128]{4,0,3,2,1:T(8,128)S(1)} %get-tuple-element.21, ...), kind=kLoop, calls=%fused_computation.1 | loop fusion | flops 7864320 | bytes 39321600 | tf_op jit(solution)/shard_map/sub | solution.py:47
  107.0 2.7 %fusion.26 = f32[40,1,8,8,128]{4,0,3,2,1:T(8,128)S(1)} fusion(f32[40,8,8,128]{3,0,2,1:T(8,128)} %get-tuple-element.15, f32[40,3,8,8,128]{4,0,3,2,1:T(8,128)} %get-tuple-element.30), kind=kLoop, calls=%fused_computation.44 | loop fusion | flops 655360 | bytes 3932160 | tf_op jit(solution)/shard_map/stack | solution.py:53
  109.7 0.6 copy-done.5
  110.3 1.6 slice_subtract_fusion.2
  112.0 0.4 fusion.23
  112.4 0.9 copy-done.8
  113.3 0.4 fusion.20
  113.9 1.2 copy-done.7
  115.1 0.4 fusion.17
  115.5 1.2 multiply_reduce_fusion.1
  116.7 0.9 multiply_reduce_fusion.2
  117.6 0.7 multiply_add_fusion
  118.4 0.7 slice_bitcast_fusion.2
  119.1 4.6 %collective-permute-start.3 = (f32[40,2,1,8,128]{4,0,3,2,1:T(8,128)S(1)}, f32[40,2,1,8,128]{4,0,3,2,1:T(8,128)S(1)}, u32[]{:S(2)}, u32[]{:S(2)}) collective-permute-start(f32[40,2,1,8,128]{4,0,3,2,1:T(8,128)S(1)} %slice.193), channel_id=1, source_target_pairs={{0,4},{4,8},{8,12},{12,16},{16,20},{20,24},{24,28},{1,5},{5,9},{9,... | collective-permute-start | bytes 983048 | tf_op jit(solution)/shard_map/ppermute | solution.py:20
  123.9 1.3 collective-permute-start.2
  125.4 4.1 %collective-permute-done.3 = f32[40,2,1,8,128]{4,0,3,2,1:T(8,128)S(1)} collective-permute-done((f32[40,2,1,8,128]{4,0,3,2,1:T(8,128)S(1)}, f32[40,2,1,8,128]{4,0,3,2,1:T(8,128)S(1)}, u32[]{:S(2)}, u32[]{:S(2)}) %collective-permute-start.3) | collective-permute-done | bytes 327712 | tf_op jit(solution)/shard_map/ppermute | solution.py:20
  129.5 0.3 slice_subtract_fusion
  129.8 0.4 fusion.32
  130.2 0.3 fusion.6
  130.7 0.4 fusion.29
  131.1 2.3 %fusion.12 = f32[20,3,8,8,128]{4,0,3,2,1:T(8,128)S(1)} fusion(f32[40,1,8,8,128]{4,0,3,2,1:T(8,128)S(1)} %slice_subtract_fusion.1, f32[40,1,8,8,128]{4,0,3,2,1:T(8,128)S(1)} %fusion.32, f32[40,1,8,8,128]{4,0,3,2,1:T(8,128)S(1)} %fusion.29, f32[40,20,1,1,1]{0,1,2,3,4:T(8,128)S(1)} %reshape.128), kind=kOutput, calls=%fused_computation.32 | convolution fusion | flops 238387200 | bytes 5901440 | tf_op jit(solution)/shard_map/dot_general | solution.py:117
  133.4 1.6 copy.27
  135.0 3.9 %all-to-all-start.2 = ((f32[20,3,8,8,128]{4,3,2,1,0:T(8,128)}), f32[20,3,8,8,128]{4,3,2,1,0:T(8,128)S(1)}, u32[]{:S(2)}, u32[]{:S(2)}) async-start(f32[20,3,8,8,128]{4,3,2,1,0:T(8,128)} %copy.27), calls=%async_computation.2 | async-start | bytes 3932160 | tf_op jit(solution)/shard_map/all_to_all | solution.py:119
  138.9 0.6 broadcast_multiply_fusion
  139.5 23.7 %all-to-all-done.2 = f32[20,3,8,8,128]{4,3,2,1,0:T(8,128)S(1)} async-done(((f32[20,3,8,8,128]{4,3,2,1,0:T(8,128)}), f32[20,3,8,8,128]{4,3,2,1,0:T(8,128)S(1)}, u32[]{:S(2)}, u32[]{:S(2)}) %all-to-all-start.2) | async-done | bytes 1966112 | tf_op jit(solution)/shard_map/all_to_all | solution.py:119
  163.2 3.1 %bitcast_subtract_fusion = f32[5,3,8,32,128]{4,3,2,1,0:T(8,128)} fusion(f32[5,3,8,32,128]{4,3,2,1,0:T(8,128)} %param.7, f32[5,3,8,4,8,128]{5,4,2,1,0,3:T(8,128)S(1)} %bitcast.73), kind=kLoop, calls=%fused_computation.31 | loop fusion | flops 491520 | bytes 5898240 | tf_op jit(solution)/shard_map/sub | solution.py:120
  (47 shorter events, 1.1 us)
Async XLA Ops:
  4.6 28.5 %all-to-all-start = ((f32[5,3,8,32,128]{4,2,1,0,3:T(8,128)}), f32[5,3,8,32,128]{4,2,1,0,3:T(8,128)S(1)}, u32[]{:S(2)}, u32[]{:S(2)}) async-start(f32[5,3,8,32,128]{4,2,1,0,3:T(8,128)} %copy.19), calls=%async_computation | async-start | bytes 3932160 | tf_op jit(solution)/shard_map/all_to_all | solution.py:99
  33.1 4.6 %copy-start.6 = (f32[5,3,8,32,128]{4,2,1,0,3:T(8,128)}, f32[5,3,8,32,128]{4,2,1,0,3:T(8,128)S(1)}, u32[]{:S(2)}) copy-start(f32[5,3,8,32,128]{4,2,1,0,3:T(8,128)S(1)} %all-to-all-done) | copy-start | bytes 5898244
  33.1 28.8 %all-to-all-start.1 = ((f32[5,3,8,32,128]{4,2,1,0,3:T(8,128)}), f32[5,3,8,32,128]{4,2,1,0,3:T(8,128)}, u32[]{:S(2)}, u32[]{:S(2)}) async-start(f32[5,3,8,32,128]{4,2,1,0,3:T(8,128)} %copy.23), calls=%async_computation.1 | async-start | bytes 3932160 | tf_op jit(solution)/shard_map/all_to_all | solution.py:100
  68.5 4.6 %copy-start = (f32[40,3,8,8,128]{4,0,3,2,1:T(8,128)}, f32[40,3,8,8,128]{4,0,3,2,1:T(8,128)S(1)}, u32[]{:S(2)}) copy-start(f32[40,3,8,8,128]{4,0,3,2,1:T(8,128)S(1)} %fusion.9) | copy-start | bytes 11796484
  73.1 1.9 %copy-start.3 = (f32[40,3,8,8,128]{4,0,3,2,1:T(8,128)}, f32[40,3,8,8,128]{4,0,3,2,1:T(8,128)S(1)}, u32[]{:S(2)}) copy-start(f32[40,3,8,8,128]{4,0,3,2,1:T(8,128)S(1)} %fusion.7) | copy-start | bytes 11796484
  73.1 3.2 %copy-start.11 = (s32[8,32,128]{2,1,0:T(8,128)S(1)}, s32[8,32,128]{2,1,0:T(8,128)}, u32[]{:S(2)}) copy-start(s32[8,32,128]{2,1,0:T(8,128)} %param.9) | copy-start | bytes 393220
  73.1 3.2 %copy-start.10 = (f32[8,32,128]{2,1,0:T(8,128)S(1)}, f32[8,32,128]{2,1,0:T(8,128)}, u32[]{:S(2)}) copy-start(f32[8,32,128]{2,1,0:T(8,128)} %param.8) | copy-start | bytes 393220
  75.0 25.7 %collective-permute-start.1 = (f32[40,6,1,8,128]{4,0,3,2,1:T(8,128)S(1)}, f32[40,6,1,8,128]{4,0,3,2,1:T(8,128)S(1)}, u32[]{:S(2)}, u32[]{:S(2)}) collective-permute-start(f32[40,6,1,8,128]{4,0,3,2,1:T(8,128)S(1)} %pad_maximum_fusion.3), channel_id=1, source_target_pairs={{4,0},{8,4},{12,8},{16,12},{20,16},{24,20},{28,24},{5,1},{9,5},{13... | collective-permute-start | bytes 2949128 | tf_op jit(solution)/shard_map/ppermute | solution.py:20
  77.6 23.2 %collective-permute-start = (f32[40,6,8,1,128]{4,0,3,2,1:T(8,128)S(1)}, f32[40,6,8,1,128]{4,0,3,2,1:T(8,128)S(1)}, u32[]{:S(2)}, u32[]{:S(2)}) collective-permute-start(f32[40,6,8,1,128]{4,0,3,2,1:T(8,128)S(1)} %pad_maximum_fusion.4), channel_id=1, source_target_pairs={{1,0},{2,1},{3,2},{5,4},{6,5},{7,6},{9,8},{10,9},{11,10},{13,12},{... | collective-permute-start | bytes 2949128 | tf_op jit(solution)/shard_map/ppermute | solution.py:20
  79.8 2.1 %copy-start.4 = (f32[40,3,8,8,128]{4,0,3,2,1:T(8,128)S(1)}, f32[40,3,8,8,128]{4,0,3,2,1:T(8,128)}, u32[]{:S(2)}) copy-start(f32[40,3,8,8,128]{4,0,3,2,1:T(8,128)} %copy-done.3) | copy-start | bytes 11796484
  79.8 22.1 %slice-start.3 = ((f32[40,3,8,8,128]{4,0,3,2,1:T(8,128)}), f32[40,3,8,7,128]{4,0,3,2,1:T(8,128)S(1)}, s32[]{:S(2)}) async-start(f32[40,3,8,8,128]{4,0,3,2,1:T(8,128)} %copy-done.3), calls=%async_computation.6 | async-start | bytes 6881280 | tf_op jit(solution)/shard_map/slice | solution.py:48
  79.8 22.1 %copy-start.2 = (f32[40,3,8,8,128]{4,0,3,2,1:T(8,128)S(1)}, f32[40,3,8,8,128]{4,0,3,2,1:T(8,128)}, u32[]{:S(2)}) copy-start(f32[40,3,8,8,128]{4,0,3,2,1:T(8,128)} %copy-done) | copy-start | bytes 11796484
  81.9 3.8 %copy-start.1 = (f32[40,3,8,8,128]{4,0,3,2,1:T(8,128)S(1)}, f32[40,3,8,8,128]{4,0,3,2,1:T(8,128)}, u32[]{:S(2)}) copy-start(f32[40,3,8,8,128]{4,0,3,2,1:T(8,128)} %copy-done) | copy-start | bytes 11796484
  81.9 20.0 %slice-start.2 = ((f32[40,3,8,8,128]{4,0,3,2,1:T(8,128)}), f32[40,3,7,8,128]{4,0,3,2,1:T(8,128)S(1)}, s32[]{:S(2)}) async-start(f32[40,3,8,8,128]{4,0,3,2,1:T(8,128)} %copy-done.3), calls=%async_computation.5 | async-start | bytes 6881280 | tf_op jit(solution)/shard_map/slice | solution.py:47
  85.8 16.2 %slice-start.1 = ((f32[40,3,8,8,128]{4,0,3,2,1:T(8,128)}), f32[40,3,8,7,128]{4,0,3,2,1:T(8,128)S(1)}, s32[]{:S(2)}) async-start(f32[40,3,8,8,128]{4,0,3,2,1:T(8,128)} %copy-done), calls=%async_computation.4 | async-start | bytes 6881280 | tf_op jit(solution)/shard_map/slice | solution.py:48
  87.5 14.4 %slice-start = ((f32[40,3,8,8,128]{4,0,3,2,1:T(8,128)}), f32[40,3,7,8,128]{4,0,3,2,1:T(8,128)S(1)}, s32[]{:S(2)}) async-start(f32[40,3,8,8,128]{4,0,3,2,1:T(8,128)} %copy-done), calls=%async_computation.3 | async-start | bytes 6881280 | tf_op jit(solution)/shard_map/slice | solution.py:47
  107.0 3.3 %copy-start.5 = (f32[40,3,8,8,128]{4,0,3,2,1:T(8,128)S(1)}, f32[40,3,8,8,128]{4,0,3,2,1:T(8,128)}, u32[]{:S(2)}) copy-start(f32[40,3,8,8,128]{4,0,3,2,1:T(8,128)} %get-tuple-element.29) | copy-start | bytes 11796484
  110.3 1.7 %copy-start.9 = (f32[40,8,8,128]{3,0,2,1:T(8,128)S(1)}, f32[40,8,8,128]{3,0,2,1:T(8,128)}, u32[]{:S(2)}) copy-start(f32[40,8,8,128]{3,0,2,1:T(8,128)} %get-tuple-element.14) | copy-start | bytes 3932164
  112.0 1.3 copy-start.8
  113.8 1.3 copy-start.7
  115.5 1.2 copy-start.12
  115.5 1.2 copy-start.13
  119.1 10.4 %collective-permute-start.3 = (f32[40,2,1,8,128]{4,0,3,2,1:T(8,128)S(1)}, f32[40,2,1,8,128]{4,0,3,2,1:T(8,128)S(1)}, u32[]{:S(2)}, u32[]{:S(2)}) collective-permute-start(f32[40,2,1,8,128]{4,0,3,2,1:T(8,128)S(1)} %slice.193), channel_id=1, source_target_pairs={{0,4},{4,8},{8,12},{12,16},{16,20},{20,24},{24,28},{1,5},{5,9},{9,... | collective-permute-start | bytes 983048 | tf_op jit(solution)/shard_map/ppermute | solution.py:20
  123.9 6.3 %collective-permute-start.2 = (f32[40,2,8,1,128]{4,0,3,2,1:T(8,128)S(1)}, f32[40,2,8,1,128]{4,0,3,2,1:T(8,128)S(1)}, u32[]{:S(2)}, u32[]{:S(2)}) collective-permute-start(f32[40,2,8,1,128]{4,0,3,2,1:T(8,128)S(1)} %pad_maximum_fusion.5), channel_id=1, source_target_pairs={{0,1},{1,2},{2,3},{4,5},{5,6},{6,7},{8,9},{9,10},{10,11},{12,13},{... | collective-permute-start | bytes 983048 | tf_op jit(solution)/shard_map/ppermute | solution.py:20
  135.0 28.2 %all-to-all-start.2 = ((f32[20,3,8,8,128]{4,3,2,1,0:T(8,128)}), f32[20,3,8,8,128]{4,3,2,1,0:T(8,128)S(1)}, u32[]{:S(2)}, u32[]{:S(2)}) async-start(f32[20,3,8,8,128]{4,3,2,1,0:T(8,128)} %copy.27), calls=%async_computation.2 | async-start | bytes 3932160 | tf_op jit(solution)/shard_map/all_to_all | solution.py:119
where the time goes:
time: 167 us; the launch traced here: 166 us
  waiting for transfers between devices  83.2 us (50%)
  local copies, waits for them, and re-layouts  27.9 us (17%)
  starting transfers between devices  21.4 us (13%)
  other arithmetic  21.3 us (13%)
  matrix products  11.5 us (7%)
    all_to_all x1, waiting for transfers between devices, local(): lax.all_to_all(coef_values, 'sample', split_axis=0, concat_axis=3, tiled=...  23.7 us
    all_to_all x1, waiting for transfers between devices, local(): lax.all_to_all(adjoint_hat, 'sample', split_axis=3, concat_axis=0, tiled=...  21.9 us
    all_to_all x1, waiting for transfers between devices, local(): lax.all_to_all(state_hat, 'sample', split_axis=3, concat_axis=0, tiled=True)  20.3 us
    ppermute x4, waiting for transfers between devices, passed_along(): return lax.ppermute(array, axis, pairs)  17.3 us
    unnamed x30, local copies, waits for them, and re-layouts  16.8 us
    ppermute x4, starting transfers between devices, passed_along(): return lax.ppermute(array, axis, pairs)  8.66 us
    sub x1, other arithmetic, curl_quarter(): x_step = jnp.concatenate([potential[:, :, 1:], x_upper], axis=2) - potential  5.09 us
    dot_general x1, matrix products, local(): jnp.tensordot(harm_table, state_cells, axes=1, precision=lax.Precision.HI...  4.6 us
  transfers between devices with their start and end apart: 7, of which 5 were waited for; matrix products, arithmetic and copies ran while one was open for 8% of the time, Pallas kernels for 0%

commit v1 on v0

v1 whole, which is shorter than its diff:
```python
import functools
import math

import jax
import jax.numpy as jnp
from jax import lax
from jax.experimental import pallas as pl
from jax.experimental.pallas import tpu as pltpu
from jax.sharding import PartitionSpec as P

NT = 40
magnet_reluct = 0.95
iron_floor = 0.05
saturation = 1.0
VMEM_LIMIT = 48 * 1024 * 1024


def passed_along(array, axis, by):
    size = lax.axis_size(axis)
    pairs = [(i, i + by) for i in range(size) if 0 <= i + by < size]
    return lax.ppermute(array, axis, pairs)


def angle(n, m, period):
    return 2.0 * math.pi * ((n * m) % period) / period


def weighted(terms):
    total = None
    for factor, value in terms:
        if abs(factor) < 1e-12:
            continue
        if abs(factor - 1.0) < 1e-12:
            total = value if total is None else total + value
        elif abs(factor + 1.0) < 1e-12:
            total = -value if total is None else total - value
        else:
            total = factor * value if total is None else total + factor * value
    return total


def add(a, b):
    return b if a is None else (a if b is None else a + b)


def sub(a, b):
    return a if b is None else (-b if a is None else a - b)


def synth(cos_of, sin_of, period):
    if period % 2:
        cos_part = {n: weighted([(math.cos(angle(n, m, period)), v) for m, v in cos_of.items()]) for n in range((period + 1) // 2)}
        sin_part = {n: weighted([(math.sin(angle(n, m, period)), v) for m, v in sin_of.items()]) for n in range((period + 1) // 2)}
        x = [None] * period
        for n in range((period + 1) // 2):
            x[n] = add(cos_part[n], sin_part[n])
            if n:
                x[period - n] = sub(cos_part[n], sin_part[n])
        return x
    half = period // 2
    odd = [None] * half
    cos_odd = {m: v for m, v in cos_of.items() if m % 2}
    sin_odd = {m: v for m, v in sin_of.items() if m % 2}
    for n in range(half // 2 + 1):
        c = weighted([(math.cos(angle(n, m, period)), v) for m, v in cos_odd.items()])
        s = weighted([(math.sin(angle(n, m, period)), v) for m, v in sin_odd.items()])
        odd[n] = add(c, s)
        if n and half - n != n:
            odd[half - n] = sub(s, c)
    cos_even = {m // 2: v for m, v in cos_of.items() if m % 2 == 0}
    sin_even = {m // 2: v for m, v in sin_of.items() if m % 2 == 0}
    if not cos_even:
        return [odd[n] for n in range(half)] + [sub(None, odd[n]) for n in range(half)]
    even = synth(cos_even, sin_even, half)
    return [add(even[n], odd[n]) for n in range(half)] + [sub(even[n], odd[n]) for n in range(half)]


def analyse(x, orders, period):
    if period % 2:
        plus = {n: (x[n] + x[period - n] if n else x[0]) for n in range((period + 1) // 2)}
        minus = {n: x[n] - x[period - n] for n in range(1, (period + 1) // 2)}
        cos_of = {m: weighted([(math.cos(angle(n, m, period)), v) for n, v in plus.items()]) for m in orders}
        sin_of = {m: weighted([(math.sin(angle(n, m, period)), v) for n, v in minus.items()]) for m in orders}
        return cos_of, sin_of
    half = period // 2
    odd = [x[n] - x[n + half] for n in range(half)]
    cos_in, sin_in = {}, {}
    for n in range(half // 2 + 1):
        if n and half - n != n:
            cos_in[n] = odd[n] - odd[half - n]
            sin_in[n] = odd[n] + odd[half - n]
        else:
            cos_in[n] = odd[n]
            sin_in[n] = odd[n]
    cos_of = {m: weighted([(math.cos(angle(n, m, period)), v) for n, v in cos_in.items()]) for m in orders if m % 2}
    sin_of = {m: weighted([(math.sin(angle(n, m, period)), v) for n, v in sin_in.items()]) for m in orders if m % 2}
    lower = [m // 2 for m in orders if m % 2 == 0]
    if lower:
        even = [x[n] + x[n + half] for n in range(half)]
        cos_even, sin_even = analyse(even, lower, half)
        cos_of.update({2 * m: v for m, v in cos_even.items()})
        sin_of.update({2 * m: v for m, v in sin_even.items()})
    return cos_of, sin_of


def lane_sum(rows, upward):
    width = rows.shape[1]
    source = lax.broadcasted_iota(jnp.int32, (2 * width, width), 0)
    source = jnp.where(source >= width, source - width, source)
    target = lax.broadcasted_iota(jnp.int32, (2 * width, width), 1)
    chosen = source >= target if upward else source <= target
    ones = jnp.where(chosen, 1.0, 0.0).astype(jnp.bfloat16)
    high = rows.astype(jnp.bfloat16)
    low = (rows - high.astype(jnp.float32)).astype(jnp.bfloat16)
    return jnp.dot(jnp.concatenate([high, low], axis=1), ones, preferred_element_type=jnp.float32)


def gauge_kernel(groups, state_ref, adjoint_ref, halo_ref, out_ref):
    planes, rows, width = state_ref.shape[2:]
    quarter = rows // groups
    for which, ref in enumerate((state_ref, adjoint_ref)):
        stacked = jnp.concatenate([ref[0, 2].reshape(planes * rows, width), halo_ref[which, 0, 1]], axis=0)
        phi = lane_sum(stacked, True).reshape(planes + 1, rows, width)
        last_row = lax.broadcasted_iota(jnp.int32, phi.shape, 1) == rows - 1
        phi_up = jnp.where(last_row, 0.0, pltpu.roll(phi, rows - 1, 1))
        p = ref[0, 0] + phi[1:] - phi[:-1]
        row_step = phi_up - phi
        q = ref[0, 1] + row_step[:-1]
        q_next = halo_ref[which, 0, 0] + row_step[planes]
        for d in range(groups):
            here = slice(d * quarter, (d + 1) * quarter)
            out_ref[d, 0, which, 0:planes] = p[:, here]
            out_ref[d, 0, which, planes : 2 * planes] = q[:, here]
            out_ref[d, 0, which, 2 * planes] = q_next[here]
            if d + 1 < groups:
                for i in range(planes):
                    out_ref[d, 0, which, 2 * planes + 1, i : i + 1] = p[i, (d + 1) * quarter : (d + 1) * quarter + 1]
            else:
                out_ref[d, 0, which, 2 * planes + 1] = jnp.zeros((quarter, width), jnp.float32)


def gauge(state_hat, adjoint_hat, halo, groups):
    coefs, parts, planes, rows, width = state_hat.shape
    quarter = rows // groups
    tiles = 2 * planes + 2
    block = pl.BlockSpec((1, parts, planes, rows, width), lambda c: (c, 0, 0, 0, 0))
    return pl.pallas_call(
        functools.partial(gauge_kernel, groups),
        grid=(coefs,),
        in_specs=[block, block, pl.BlockSpec((2, 1, 2, rows, width), lambda c: (0, c, 0, 0, 0))],
        out_specs=pl.BlockSpec((groups, 1, 2, tiles, quarter, width), lambda c: (0, c, 0, 0, 0, 0)),
        out_shape=jax.ShapeDtypeStruct((groups, coefs, 2, tiles, quarter, width), jnp.float32),
        compiler_params=pltpu.CompilerParams(vmem_limit_bytes=VMEM_LIMIT),
        name="gauge",
    )(state_hat, adjoint_hat, halo)


def sample_kernel(planes, me_ref, cells_ref, density_ref, region_ref, out_ref, grad_ref, time_ref, third_ref, psi_ref):
    coefs = cells_ref.shape[0]
    quarter, width = cells_ref.shape[3:]
    shape = (quarter, width)
    row = lax.broadcasted_iota(jnp.int32, shape, 0)
    lane = lax.broadcasted_iota(jnp.int32, shape, 1)
    last_lane = lane == width - 1
    last_row = row == quarter - 1
    first_row = row == 0
    my_rows = pl.ds(pl.multiple_of(me_ref[0] * quarter, quarter), quarter)
    orders = list(range(1, coefs // 2 + 1))
    psi_ref[...] = jnp.zeros(psi_ref.shape, jnp.float32)

    def next_lane(v):
        return jnp.where(last_lane, 0.0, pltpu.roll(v, width - 1, 1))

    def one_plane(i, carry):
        for which in range(2):
            for part in range(3):
                flux = []
                for c in range(coefs):
                    if part == 0:
                        q = cells_ref[c, which, planes + i]
                        flux.append(q - next_lane(q))
                    elif part == 1:
                        p = cells_ref[c, which, i]
                        flux.append(next_lane(p) - p)
                    else:
                        p = cells_ref[c, which, i]
                        edge = cells_ref[c, which, 2 * planes + 1, pl.ds(i, 1), :]
                        up = jnp.where(last_row, jnp.broadcast_to(edge, shape), pltpu.roll(p, quarter - 1, 0))
                        flux.append(cells_ref[c, which, planes + 1 + i] - cells_ref[c, which, planes + i] - (up - p))
                samples = synth({m: flux[2 * m - 2] for m in orders}, {m: flux[2 * m - 1] for m in orders}, NT)
                for n in range(NT):
                    time_ref[which * 3 + part, n] = samples[n]
        density = density_ref[i, my_rows]
        region = region_ref[i, my_rows]
        iron = region == 0
        share = jnp.where(iron, density * density * density, 0.0) * (1.0 - iron_floor)
        slope = jnp.where(iron, 3.0 * density * density, 0.0)
        base = jnp.where(region == 1, magnet_reluct, 1.0)
        total = jnp.zeros(shape, jnp.float32)
        for n in range(NT):
            b = [time_ref[j, n] for j in range(3)]
            a = [time_ref[3 + j, n] for j in range(3)]
            square = b[0] * b[0] + b[1] * b[1] + b[2] * b[2]
            inner = b[0] * a[0] + b[1] * a[1] + b[2] * a[2]
            inverse = 1.0 / (square + saturation)
            scaled = share * inverse
            reluct_now = base - scaled
            ratio = inverse * inner
            total = total + ratio
            along = scaled * ratio
            along = along + along
            for j in range(3):
                time_ref[j, n] = reluct_now * a[j] + along * b[j]
        grad_ref[i] = ((1.0 - iron_floor) / NT) * slope * total
        results = []
        for part in (2, 0, 1):
            x = [time_ref[part, n] for n in range(NT)]
            cos_of, sin_of = analyse(x, orders, NT)
            field = []
            for m in orders:
                field += [cos_of[m], sin_of[m]]
            if part == 2:
                for c in range(coefs):
                    third_ref[c] = field[c]
                psi = lane_sum(third_ref[...].reshape(coefs * quarter, width), False).reshape(coefs, quarter, width)
                third_ref[...] = psi
            elif part == 0:
                for c in range(coefs):
                    out_ref[c, i] = field[c] + (psi_ref[c] - third_ref[c])
            else:
                for c in range(coefs):
                    psi = third_ref[c]
                    down = jnp.where(first_row, 0.0, pltpu.roll(psi, 1, 0))
                    out_ref[c, planes + i] = field[c] + (down - psi)
                    out_ref[c, 2 * planes + 1, pl.ds(i, 1), :] = psi[quarter - 1 : quarter]
                    psi_ref[c] = psi
        return carry

    lax.fori_loop(0, planes, one_plane, 0)
    for c in range(coefs):
        out_ref[c, 2 * planes] = psi_ref[c]


def sample_fields(cells, density, region, planes):
    coefs, _, tiles, quarter, width = cells.shape
    me = lax.axis_index("sample").astype(jnp.int32).reshape(1)
    vmem = pl.BlockSpec(memory_space=pltpu.VMEM)
    return pl.pallas_call(
        functools.partial(sample_kernel, planes),
        in_specs=[pl.BlockSpec(memory_space=pltpu.SMEM), vmem, vmem, vmem],
        out_specs=[vmem, vmem],
        out_shape=[
            jax.ShapeDtypeStruct((coefs, tiles, quarter, width), jnp.float32),
            jax.ShapeDtypeStruct((planes, quarter, width), jnp.float32),
        ],
        scratch_shapes=[
            pltpu.VMEM((6, NT, quarter, width), jnp.float32),
            pltpu.VMEM((coefs, quarter, width), jnp.float32),
            pltpu.VMEM((coefs, quarter, width), jnp.float32),
        ],
        compiler_params=pltpu.CompilerParams(vmem_limit_bytes=VMEM_LIMIT),
        name="samples",
    )(me, cells, density, region)


def residual_kernel(fields_ref, halo_ref, objective_ref, out_ref):
    groups = fields_ref.shape[0]
    parts, planes, rows, width = objective_ref.shape[1:]
    quarter = rows // groups
    row = lax.broadcasted_iota(jnp.int32, (rows, width), 0)
    lane = lax.broadcasted_iota(jnp.int32, (rows, width), 1)

    def joined(ref, tile):
        return jnp.concatenate([ref[d, 0, tile] for d in range(groups)], axis=0)

    def with_edges(value, ref, tile, i):
        first = lax.broadcasted_iota(jnp.int32, (quarter, width), 0) == 0
        parts_of = [value[0:quarter]]
        for d in range(1, groups):
            edge = jnp.broadcast_to(ref[d - 1, 0, tile, i : i + 1, :], (quarter, width))
            parts_of.append(value[d * quarter : (d + 1) * quarter] + jnp.where(first, edge, 0.0))
        return jnp.concatenate(parts_of, axis=0)

    def lower_lane(v):
        return jnp.where(lane == 0, 0.0, pltpu.roll(v, 1, 1))

    before = with_edges(joined(halo_ref, 0), halo_ref, 2, planes - 1)
    for i in range(planes):
        h0 = joined(fields_ref, i)
        if i == 0:
            h0 = h0 + joined(halo_ref, 1)
        h1 = with_edges(joined(fields_ref, planes + i), fields_ref, 2 * planes + 1, i)
        out_ref[0, 0, i] = objective_ref[0, 0, i] - (2.0 / NT) * (lower_lane(h1) - h1)
        out_ref[0, 1, i] = objective_ref[0, 1, i] - (2.0 / NT) * (h0 - lower_lane(h0))
        lower_row = jnp.where(row == 0, 0.0, pltpu.roll(h0, 1, 0))
        out_ref[0, 2, i] = objective_ref[0, 2, i] - (2.0 / NT) * ((lower_row - h0) - (before - h1))
        before = h1


def residual(fields, halo, objective_hat):
    coefs, parts, planes, rows, width = objective_hat.shape
    groups, _, tiles, quarter, _ = fields.shape
    block = pl.BlockSpec((1, parts, planes, rows, width), lambda c: (c, 0, 0, 0, 0))
    return pl.pallas_call(
        residual_kernel,
        grid=(coefs,),
        in_specs=[
            pl.BlockSpec((groups, 1, tiles, quarter, width), lambda c: (0, c, 0, 0, 0)),
            pl.BlockSpec((groups, 1, 3, quarter, width), lambda c: (0, c, 0, 0, 0)),
            block,
        ],
        out_specs=block,
        out_shape=jax.ShapeDtypeStruct(objective_hat.shape, jnp.float32),
        compiler_params=pltpu.CompilerParams(vmem_limit_bytes=VMEM_LIMIT),
        name="residual",
    )(fields, halo, objective_hat)


def exchange(array):
    return lax.all_to_all(array, "sample", split_axis=0, concat_axis=0, tiled=True)


def local(state_hat, adjoint_hat, objective_hat, density, region):
    groups = lax.axis_size("sample")
    coefs, parts, planes, rows, width = state_hat.shape
    first = jnp.stack([state_hat[:, 1:3, 0], adjoint_hat[:, 1:3, 0]], axis=0)
    upper = passed_along(first, "space", -1)
    sent = gauge(state_hat, adjoint_hat, upper, groups)
    cells = exchange(sent).reshape((groups * coefs,) + sent.shape[2:])
    fields, density_gradient = sample_fields(cells, density, region, planes)
    back = exchange(fields.reshape((groups, coefs) + fields.shape[1:]))
    lower = passed_along(back[:, :, 2 * planes - 1 : 2 * planes + 2], "space", 1)
    return residual(back, lower, objective_hat), density_gradient


def solution(mesh):
    in_specs = (
        P("sample", None, "space", None, None),
        P("sample", None, "space", None, None),
        P("sample", None, "space", None, None),
        P("space", None, None),
        P("space", None, None),
    )
    out_specs = (P("sample", None, "space", None, None), P("space", "sample", None))
    return jax.shard_map(local, mesh=mesh, in_specs=in_specs, out_specs=out_specs, check_vma=False)
```

time: 167 us -> 100 us (0.60)
  waiting for transfers between devices: 83.2 us -> 51.3 us
  local copies, waits for them, and re-layouts: 27.9 us -> 4.15 us
  blocking collectives: 0 us -> 21.6 us
  other arithmetic: 21.3 us -> 0.02 us
  Pallas kernels: 0 us -> 12.7 us
  starting transfers between devices: 21.4 us -> 9.65 us
  matrix products: 11.5 us -> 0 us
    all_to_all x3 -> x1, waiting for transfers between devices: 65.9 us -> 34.8 us  [exchange(): lax.all_to_all(array, 'sample', split_axis=0, concat_axis=0, tiled=True)]
    all_to_all x0 -> x1, blocking collectives: none -> 21.6 us  [exchange(): lax.all_to_all(array, 'sample', split_axis=0, concat_axis=0, tiled=True)]
    unnamed x30 -> x10, local copies, waits for them, and re-layouts: 16.8 us -> 3.1 us
    pallas_call x0 -> x3, Pallas kernels: none -> 12.7 us  [the longest x1 6.7 us: sample_fields(): pl.pallas_call(functools.partial(sample_kernel, planes), in_specs=[pl.Blo...]
    dot_general x3 -> x0, matrix products: 11.5 us -> none  [the longest x1 4.6 us: local(): jnp.tensordot(harm_table, state_cells, axes=1, precision=lax.Precision.HI...]
    sub x7 -> x0, other arithmetic: 10.7 us -> none  [the longest x1 5.09 us: curl_quarter(): x_step = jnp.concatenate([potential[:, :, 1:], x_upper], axis=2) - potential]
    all_to_all x3 -> x1, starting transfers between devices: 12.7 us -> 3.81 us  [exchange(): lax.all_to_all(array, 'sample', split_axis=0, concat_axis=0, tiled=True)]
    another operation x9 -> x1, other arithmetic: 4.91 us -> 0.02 us  [local(): first = jnp.stack([state_hat[:, 1:3, 0], adjoint_hat[:, 1:3, 0]], axis=0)]
  transfers between devices with their start and end apart: 7 -> 3, of which waited for: 5 -> 3; matrix products, arithmetic and copies ran while one was open for 8% -> 0% of each run, Pallas kernels for 0% -> 0%
where the time goes in v1:
time: 100 us
  waiting for transfers between devices  51.3 us (51%)
  blocking collectives  21.6 us (22%)
  Pallas kernels  12.7 us (13%)
  starting transfers between devices  9.65 us (10%)
  local copies, waits for them, and re-layouts  4.15 us (4%)
    all_to_all x1, waiting for transfers between devices, exchange(): lax.all_to_all(array, 'sample', split_axis=0, concat_axis=0, tiled=True)  34.8 us
    all_to_all x1, blocking collectives, exchange(): lax.all_to_all(array, 'sample', split_axis=0, concat_axis=0, tiled=True)  21.6 us
    ppermute x2, waiting for transfers between devices, passed_along(): return lax.ppermute(array, axis, pairs)  16.5 us
    pallas_call x1, Pallas kernels, sample_fields(): pl.pallas_call(functools.partial(sample_kernel, planes), in_specs=[pl.Blo...  6.7 us
    ppermute x2, starting transfers between devices, passed_along(): return lax.ppermute(array, axis, pairs)  5.84 us
    all_to_all x1, starting transfers between devices, exchange(): lax.all_to_all(array, 'sample', split_axis=0, concat_axis=0, tiled=True)  3.81 us
    pallas_call x1, Pallas kernels, gauge(): pl.pallas_call(functools.partial(gauge_kernel, groups), grid=(coefs,), in...  3.26 us
    unnamed x10, local copies, waits for them, and re-layouts  3.1 us
  transfers between devices with their start and end apart: 3, of which 3 were waited for; matrix products, arithmetic and copies ran while one was open for 0% of the time, Pallas kernels for 0%

profile of v1, /device:TPU:0, one launch (start us, length us, event | category | flops | bytes accessed | tf_op | source)
XLA Modules:
  0.0 100.1 jit_solution(293187114323619373)
XLA Ops:
  0.6 1.0 %slice_bitcast_fusion = (f32[1,5,2,32,128]{4,3,2,1,0:T(8,128)S(1)}, f32[1,5,2,32,128]{4,3,2,1,0:T(8,128)S(1)}) fusion(f32[5,3,8,32,128]{4,3,2,1,0:T(8,128)} %adjoint_ref.1, f32[5,3,8,32,128]{4,3,2,1,0:T(8,128)} %state_ref.1), kind=kLoop, calls=%fused_computation.1 | loop fusion | bytes 655360 | tf_op jit(solution)/shard_map/stack;squeeze | solution.py:326
  1.7 1.3 %collective-permute-start = (f32[2,5,2,32,128]{4,3,2,1,0:T(8,128)S(1)}, f32[2,5,2,32,128]{4,3,2,1,0:T(8,128)S(1)}, u32[]{:S(2)}, u32[]{:S(2)}) collective-permute-start(f32[2,5,2,32,128]{4,3,2,1,0:T(8,128)S(1)} %pad_maximum_fusion), channel_id=1, source_target_pairs={{4,0},{8,4},{12,8},{16,12},{20,16},{24,20},{28,24},{5,1},{9,5},{13... | collective-permute-start | bytes 983048 | tf_op jit(solution)/shard_map/ppermute | solution.py:21
  3.0 11.2 %collective-permute-done.halo_ref = f32[2,5,2,32,128]{4,3,2,1,0:T(8,128)S(1)} collective-permute-done((f32[2,5,2,32,128]{4,3,2,1,0:T(8,128)S(1)}, f32[2,5,2,32,128]{4,3,2,1,0:T(8,128)S(1)}, u32[]{:S(2)}, u32[]{:S(2)}) %collective-permute-start) | collective-permute-done | bytes 327712 | tf_op jit(solution)/shard_map/ppermute | solution.py:21
  14.2 0.0 copy-start
  14.2 1.5 %copy-done = f32[5,3,8,32,128]{4,3,2,1,0:T(8,128)S(1)} copy-done((f32[5,3,8,32,128]{4,3,2,1,0:T(8,128)S(1)}, f32[5,3,8,32,128]{4,3,2,1,0:T(8,128)}, u32[]{:S(2)}) %copy-start) | copy-done | bytes 1966104
  15.8 0.0 copy-start.1
  15.8 1.5 %copy-done.1 = f32[5,3,8,32,128]{4,3,2,1,0:T(8,128)S(1)} copy-done((f32[5,3,8,32,128]{4,3,2,1,0:T(8,128)S(1)}, f32[5,3,8,32,128]{4,3,2,1,0:T(8,128)}, u32[]{:S(2)}) %copy-start.1) | copy-done | bytes 1966104
  17.3 3.3 %gauge.1 = f32[4,5,2,18,8,128]{5,4,3,2,1,0:T(8,128)} custom-call(f32[5,3,8,32,128]{4,3,2,1,0:T(8,128)S(1)} %copy-done, f32[5,3,8,32,128]{4,3,2,1,0:T(8,128)S(1)} %copy-done.1, f32[2,5,2,32,128]{4,3,2,1,0:T(8,128)S(1)} %collective-permute-done.halo_ref), custom_call_target="tpu_custom_call" | custom-call | tf_op jit(solution)/shard_map/gauge/pallas_call | solution.py:147
  20.6 0.0 copy-start.3
  20.6 0.0 copy-start.4
  20.6 3.8 %all-to-all-start = ((f32[4,5,2,18,8,128]{5,4,3,2,1,0:T(8,128)}), f32[4,5,2,18,8,128]{5,4,3,2,1,0:T(8,128)S(1)}, u32[]{:S(2)}, u32[]{:S(2)}) async-start(f32[4,5,2,18,8,128]{5,4,3,2,1,0:T(8,128)} %gauge.1), calls=%async_computation | async-start | bytes 5898240 | tf_op jit(solution)/shard_map/all_to_all | solution.py:320
  24.4 34.8 %all-to-all-done = f32[4,5,2,18,8,128]{5,4,3,2,1,0:T(8,128)S(1)} async-done(((f32[4,5,2,18,8,128]{5,4,3,2,1,0:T(8,128)}), f32[4,5,2,18,8,128]{5,4,3,2,1,0:T(8,128)S(1)}, u32[]{:S(2)}, u32[]{:S(2)}) %all-to-all-start) | async-done | bytes 2949152 | tf_op jit(solution)/shard_map/all_to_all | solution.py:320
  59.2 0.0 copy-done.3
  59.2 0.0 copy-done.4
  59.2 6.7 %samples.1 = (f32[20,18,8,128]{3,2,1,0:T(8,128)S(1)}, f32[8,8,128]{2,1,0:T(8,128)}) custom-call(s32[1]{0:T(128)} %bitcast.me_ref, f32[20,2,18,8,128]{4,3,2,1,0:T(8,128)S(1)} %bitcast.11, f32[8,32,128]{2,1,0:T(8,128)S(1)} %copy-done.3, s32[8,32,128]{2,1,0:T(8,128)S(1)} %copy-done.4), custom_call_target="tpu_custom_call" | custom-call | tf_op jit(solution)/shard_map/samples/pallas_call | solution.py:248
  65.9 0.0 copy-start.2
  65.9 21.6 %all_to_all.10.fields_ref = f32[4,5,18,8,128]{4,3,2,1,0:T(8,128)S(1)} all-to-all(f32[4,5,18,8,128]{4,3,2,1,0:T(8,128)S(1)} %bitcast.12), channel_id=1, replica_groups=mesh['space'=8,'sample'=4] {'sample'}, dimensions={0} | all-to-all | bytes 2949120 | tf_op jit(solution)/shard_map/all_to_all | solution.py:320
  87.5 4.5 %collective-permute-start.1 = (f32[4,5,3,8,128]{4,3,2,1,0:T(8,128)S(1)}, f32[4,5,3,8,128]{4,3,2,1,0:T(8,128)S(1)}, u32[]{:S(2)}, u32[]{:S(2)}) collective-permute-start(f32[4,5,3,8,128]{4,3,2,1,0:T(8,128)S(1)} %slice.12), channel_id=1, source_target_pairs={{0,4},{4,8},{8,12},{12,16},{16,20},{20,24},{24,28},{1,5},{5,9},{9,... | collective-permute-start | bytes 737288 | tf_op jit(solution)/shard_map/ppermute | solution.py:21
  92.1 5.3 %collective-permute-done.1.halo_ref = f32[4,5,3,8,128]{4,3,2,1,0:T(8,128)S(1)} collective-permute-done((f32[4,5,3,8,128]{4,3,2,1,0:T(8,128)S(1)}, f32[4,5,3,8,128]{4,3,2,1,0:T(8,128)S(1)}, u32[]{:S(2)}, u32[]{:S(2)}) %collective-permute-start.1) | collective-permute-done | bytes 245792 | tf_op jit(solution)/shard_map/ppermute | solution.py:21
  97.3 0.0 copy-done.2
  97.3 2.8 %residual.1 = f32[5,3,8,32,128]{4,3,2,1,0:T(8,128)} custom-call(f32[4,5,18,8,128]{4,3,2,1,0:T(8,128)S(1)} %all_to_all.10.fields_ref, f32[4,5,3,8,128]{4,3,2,1,0:T(8,128)S(1)} %collective-permute-done.1.halo_ref, f32[5,3,8,32,128]{4,3,2,1,0:T(8,128)S(1)} %copy-done.2), custom_call_target="tpu_custom_call" | custom-call | tf_op jit(solution)/shard_map/residual/pallas_call | solution.py:304
  (2 shorter events, 0.0 us)
Async XLA Ops:
  1.7 12.5 %collective-permute-start = (f32[2,5,2,32,128]{4,3,2,1,0:T(8,128)S(1)}, f32[2,5,2,32,128]{4,3,2,1,0:T(8,128)S(1)}, u32[]{:S(2)}, u32[]{:S(2)}) collective-permute-start(f32[2,5,2,32,128]{4,3,2,1,0:T(8,128)S(1)} %pad_maximum_fusion), channel_id=1, source_target_pairs={{4,0},{8,4},{12,8},{16,12},{20,16},{24,20},{28,24},{5,1},{9,5},{13... | collective-permute-start | bytes 983048 | tf_op jit(solution)/shard_map/ppermute | solution.py:21
  14.2 1.5 %copy-start = (f32[5,3,8,32,128]{4,3,2,1,0:T(8,128)S(1)}, f32[5,3,8,32,128]{4,3,2,1,0:T(8,128)}, u32[]{:S(2)}) copy-start(f32[5,3,8,32,128]{4,3,2,1,0:T(8,128)} %state_ref.1) | copy-start | bytes 5898244
  15.8 1.5 %copy-start.1 = (f32[5,3,8,32,128]{4,3,2,1,0:T(8,128)S(1)}, f32[5,3,8,32,128]{4,3,2,1,0:T(8,128)}, u32[]{:S(2)}) copy-start(f32[5,3,8,32,128]{4,3,2,1,0:T(8,128)} %adjoint_ref.1) | copy-start | bytes 5898244
  20.6 38.6 %copy-start.3 = (f32[8,32,128]{2,1,0:T(8,128)S(1)}, f32[8,32,128]{2,1,0:T(8,128)}, u32[]{:S(2)}) copy-start(f32[8,32,128]{2,1,0:T(8,128)} %density_ref.1) | copy-start | bytes 393220
  20.6 38.6 %copy-start.4 = (s32[8,32,128]{2,1,0:T(8,128)S(1)}, s32[8,32,128]{2,1,0:T(8,128)}, u32[]{:S(2)}) copy-start(s32[8,32,128]{2,1,0:T(8,128)} %region_ref.1) | copy-start | bytes 393220
  20.6 38.6 %all-to-all-start = ((f32[4,5,2,18,8,128]{5,4,3,2,1,0:T(8,128)}), f32[4,5,2,18,8,128]{5,4,3,2,1,0:T(8,128)S(1)}, u32[]{:S(2)}, u32[]{:S(2)}) async-start(f32[4,5,2,18,8,128]{5,4,3,2,1,0:T(8,128)} %gauge.1), calls=%async_computation | async-start | bytes 5898240 | tf_op jit(solution)/shard_map/all_to_all | solution.py:320
  65.9 31.4 %copy-start.2 = (f32[5,3,8,32,128]{4,3,2,1,0:T(8,128)S(1)}, f32[5,3,8,32,128]{4,3,2,1,0:T(8,128)}, u32[]{:S(2)}) copy-start(f32[5,3,8,32,128]{4,3,2,1,0:T(8,128)} %objective_ref.1) | copy-start | bytes 5898244
  87.5 9.8 %collective-permute-start.1 = (f32[4,5,3,8,128]{4,3,2,1,0:T(8,128)S(1)}, f32[4,5,3,8,128]{4,3,2,1,0:T(8,128)S(1)}, u32[]{:S(2)}, u32[]{:S(2)}) collective-permute-start(f32[4,5,3,8,128]{4,3,2,1,0:T(8,128)S(1)} %slice.12), channel_id=1, source_target_pairs={{0,4},{4,8},{8,12},{12,16},{16,20},{20,24},{24,28},{1,5},{5,9},{9,... | collective-permute-start | bytes 737288 | tf_op jit(solution)/shard_map/ppermute | solution.py:21

commit v2 on v1

v2 whole, which is shorter than its diff:
```python
import functools
import math

import jax
import jax.numpy as jnp
from jax import lax
from jax.experimental import pallas as pl
from jax.experimental.pallas import tpu as pltpu
from jax.sharding import PartitionSpec as P

NT = 40
magnet_reluct = 0.95
iron_floor = 0.05
saturation = 1.0
GAUGE_LIMIT = 16 * 1024 * 1024
SAMPLE_LIMIT = 16 * 1024 * 1024
RESIDUAL_LIMIT = 16 * 1024 * 1024


def passed_along(array, axis, by):
    size = lax.axis_size(axis)
    pairs = [(i, i + by) for i in range(size) if 0 <= i + by < size]
    return lax.ppermute(array, axis, pairs)


def angle(n, m, period):
    return 2.0 * math.pi * ((n * m) % period) / period


def weighted(terms):
    total = None
    for factor, value in terms:
        if abs(factor) < 1e-12:
            continue
        if abs(factor - 1.0) < 1e-12:
            total = value if total is None else total + value
        elif abs(factor + 1.0) < 1e-12:
            total = -value if total is None else total - value
        else:
            total = factor * value if total is None else total + factor * value
    return total


def add(a, b):
    return b if a is None else (a if b is None else a + b)


def sub(a, b):
    return a if b is None else (-b if a is None else a - b)


def synth(cos_of, sin_of, period):
    if period % 2:
        cos_part = {n: weighted([(math.cos(angle(n, m, period)), v) for m, v in cos_of.items()]) for n in range((period + 1) // 2)}
        sin_part = {n: weighted([(math.sin(angle(n, m, period)), v) for m, v in sin_of.items()]) for n in range((period + 1) // 2)}
        x = [None] * period
        for n in range((period + 1) // 2):
            x[n] = add(cos_part[n], sin_part[n])
            if n:
                x[period - n] = sub(cos_part[n], sin_part[n])
        return x
    half = period // 2
    odd = [None] * half
    cos_odd = {m: v for m, v in cos_of.items() if m % 2}
    sin_odd = {m: v for m, v in sin_of.items() if m % 2}
    for n in range(half // 2 + 1):
        c = weighted([(math.cos(angle(n, m, period)), v) for m, v in cos_odd.items()])
        s = weighted([(math.sin(angle(n, m, period)), v) for m, v in sin_odd.items()])
        odd[n] = add(c, s)
        if n and half - n != n:
            odd[half - n] = sub(s, c)
    cos_even = {m // 2: v for m, v in cos_of.items() if m % 2 == 0}
    sin_even = {m // 2: v for m, v in sin_of.items() if m % 2 == 0}
    if not cos_even:
        return [odd[n] for n in range(half)] + [sub(None, odd[n]) for n in range(half)]
    even = synth(cos_even, sin_even, half)
    return [add(even[n], odd[n]) for n in range(half)] + [sub(even[n], odd[n]) for n in range(half)]


def analyse(x, orders, period):
    if period % 2:
        plus = {n: (x[n] + x[period - n] if n else x[0]) for n in range((period + 1) // 2)}
        minus = {n: x[n] - x[period - n] for n in range(1, (period + 1) // 2)}
        cos_of = {m: weighted([(math.cos(angle(n, m, period)), v) for n, v in plus.items()]) for m in orders}
        sin_of = {m: weighted([(math.sin(angle(n, m, period)), v) for n, v in minus.items()]) for m in orders}
        return cos_of, sin_of
    half = period // 2
    odd = [x[n] - x[n + half] for n in range(half)]
    cos_in, sin_in = {}, {}
    for n in range(half // 2 + 1):
        if n and half - n != n:
            cos_in[n] = odd[n] - odd[half - n]
            sin_in[n] = odd[n] + odd[half - n]
        else:
            cos_in[n] = odd[n]
            sin_in[n] = odd[n]
    cos_of = {m: weighted([(math.cos(angle(n, m, period)), v) for n, v in cos_in.items()]) for m in orders if m % 2}
    sin_of = {m: weighted([(math.sin(angle(n, m, period)), v) for n, v in sin_in.items()]) for m in orders if m % 2}
    lower = [m // 2 for m in orders if m % 2 == 0]
    if lower:
        even = [x[n] + x[n + half] for n in range(half)]
        cos_even, sin_even = analyse(even, lower, half)
        cos_of.update({2 * m: v for m, v in cos_even.items()})
        sin_of.update({2 * m: v for m, v in sin_even.items()})
    return cos_of, sin_of


def lane_sum(rows, upward):
    width = rows.shape[1]
    source = lax.broadcasted_iota(jnp.int32, (2 * width, width), 0)
    source = jnp.where(source >= width, source - width, source)
    target = lax.broadcasted_iota(jnp.int32, (2 * width, width), 1)
    chosen = source >= target if upward else source <= target
    ones = jnp.where(chosen, 1.0, 0.0).astype(jnp.bfloat16)
    high = rows.astype(jnp.bfloat16)
    low = (rows - high.astype(jnp.float32)).astype(jnp.bfloat16)
    return jnp.dot(jnp.concatenate([high, low], axis=1), ones, preferred_element_type=jnp.float32)


def partner(me, r, groups):
    if groups & (groups - 1) == 0:
        return jnp.bitwise_xor(me, r)
    return lax.rem(me + r, groups)


def origin(me, r, groups):
    if groups & (groups - 1) == 0:
        return jnp.bitwise_xor(me, r)
    return lax.rem(me + groups - r, groups)


def exchange(messages):
    groups = len(messages)
    taken = [messages[0]] + [None] * (groups - 1)
    for r in list(range(2, groups)) + [1]:
        if groups & (groups - 1) == 0:
            pairs = [(i, i ^ r) for i in range(groups)]
        else:
            pairs = [(i, (i + r) % groups) for i in range(groups)]
        taken[r] = lax.ppermute(messages[r], "sample", pairs)
    return taken


def tiles_for(rows, quarter):
    return -(-rows // quarter)


VMEM = pl.BlockSpec(memory_space=pltpu.VMEM)
SMEM = pl.BlockSpec(memory_space=pltpu.SMEM)
HBM = pl.BlockSpec(memory_space=pltpu.HBM)


class Chunk:
    def __init__(self, kind, lo, hi):
        self.kind, self.lo, self.hi, self.n = kind, lo, hi, hi - lo
        self.q_from = 1 if kind == 1 else 0
        self.q_to = self.n if kind == 2 else self.n + 1
        self.nq = self.q_to - self.q_from
        self.h_from = 1 if kind == 0 else 0
        self.h_to = self.n + 1 if kind == 2 else self.n
        self.nh = self.h_to - self.h_from + (1 if kind == 1 else 0)

    def sent(self, coefs, quarter):
        return 2 * coefs * (self.n + self.nq) + tiles_for(2 * coefs * self.n, quarter)

    def back(self, coefs, quarter):
        return coefs * (self.nh + self.n) + tiles_for(coefs * self.n, quarter)


def gauge_kernel(chunk, groups, me_ref, state_ref, adjoint_ref, halo_ref, *rest):
    out_refs, (held, p_held, q_held, sems) = rest[:groups], rest[groups:]
    coefs, parts, planes, rows, width = state_ref.shape
    quarter = rows // groups
    n, nq = chunk.n, chunk.nq
    own = held.shape[3]
    me = me_ref[0]
    copies = []
    for c in range(coefs):
        for which, ref in enumerate((state_ref, adjoint_ref)):
            copy = pltpu.make_async_copy(ref.at[c, :, pl.ds(chunk.lo, own)], held.at[which, c], sems.at[which, c])
            copy.start()
            copies.append((c, which, copy))
    zero_rows = jnp.zeros((n, quarter, width), jnp.float32)
    last_row = lax.broadcasted_iota(jnp.int32, (n + 1, rows, width), 1) == rows - 1
    for c, which, copy in copies:
        copy.wait()
        third = held[which, c, 2]
        second = held[which, c, 1]
        if own == n:
            third = jnp.concatenate([third, halo_ref[which, c, 1][None]], axis=0)
            second = jnp.concatenate([second, halo_ref[which, c, 0][None]], axis=0)
        phi = lane_sum(third.reshape((n + 1) * rows, width), True).reshape(n + 1, rows, width)
        phi_up = jnp.where(last_row, 0.0, pltpu.roll(phi, rows - 1, 1))
        p_held[which, c, :, 0:rows] = held[which, c, 0, 0:n] + phi[1:] - phi[:-1]
        p_held[which, c, :, rows : rows + quarter] = zero_rows
        q_held[which, c] = (second + (phi_up - phi))[chunk.q_from : chunk.q_to]
        base = (which * coefs + c) * (n + nq)
        for r in range(groups):
            start = pl.multiple_of(partner(me, r, groups) * quarter, quarter)
            out_refs[r][base : base + n] = p_held[which, c, :, pl.ds(start, quarter)]
            out_refs[r][base + n : base + n + nq] = q_held[which, c, :, pl.ds(start, quarter)]
            for i in range(n):
                spot = (which * coefs + c) * n + i
                edge = p_held[which, c, i, pl.ds(pl.multiple_of(start + quarter, quarter), quarter)]
                tile = 2 * coefs * (n + nq) + spot // quarter
                out_refs[r][tile, spot % quarter : spot % quarter + 1] = edge[0:1]


def gauge(chunk, groups, me, state_hat, adjoint_hat, halo):
    coefs, parts, planes, rows, width = state_hat.shape
    quarter = rows // groups
    own = min(chunk.n + 1, planes - chunk.lo)
    shape = jax.ShapeDtypeStruct((chunk.sent(coefs, quarter), quarter, width), jnp.float32)
    return pl.pallas_call(
        functools.partial(gauge_kernel, chunk, groups),
        in_specs=[SMEM, HBM, HBM, VMEM],
        out_specs=[VMEM] * groups,
        out_shape=[shape] * groups,
        scratch_shapes=[
            pltpu.VMEM((2, coefs, parts, own, rows, width), jnp.float32),
            pltpu.VMEM((2, coefs, chunk.n, rows + quarter, width), jnp.float32),
            pltpu.VMEM((2, coefs, chunk.nq, rows, width), jnp.float32),
            pltpu.SemaphoreType.DMA((2, coefs)),
        ],
        compiler_params=pltpu.CompilerParams(vmem_limit_bytes=GAUGE_LIMIT),
        cost_estimate=pl.CostEstimate(flops=2 * 10**9, bytes_accessed=4 * 10**6, transcendentals=0),
        name="gauge%d" % chunk.kind,
    )(me, state_hat, adjoint_hat, halo)


def sample_kernel(chunk, groups, coefs, *refs):
    n, nq, kind = chunk.n, chunk.nq, chunk.kind
    me_ref, message_refs, refs = refs[0], refs[1 : 1 + groups], refs[1 + groups :]
    density_ref, region_ref, refs = refs[0], refs[1], refs[2:]
    edge_q_ref = edge_h_ref = None
    if kind:
        edge_q_ref, edge_h_ref, refs = refs[0], refs[1], refs[2:]
    out_refs, grad_ref, refs = refs[:groups], refs[groups], refs[groups + 1 :]
    if kind == 0:
        first_q_ref, last_q_ref, pending_ref, last_psi_ref = refs[:4]
        refs = refs[4:]
    p_ref, q_ref, edge_ref, time_ref, third_ref, psi_ref, h0_ref, h1_ref, tail_ref = refs
    quarter, width = p_ref.shape[4:]
    shape = (quarter, width)
    me = me_ref[0]
    row = lax.broadcasted_iota(jnp.int32, shape, 0)
    lane = lax.broadcasted_iota(jnp.int32, shape, 1)
    last_lane = lane == width - 1
    last_row = row == quarter - 1
    first_row = row == 0
    my_rows = pl.ds(pl.multiple_of(me * quarter, quarter), quarter)
    total_coefs = groups * coefs
    orders = list(range(1, total_coefs // 2 + 1))
    place = [(c // coefs, c % coefs) for c in range(total_coefs)]

    for r in range(groups):
        g = origin(me, r, groups)
        for which in range(2):
            for c in range(coefs):
                base = (which * coefs + c) * (n + nq)
                p_ref[which, g, c] = message_refs[r][base : base + n]
                q_ref[which, g, c, chunk.q_from : chunk.q_to] = message_refs[r][base + n : base + n + nq]
        for t in range(tiles_for(2 * coefs * n, quarter)):
            edge_ref[g, t * quarter : (t + 1) * quarter] = message_refs[r][2 * coefs * (n + nq) + t]
    for which in range(2):
        for g in range(groups):
            for c in range(coefs):
                if kind == 0:
                    first_q_ref[which, g, c] = q_ref[which, g, c, 0]
                    last_q_ref[which, g, c] = q_ref[which, g, c, n]
                elif kind == 1:
                    q_ref[which, g, c, 0] = edge_q_ref[which, g, c]
                else:
                    q_ref[which, g, c, n] = edge_q_ref[which, g, c]
    if kind == 1:
        psi_ref[...] = edge_h_ref[...]
    else:
        psi_ref[...] = jnp.zeros(psi_ref.shape, jnp.float32)

    def next_lane(v):
        return jnp.where(last_lane, 0.0, pltpu.roll(v, width - 1, 1))

    def one_plane(i, carry):
        for which in range(2):
            for part in range(3):
                flux = []
                for g, c in place:
                    if part == 0:
                        q = q_ref[which, g, c, i]
                        flux.append(q - next_lane(q))
                    elif part == 1:
                        p = p_ref[which, g, c, i]
                        flux.append(next_lane(p) - p)
                    else:
                        p = p_ref[which, g, c, i]
                        edge = edge_ref[g, pl.ds((which * coefs + c) * n + i, 1), :]
                        up = jnp.where(last_row, jnp.broadcast_to(edge, shape), pltpu.roll(p, quarter - 1, 0))
                        flux.append(q_ref[which, g, c, i + 1] - q_ref[which, g, c, i] - (up - p))
                samples = synth({m: flux[2 * m - 2] for m in orders}, {m: flux[2 * m - 1] for m in orders}, NT)
                for k in range(NT):
                    time_ref[which * 3 + part, k] = samples[k]
        density = density_ref[chunk.lo + i, my_rows]
        region = region_ref[chunk.lo + i, my_rows]
        iron = region == 0
        share = jnp.where(iron, density * density * density, 0.0) * (1.0 - iron_floor)
        slope = jnp.where(iron, 3.0 * density * density, 0.0)
        base = jnp.where(region == 1, magnet_reluct, 1.0)
        total = jnp.zeros(shape, jnp.float32)
        for k in range(NT):
            b = [time_ref[j, k] for j in range(3)]
            a = [time_ref[3 + j, k] for j in range(3)]
            square = b[0] * b[0] + b[1] * b[1] + b[2] * b[2]
            inner = b[0] * a[0] + b[1] * a[1] + b[2] * a[2]
            inverse = 1.0 / (square + saturation)
            scaled = share * inverse
            reluct_now = base - scaled
            ratio = inverse * inner
            total = total + ratio
            along = scaled * ratio
            along = along + along
            for j in range(3):
                time_ref[j, k] = reluct_now * a[j] + along * b[j]
        grad_ref[i] = ((1.0 - iron_floor) / NT) * slope * total
        for part in (2, 0, 1):
            cos_of, sin_of = analyse([time_ref[part, k] for k in range(NT)], orders, NT)
            field = []
            for m in orders:
                field += [cos_of[m], sin_of[m]]
            if part == 2:
                for at in range(total_coefs):
                    third_ref[at] = field[at]
                psi = lane_sum(third_ref[...].reshape(total_coefs * quarter, width), False)
                third_ref[...] = psi.reshape(total_coefs, quarter, width)
            elif part == 0:
                for at, (g, c) in enumerate(place):
                    h0_ref[g, c, i] = field[at] + (psi_ref[g, c] - third_ref[at])
            else:
                for at, (g, c) in enumerate(place):
                    psi = third_ref[at]
                    down = jnp.where(first_row, 0.0, pltpu.roll(psi, 1, 0))
                    h1_ref[g, c, i] = field[at] + (down - psi)
                    tail_ref[g, pl.ds(c * n + i, 1), :] = psi[quarter - 1 : quarter]
                    psi_ref[g, c] = psi
        return carry

    lax.fori_loop(0, n, one_plane, 0)
    for g, c in place:
        if kind == 0:
            pending_ref[g, c] = h0_ref[g, c, 0]
            last_psi_ref[g, c] = psi_ref[g, c]
        elif kind == 1:
            h0_ref[g, c, n] = psi_ref[g, c]
        else:
            h0_ref[g, c, n] = edge_h_ref[g, c] + psi_ref[g, c]
    step = chunk.nh + n
    for r in range(groups):
        g = partner(me, r, groups)
        for c in range(coefs):
            out_refs[r][c * step : c * step + chunk.nh] = h0_ref[g, c, chunk.h_from : chunk.h_from + chunk.nh]
            out_refs[r][c * step + chunk.nh : (c + 1) * step] = h1_ref[g, c]
        for t in range(tiles_for(coefs * n, quarter)):
            out_refs[r][coefs * step + t] = tail_ref[g, t * quarter : (t + 1) * quarter]


def sample_fields(chunk, me, messages, density, region, coefs, edges):
    groups = len(messages)
    _, quarter, width = messages[0].shape
    n = chunk.n
    f32 = jnp.float32
    shapes = [jax.ShapeDtypeStruct((chunk.back(coefs, quarter), quarter, width), f32)] * groups
    shapes.append(jax.ShapeDtypeStruct((n, quarter, width), f32))
    if chunk.kind == 0:
        shapes += [jax.ShapeDtypeStruct((2, groups, coefs, quarter, width), f32)] * 2
        shapes += [jax.ShapeDtypeStruct((groups, coefs, quarter, width), f32)] * 2
    operands = [me, *messages, density, region, *edges]
    return pl.pallas_call(
        functools.partial(sample_kernel, chunk, groups, coefs),
        in_specs=[SMEM] + [VMEM] * (len(operands) - 1),
        out_specs=[VMEM] * len(shapes),
        out_shape=shapes,
        scratch_shapes=[
            pltpu.VMEM((2, groups, coefs, n, quarter, width), f32),
            pltpu.VMEM((2, groups, coefs, n + 1, quarter, width), f32),
            pltpu.VMEM((groups, tiles_for(2 * coefs * n, quarter) * quarter, width), f32),
            pltpu.VMEM((6, NT, quarter, width), f32),
            pltpu.VMEM((groups * coefs, quarter, width), f32),
            pltpu.VMEM((groups, coefs, quarter, width), f32),
            pltpu.VMEM((groups, coefs, n + 1, quarter, width), f32),
            pltpu.VMEM((groups, coefs, n, quarter, width), f32),
            pltpu.VMEM((groups, tiles_for(coefs * n, quarter) * quarter, width), f32),
        ],
        compiler_params=pltpu.CompilerParams(vmem_limit_bytes=SAMPLE_LIMIT),
        cost_estimate=pl.CostEstimate(flops=3 * 10**9, bytes_accessed=8 * 10**6, transcendentals=0),
        name="samples%d" % chunk.kind,
    )(*operands)


def last_plane_kernel(chunk, coefs, me_ref, *refs):
    groups = len(refs) - 2
    message_refs, out_ref, row_ref = refs[:groups], refs[groups], refs[groups + 1]
    quarter, width = message_refs[0].shape[1:]
    rows = quarter * groups
    step = chunk.nh + chunk.n
    me = me_ref[0]
    for c in range(coefs):
        for r in range(groups):
            here = pl.ds(pl.multiple_of(origin(me, r, groups) * quarter, quarter), quarter)
            row_ref[c, here] = message_refs[r][(c + 1) * step - 1]
            out_ref[c, 1, here] = message_refs[r][c * step + chunk.nh - 1]
        for r in range(groups):
            add_edge(row_ref.at[c], message_refs[r], chunk, coefs, c * chunk.n + chunk.n - 1, origin(me, r, groups) * quarter + quarter)
        out_ref[c, 0] = row_ref[c, 0:rows]


def add_edge(target, message_ref, chunk, coefs, spot, row):
    quarter = message_ref.shape[1]
    tile = coefs * (chunk.nh + chunk.n) + spot // quarter
    here = pl.ds(pl.multiple_of(row, quarter), 1)
    target[here] = target[here] + message_ref[tile, spot % quarter : spot % quarter + 1]


def last_plane(chunk, me, messages, coefs):
    groups = len(messages)
    _, quarter, width = messages[0].shape
    rows = groups * quarter
    return pl.pallas_call(
        functools.partial(last_plane_kernel, chunk, coefs),
        in_specs=[SMEM] + [VMEM] * groups,
        out_specs=VMEM,
        out_shape=jax.ShapeDtypeStruct((coefs, 2, rows, width), jnp.float32),
        scratch_shapes=[pltpu.VMEM((coefs, rows + quarter, width), jnp.float32)],
        name="last_plane",
    )(me, *messages)


def residual_kernel(chunks, groups, coefs, me_ref, *refs):
    message_refs = [refs[k * groups : (k + 1) * groups] for k in range(len(chunks))]
    halo_ref, objective_ref, out_ref, h0_ref, h1_ref = refs[len(chunks) * groups :]
    parts, planes, rows, width = objective_ref.shape[1:]
    quarter = rows // groups
    me = me_ref[0]
    row = lax.broadcasted_iota(jnp.int32, (rows, width), 0)
    lane = lax.broadcasted_iota(jnp.int32, (rows, width), 1)

    def lower_lane(v):
        return jnp.where(lane == 0, 0.0, pltpu.roll(v, 1, 1))

    def one_coef(c):
        for chunk, messages in zip(chunks, message_refs):
            n = chunk.n
            step = chunk.nh + n
            for r in range(groups):
                g = origin(me, r, groups)
                here = pl.ds(pl.multiple_of(g * quarter, quarter), quarter)
                count = chunk.h_to - chunk.h_from
                h0_ref[chunk.lo + chunk.h_from : chunk.lo + chunk.h_to, here] = messages[r][c * step : c * step + count]
                h1_ref[chunk.lo : chunk.hi, here] = messages[r][c * step + chunk.nh : (c + 1) * step]
            for r in range(groups):
                g = origin(me, r, groups)
                for i in range(n):
                    add_edge(h1_ref.at[chunk.lo + i], messages[r], chunk, coefs, c * n + i, g * quarter + quarter)
        before = halo_ref[c, 0]
        for i in range(planes):
            h0 = h0_ref[i]
            if i == 0:
                h0 = h0 + halo_ref[c, 1]
            h1 = h1_ref[i, 0:rows]
            out_ref[0, 0, i] = objective_ref[0, 0, i] - (2.0 / NT) * (lower_lane(h1) - h1)
            out_ref[0, 1, i] = objective_ref[0, 1, i] - (2.0 / NT) * (h0 - lower_lane(h0))
            lower_row = jnp.where(row == 0, 0.0, pltpu.roll(h0, 1, 0))
            out_ref[0, 2, i] = objective_ref[0, 2, i] - (2.0 / NT) * ((lower_row - h0) - (before - h1))
            before = h1

    for c in range(coefs):
        pl.when(pl.program_id(0) == c)(functools.partial(one_coef, c))


def residual(chunks, me, returned, halo, objective_hat):
    coefs, parts, planes, rows, width = objective_hat.shape
    groups = len(returned[0])
    quarter = rows // groups
    block = pl.BlockSpec((1, parts, planes, rows, width), lambda c: (c, 0, 0, 0, 0))
    operands = [m for messages in returned for m in messages]
    return pl.pallas_call(
        functools.partial(residual_kernel, chunks, groups, coefs),
        grid=(coefs,),
        in_specs=[SMEM] + [VMEM] * (len(operands) + 1) + [block],
        out_specs=block,
        out_shape=jax.ShapeDtypeStruct(objective_hat.shape, jnp.float32),
        scratch_shapes=[
            pltpu.VMEM((planes, rows, width), jnp.float32),
            pltpu.VMEM((planes, rows + quarter, width), jnp.float32),
        ],
        compiler_params=pltpu.CompilerParams(vmem_limit_bytes=RESIDUAL_LIMIT),
        name="residual",
    )(me, *operands, halo, objective_hat)


def local(state_hat, adjoint_hat, objective_hat, density, region):
    groups = lax.axis_size("sample")
    coefs, parts, planes, rows, width = state_hat.shape
    me = lax.axis_index("sample").astype(jnp.int32).reshape(1)
    first = planes // 4
    last = first + (planes - first) // 2
    middle_chunk, last_chunk, first_chunk = Chunk(0, first, last), Chunk(1, last, planes), Chunk(2, 0, first)
    upper = passed_along(jnp.stack([state_hat[:, 1:3, 0], adjoint_hat[:, 1:3, 0]], axis=0), "space", -1)
    sent0 = gauge(middle_chunk, groups, me, state_hat, adjoint_hat, jnp.zeros((8, 128), jnp.float32))
    cells0 = exchange(sent0)
    sent1 = gauge(last_chunk, groups, me, state_hat, adjoint_hat, upper)
    cells1 = exchange(sent1)
    sent2 = gauge(first_chunk, groups, me, state_hat, adjoint_hat, upper)
    cells2 = exchange(sent2)
    *out0, grad0, first_q, last_q, pending, last_psi = sample_fields(middle_chunk, me, cells0, density, region, coefs, ())
    back0 = exchange(out0)
    *out1, grad1 = sample_fields(last_chunk, me, cells1, density, region, coefs, (last_q, last_psi))
    back1 = exchange(out1)
    *out2, grad2 = sample_fields(first_chunk, me, cells2, density, region, coefs, (first_q, pending))
    back2 = exchange(out2)
    lower = passed_along(last_plane(last_chunk, me, back1, coefs), "space", 1)
    adjoint_residual = residual((middle_chunk, last_chunk, first_chunk), me, (back0, back1, back2), lower, objective_hat)
    return adjoint_residual, jnp.concatenate([grad2, grad0, grad1], axis=0)


def solution(mesh):
    in_specs = (
        P("sample", None, "space", None, None),
        P("sample", None, "space", None, None),
        P("sample", None, "space", None, None),
        P("space", None, None),
        P("space", None, None),
    )
    out_specs = (P("sample", None, "space", None, None), P("space", "sample", None))
    return jax.shard_map(local, mesh=mesh, in_specs=in_specs, out_specs=out_specs, check_vma=False)
```

time: 100 us -> 80.8 us (0.81)
  blocking collectives: 21.6 us -> 0 us
  waiting for transfers between devices: 51.3 us -> 35.6 us
  starting transfers between devices: 9.65 us -> 19.6 us
  Pallas kernels: 12.7 us -> 19 us
    all_to_all x1 -> x0, waiting for transfers between devices: 34.8 us -> none  [exchange(): lax.all_to_all(array, 'sample', split_axis=0, concat_axis=0, tiled=True)]
    ppermute x0 -> x18, waiting for transfers between devices: none -> 33.4 us  [exchange(): taken[r] = lax.ppermute(messages[r], 'sample', pairs)]
    all_to_all x1 -> x0, blocking collectives: 21.6 us -> none  [exchange(): lax.all_to_all(array, 'sample', split_axis=0, concat_axis=0, tiled=True)]
    ppermute x2, waiting for transfers between devices: 16.5 us -> 2.17 us  [passed_along(): return lax.ppermute(array, axis, pairs)]
    ppermute x0 -> x18, starting transfers between devices: none -> 13.7 us  [exchange(): taken[r] = lax.ppermute(messages[r], 'sample', pairs)]
    pallas_call x3 -> x8, Pallas kernels: 12.7 us -> 19 us  [the longest x3 7.7 us: gauge(): pl.pallas_call(functools.partial(gauge_kernel, chunk, groups), in_specs=[...]
    all_to_all x1 -> x0, starting transfers between devices: 3.81 us -> none  [exchange(): lax.all_to_all(array, 'sample', split_axis=0, concat_axis=0, tiled=True)]
    unnamed x10 -> x30, local copies, waits for them, and re-layouts: 3.1 us -> 3.79 us
  transfers between devices with their start and end apart: 3 -> 20, of which waited for: 3 -> 9; matrix products, arithmetic and copies ran while one was open for 0% -> 1% of each run, Pallas kernels for 0% -> 17%
where the time goes in v2:
time: 80.8 us; the launch traced here: 80.5 us
  waiting for transfers between devices  35.6 us (44%)
  starting transfers between devices  19.6 us (24%)
  Pallas kernels  19 us (24%)
  local copies, waits for them, and re-layouts  4.82 us (6%)
  between operations  0.86 us (1%)
    ppermute x18, waiting for transfers between devices, exchange(): taken[r] = lax.ppermute(messages[r], 'sample', pairs)  33.4 us
    ppermute x18, starting transfers between devices, exchange(): taken[r] = lax.ppermute(messages[r], 'sample', pairs)  13.7 us
    pallas_call x3, Pallas kernels, gauge(): pl.pallas_call(functools.partial(gauge_kernel, chunk, groups), in_specs=[...  7.7 us
    pallas_call x3, Pallas kernels, sample_fields(): pl.pallas_call(functools.partial(sample_kernel, chunk, groups, coefs), in...  6.5 us
    ppermute x2, starting transfers between devices, passed_along(): return lax.ppermute(array, axis, pairs)  5.84 us
    unnamed x30, local copies, waits for them, and re-layouts  3.79 us
    pallas_call x1, Pallas kernels, residual(): pl.pallas_call(functools.partial(residual_kernel, chunks, groups, coefs),...  2.92 us
    ppermute x2, waiting for transfers between devices, passed_along(): return lax.ppermute(array, axis, pairs)  2.17 us
  transfers between devices with their start and end apart: 20, of which 9 were waited for; matrix products, arithmetic and copies ran while one was open for 1% of the time, Pallas kernels for 17%

profile of v2, /device:TPU:0, one launch (start us, length us, event | category | flops | bytes accessed | tf_op | source)
XLA Modules:
  0.0 80.5 jit_solution(15284696121326715367)
XLA Ops:
  0.6 1.0 %slice_bitcast_fusion = (f32[1,5,2,32,128]{4,3,2,1,0:T(8,128)S(1)}, f32[1,5,2,32,128]{4,3,2,1,0:T(8,128)S(1)}) fusion(f32[5,3,8,32,128]{4,3,2,1,0:T(8,128)} %adjoint_ref.5, f32[5,3,8,32,128]{4,3,2,1,0:T(8,128)} %state_ref.5), kind=kLoop, calls=%fused_computation.1 | loop fusion | bytes 655360 | tf_op jit(solution)/shard_map/stack;squeeze | solution.py:506
  1.7 1.3 %collective-permute-start.6 = (f32[2,5,2,32,128]{4,3,2,1,0:T(8,128)S(1)}, f32[2,5,2,32,128]{4,3,2,1,0:T(8,128)S(1)}, u32[]{:S(2)}, u32[]{:S(2)}) collective-permute-start(f32[2,5,2,32,128]{4,3,2,1,0:T(8,128)S(1)} %pad_maximum_fusion), channel_id=1, source_target_pairs={{4,0},{8,4},{12,8},{16,12},{20,16},{24,20},{28,24},{5,1},{9,5},{13... | collective-permute-start | bytes 983048 | tf_op jit(solution)/shard_map/ppermute | solution.py:23
  3.0 0.0 copy-start.9
  3.0 1.5 %copy-done.9 = f32[5,3,8,32,128]{4,3,2,1,0:T(8,128)S(1)} copy-done((f32[5,3,8,32,128]{4,3,2,1,0:T(8,128)S(1)}, f32[5,3,8,32,128]{4,3,2,1,0:T(8,128)}, u32[]{:S(2)}) %copy-start.9) | copy-done | bytes 1966104
  4.6 1.5 %copy-done.11 = f32[5,3,8,32,128]{4,3,2,1,0:T(8,128)S(1)} copy-done((f32[5,3,8,32,128]{4,3,2,1,0:T(8,128)S(1)}, f32[5,3,8,32,128]{4,3,2,1,0:T(8,128)}, u32[]{:S(2)}) %copy-start.11) | copy-done | bytes 1966104
  6.1 2.8 %gauge0.1 = (f32[74,8,128]{2,1,0:T(8,128)S(1)}, f32[74,8,128]{2,1,0:T(8,128)S(1)}, f32[74,8,128]{2,1,0:T(8,128)S(1)}, f32[74,8,128]{2,1,0:T(8,128)S(1)}) custom-call(s32[1]{0:T(128)} %bitcast.me_ref.refs_0_, f32[5,3,8,32,128]{4,3,2,1,0:T(8,128)S(1)} %copy-done.9, f32[5,3,8,32,128]{4,3,2,1,0:T(8,128)S(1)} %copy-done.11, f32[8,128]{1,0:T(8,128)S(1)} %broadcast_in_dim.3.halo_ref), custom_call_target="tpu_custom_call" | custom-call | flops 2000000000 | bytes 4000000 | tf_op jit(solution)/shard_map/gauge0/pallas_call | solution.py:214
  8.9 0.5 collective-permute-start
  9.4 2.6 %collective-permute-start.1 = (f32[74,8,128]{2,1,0:T(8,128)S(1)}, f32[74,8,128]{2,1,0:T(8,128)S(1)}, u32[]{:S(2)}, u32[]{:S(2)}) collective-permute-start(f32[74,8,128]{2,1,0:T(8,128)S(1)} %get-tuple-element.35), channel_id=1, source_target_pairs={{0,2},{1,3},{2,0},{3,1},{4,6},{5,7},{6,4},{7,5},{8,10},{9,11},{10,... | collective-permute-start | bytes 909320 | tf_op jit(solution)/shard_map/ppermute | solution.py:140
  12.0 0.1 collective-permute-start.2
  12.1 2.2 %collective-permute-done.6.halo_ref = f32[2,5,2,32,128]{4,3,2,1,0:T(8,128)S(1)} collective-permute-done((f32[2,5,2,32,128]{4,3,2,1,0:T(8,128)S(1)}, f32[2,5,2,32,128]{4,3,2,1,0:T(8,128)S(1)}, u32[]{:S(2)}, u32[]{:S(2)}) %collective-permute-start.6) | collective-permute-done | bytes 327712 | tf_op jit(solution)/shard_map/ppermute | solution.py:23
  14.2 2.5 %gauge1.1 = (f32[64,8,128]{2,1,0:T(8,128)S(1)}, f32[64,8,128]{2,1,0:T(8,128)S(1)}, f32[64,8,128]{2,1,0:T(8,128)S(1)}, f32[64,8,128]{2,1,0:T(8,128)S(1)}) custom-call(s32[1]{0:T(128)} %bitcast.me_ref.refs_0_, f32[5,3,8,32,128]{4,3,2,1,0:T(8,128)S(1)} %copy-done.9, f32[5,3,8,32,128]{4,3,2,1,0:T(8,128)S(1)} %copy-done.11, ...), custom_call_target="tpu_custom_call" | custom-call | flops 2000000000 | bytes 4000000 | tf_op jit(solution)/shard_map/gauge1/pallas_call | solution.py:214
  16.8 0.1 collective-permute-start.7
  16.9 1.8 %collective-permute-start.8 = (f32[64,8,128]{2,1,0:T(8,128)S(1)}, f32[64,8,128]{2,1,0:T(8,128)S(1)}, u32[]{:S(2)}, u32[]{:S(2)}) collective-permute-start(f32[64,8,128]{2,1,0:T(8,128)S(1)} %get-tuple-element.43), channel_id=1, source_target_pairs={{0,2},{1,3},{2,0},{3,1},{4,6},{5,7},{6,4},{7,5},{8,10},{9,11},{10,... | collective-permute-start | bytes 786440 | tf_op jit(solution)/shard_map/ppermute | solution.py:140
  18.7 0.0 collective-permute-done.refs_2_
  18.7 0.1 collective-permute-start.9
  18.8 1.3 %collective-permute-done.1.refs_3_ = f32[74,8,128]{2,1,0:T(8,128)S(1)} collective-permute-done((f32[74,8,128]{2,1,0:T(8,128)S(1)}, f32[74,8,128]{2,1,0:T(8,128)S(1)}, u32[]{:S(2)}, u32[]{:S(2)}) %collective-permute-start.1) | collective-permute-done | bytes 303136 | tf_op jit(solution)/shard_map/ppermute | solution.py:140
  20.0 6.0 %collective-permute-done.2.refs_4_ = f32[74,8,128]{2,1,0:T(8,128)S(1)} collective-permute-done((f32[74,8,128]{2,1,0:T(8,128)S(1)}, f32[74,8,128]{2,1,0:T(8,128)S(1)}, u32[]{:S(2)}, u32[]{:S(2)}) %collective-permute-start.2) | collective-permute-done | bytes 303136 | tf_op jit(solution)/shard_map/ppermute | solution.py:140
  26.0 2.4 %samples0.1 = (f32[27,8,128]{2,1,0:T(8,128)S(1)}, f32[27,8,128]{2,1,0:T(8,128)S(1)}, f32[27,8,128]{2,1,0:T(8,128)S(1)}, f32[27,8,128]{2,1,0:T(8,128)S(1)}, f32[3...) custom-call(s32[1]{0:T(128)} %bitcast.me_ref.refs_0_, ...), custom_call_target="tpu_custom_call" | custom-call | flops 3000000000 | bytes 8000000 | tf_op jit(solution)/shard_map/samples0/pallas_call | solution.py:376
  28.5 0.0 collective-permute-done.7.refs_2_
  28.5 3.7 %collective-permute-done.8.refs_3_ = f32[64,8,128]{2,1,0:T(8,128)S(1)} collective-permute-done((f32[64,8,128]{2,1,0:T(8,128)S(1)}, f32[64,8,128]{2,1,0:T(8,128)S(1)}, u32[]{:S(2)}, u32[]{:S(2)}) %collective-permute-start.8) | collective-permute-done | bytes 262176 | tf_op jit(solution)/shard_map/ppermute | solution.py:140
  32.1 5.1 %collective-permute-done.9.refs_4_ = f32[64,8,128]{2,1,0:T(8,128)S(1)} collective-permute-done((f32[64,8,128]{2,1,0:T(8,128)S(1)}, f32[64,8,128]{2,1,0:T(8,128)S(1)}, u32[]{:S(2)}, u32[]{:S(2)}) %collective-permute-start.9) | collective-permute-done | bytes 262176 | tf_op jit(solution)/shard_map/ppermute | solution.py:140
  37.2 2.4 %samples1.1 = (f32[37,8,128]{2,1,0:T(8,128)S(1)}, f32[37,8,128]{2,1,0:T(8,128)S(1)}, f32[37,8,128]{2,1,0:T(8,128)S(1)}, f32[37,8,128]{2,1,0:T(8,128)S(1)}, f32[3,8,128]{2,1,0:T(8,128)S(1)}) custom-call(s32[1]{0:T(128)} %bitcast.me_ref.refs_0_, f32[64,8,128]{2,1,0:T(8,128)S(1)} %get-tuple-element.41.refs_1_, ...), custom_call_target="tpu_custom_call" | custom-call | flops 3000000000 | bytes 8000000 | tf_op jit(solution)/shard_map/samples1/pallas_call | solution.py:376
  39.7 0.6 copy-done.1
  40.4 0.1 collective-permute-start.10
  40.5 2.4 %gauge2.1 = (f32[43,8,128]{2,1,0:T(8,128)S(1)}, f32[43,8,128]{2,1,0:T(8,128)S(1)}, f32[43,8,128]{2,1,0:T(8,128)S(1)}, f32[43,8,128]{2,1,0:T(8,128)S(1)}) custom-call(s32[1]{0:T(128)} %bitcast.me_ref.refs_0_, f32[5,3,8,32,128]{4,3,2,1,0:T(8,128)S(1)} %copy-done.10, f32[5,3,8,32,128]{4,3,2,1,0:T(8,128)S(1)} %copy-done.12, ...), custom_call_target="tpu_custom_call" | custom-call | flops 2000000000 | bytes 4000000 | tf_op jit(solution)/shard_map/gauge2/pallas_call | solution.py:214
  42.9 0.5 collective-permute-start.13
  43.3 1.6 %collective-permute-start.14 = (f32[43,8,128]{2,1,0:T(8,128)S(1)}, f32[43,8,128]{2,1,0:T(8,128)S(1)}, u32[]{:S(2)}, u32[]{:S(2)}) collective-permute-start(f32[43,8,128]{2,1,0:T(8,128)S(1)} %get-tuple-element.53), channel_id=1, source_target_pairs={{0,2},{1,3},{2,0},{3,1},{4,6},{5,7},{6,4},{7,5},{8,10},{9,11},{10,... | collective-permute-start | bytes 528392 | tf_op jit(solution)/shard_map/ppermute | solution.py:140
  44.9 0.0 collective-permute-start.15
  44.9 1.6 %collective-permute-start.11 = (f32[37,8,128]{2,1,0:T(8,128)S(1)}, f32[37,8,128]{2,1,0:T(8,128)S(1)}, u32[]{:S(2)}, u32[]{:S(2)}) collective-permute-start(f32[37,8,128]{2,1,0:T(8,128)S(1)} %get-tuple-element.49), channel_id=1, source_target_pairs={{0,2},{1,3},{2,0},{3,1},{4,6},{5,7},{6,4},{7,5},{8,10},{9,11},{10,... | collective-permute-start | bytes 454664 | tf_op jit(solution)/shard_map/ppermute | solution.py:140
  46.6 0.3 collective-permute-start.12
  46.8 10.8 %collective-permute-done.11.refs_2_.refs_6_ = f32[37,8,128]{2,1,0:T(8,128)S(1)} collective-permute-done((f32[37,8,128]{2,1,0:T(8,128)S(1)}, f32[37,8,128]{2,1,0:T(8,128)S(1)}, u32[]{:S(2)}, u32[]{:S(2)}) %collective-permute-start.11) | collective-permute-done | bytes 151584 | tf_op jit(solution)/shard_map/ppermute | solution.py:140
  57.7 1.7 %collective-permute-done.12.refs_3_.refs_7_ = f32[37,8,128]{2,1,0:T(8,128)S(1)} collective-permute-done((f32[37,8,128]{2,1,0:T(8,128)S(1)}, f32[37,8,128]{2,1,0:T(8,128)S(1)}, u32[]{:S(2)}, u32[]{:S(2)}) %collective-permute-start.12) | collective-permute-done | bytes 151584 | tf_op jit(solution)/shard_map/ppermute | solution.py:140
  59.4 1.8 %collective-permute-start.4 = (f32[27,8,128]{2,1,0:T(8,128)S(1)}, f32[27,8,128]{2,1,0:T(8,128)S(1)}, u32[]{:S(2)}, u32[]{:S(2)}) collective-permute-start(f32[27,8,128]{2,1,0:T(8,128)S(1)} %get-tuple-element.39), channel_id=1, source_target_pairs={{0,2},{1,3},{2,0},{3,1},{4,6},{5,7},{6,4},{7,5},{8,10},{9,11},{10,... | collective-permute-start | bytes 331784 | tf_op jit(solution)/shard_map/ppermute | solution.py:140
  61.2 1.9 %last_plane.1 = f32[5,2,32,128]{3,2,1,0:T(8,128)} custom-call(s32[1]{0:T(128)} %bitcast.me_ref.refs_0_, f32[37,8,128]{2,1,0:T(8,128)} %copy-done.1, f32[37,8,128]{2,1,0:T(8,128)} %copy-done.3, f32[37,8,128]{2,1,0:T(8,128)} %copy-done.5, f32[37,8,128]{2,1,0:T(8,128)} %copy-done.7), custom_call_target="tpu_custom_call" | custom-call | tf_op jit(solution)/shard_map/last_plane/pallas_call | solution.py:426
  63.1 0.7 collective-permute-start.5
  63.8 0.0 collective-permute-done.14.refs_3_
  63.8 4.5 %collective-permute-start.19 = (f32[5,2,32,128]{3,2,1,0:T(8,128)}, f32[5,2,32,128]{3,2,1,0:T(8,128)S(1)}, u32[]{:S(2)}, u32[]{:S(2)}) collective-permute-start(f32[5,2,32,128]{3,2,1,0:T(8,128)} %last_plane.1), channel_id=1, source_target_pairs={{0,4},{4,8},{8,12},{12,16},{16,20},{20,24},{24,28},{1,5},{5,9},{9,... | collective-permute-start | bytes 491528 | tf_op jit(solution)/shard_map/ppermute | solution.py:23
  68.4 0.0 copy-start
  68.4 1.6 %samples2.1 = (f32[27,8,128]{2,1,0:T(8,128)S(1)}, f32[27,8,128]{2,1,0:T(8,128)S(1)}, f32[27,8,128]{2,1,0:T(8,128)S(1)}, f32[27,8,128]{2,1,0:T(8,128)S(1)}, f32[2,8,128]{2,1,0:T(8,128)S(1)}) custom-call(s32[1]{0:T(128)} %bitcast.me_ref.refs_0_, f32[43,8,128]{2,1,0:T(8,128)S(1)} %get-tuple-element.51.refs_1_, ...), custom_call_target="tpu_custom_call" | custom-call | flops 3000000000 | bytes 8000000 | tf_op jit(solution)/shard_map/samples2/pallas_call | solution.py:376
  70.1 0.1 collective-permute-start.16
  70.2 1.2 %collective-permute-start.17 = (f32[27,8,128]{2,1,0:T(8,128)S(1)}, f32[27,8,128]{2,1,0:T(8,128)S(1)}, u32[]{:S(2)}, u32[]{:S(2)}) collective-permute-start(f32[27,8,128]{2,1,0:T(8,128)S(1)} %get-tuple-element.59), channel_id=1, source_target_pairs={{0,2},{1,3},{2,0},{3,1},{4,6},{5,7},{6,4},{7,5},{8,10},{9,11},{10,... | collective-permute-start | bytes 331784 | tf_op jit(solution)/shard_map/ppermute | solution.py:140
  71.3 0.7 collective-permute-start.18
  72.0 0.6 pad_maximum_fusion.1
  72.7 0.0 collective-permute-done.5.refs_3_
  72.7 0.0 collective-permute-done.16.refs_9_
  72.7 3.4 %collective-permute-done.17.refs_10_ = f32[27,8,128]{2,1,0:T(8,128)S(1)} collective-permute-done((f32[27,8,128]{2,1,0:T(8,128)S(1)}, f32[27,8,128]{2,1,0:T(8,128)S(1)}, u32[]{:S(2)}, u32[]{:S(2)}) %collective-permute-start.17) | collective-permute-done | bytes 110624 | tf_op jit(solution)/shard_map/ppermute | solution.py:140
  76.1 1.4 %collective-permute-done.18.refs_11_ = f32[27,8,128]{2,1,0:T(8,128)S(1)} collective-permute-done((f32[27,8,128]{2,1,0:T(8,128)S(1)}, f32[27,8,128]{2,1,0:T(8,128)S(1)}, u32[]{:S(2)}, u32[]{:S(2)}) %collective-permute-start.18) | collective-permute-done | bytes 110624 | tf_op jit(solution)/shard_map/ppermute | solution.py:140
  77.6 2.9 %residual.1 = f32[5,3,8,32,128]{4,3,2,1,0:T(8,128)} custom-call(s32[1]{0:T(128)} %bitcast.me_ref.refs_0_, f32[27,8,128]{2,1,0:T(8,128)S(1)} %get-tuple-element.37.refs_0_, f32[27,8,128]{2,1,0:T(8,128)S(1)} %collective-permute-done.3.refs_1_, f32[27,8,128]{2,1,0:T(8,128)S(1)} %collective-permute-done.4.refs_2_, ...), custom_call_target="tpu_custom_call" | custom-call | tf_op jit(solution)/shard_map/residual/pallas_call | solution.py:484
  (34 shorter events, 0.1 us)
Async XLA Ops:
  1.7 12.5 %collective-permute-start.6 = (f32[2,5,2,32,128]{4,3,2,1,0:T(8,128)S(1)}, f32[2,5,2,32,128]{4,3,2,1,0:T(8,128)S(1)}, u32[]{:S(2)}, u32[]{:S(2)}) collective-permute-start(f32[2,5,2,32,128]{4,3,2,1,0:T(8,128)S(1)} %pad_maximum_fusion), channel_id=1, source_target_pairs={{4,0},{8,4},{12,8},{16,12},{20,16},{24,20},{28,24},{5,1},{9,5},{13... | collective-permute-start | bytes 983048 | tf_op jit(solution)/shard_map/ppermute | solution.py:23
  3.0 1.5 %copy-start.9 = (f32[5,3,8,32,128]{4,3,2,1,0:T(8,128)S(1)}, f32[5,3,8,32,128]{4,3,2,1,0:T(8,128)}, u32[]{:S(2)}) copy-start(f32[5,3,8,32,128]{4,3,2,1,0:T(8,128)} %state_ref.5) | copy-start | bytes 5898244
  4.6 1.5 %copy-start.11 = (f32[5,3,8,32,128]{4,3,2,1,0:T(8,128)S(1)}, f32[5,3,8,32,128]{4,3,2,1,0:T(8,128)}, u32[]{:S(2)}) copy-start(f32[5,3,8,32,128]{4,3,2,1,0:T(8,128)} %adjoint_ref.5) | copy-start | bytes 5898244
  8.9 9.8 %collective-permute-start = (f32[74,8,128]{2,1,0:T(8,128)S(1)}, f32[74,8,128]{2,1,0:T(8,128)S(1)}, u32[]{:S(2)}, u32[]{:S(2)}) collective-permute-start(f32[74,8,128]{2,1,0:T(8,128)S(1)} %get-tuple-element.34), channel_id=1, source_target_pairs={{0,1},{1,0},{2,3},{3,2},{4,5},{5,4},{6,7},{7,6},{8,9},{9,8},{10,11... | collective-permute-start | bytes 909320 | tf_op jit(solution)/shard_map/ppermute | solution.py:140
  9.4 10.6 %collective-permute-start.1 = (f32[74,8,128]{2,1,0:T(8,128)S(1)}, f32[74,8,128]{2,1,0:T(8,128)S(1)}, u32[]{:S(2)}, u32[]{:S(2)}) collective-permute-start(f32[74,8,128]{2,1,0:T(8,128)S(1)} %get-tuple-element.35), channel_id=1, source_target_pairs={{0,2},{1,3},{2,0},{3,1},{4,6},{5,7},{6,4},{7,5},{8,10},{9,11},{10,... | collective-permute-start | bytes 909320 | tf_op jit(solution)/shard_map/ppermute | solution.py:140
  12.0 14.0 %copy-start.13 = (f32[8,32,128]{2,1,0:T(8,128)S(1)}, f32[8,32,128]{2,1,0:T(8,128)}, u32[]{:S(2)}) copy-start(f32[8,32,128]{2,1,0:T(8,128)} %refs_5_.5) | copy-start | bytes 393220
  12.0 14.0 %copy-start.14 = (s32[8,32,128]{2,1,0:T(8,128)S(1)}, s32[8,32,128]{2,1,0:T(8,128)}, u32[]{:S(2)}) copy-start(s32[8,32,128]{2,1,0:T(8,128)} %refs_6_.5) | copy-start | bytes 393220
  12.0 14.0 %collective-permute-start.2 = (f32[74,8,128]{2,1,0:T(8,128)S(1)}, f32[74,8,128]{2,1,0:T(8,128)S(1)}, u32[]{:S(2)}, u32[]{:S(2)}) collective-permute-start(f32[74,8,128]{2,1,0:T(8,128)S(1)} %get-tuple-element.36), channel_id=1, source_target_pairs={{0,3},{1,2},{2,1},{3,0},{4,7},{5,6},{6,5},{7,4},{8,11},{9,10},{10,... | collective-permute-start | bytes 909320 | tf_op jit(solution)/shard_map/ppermute | solution.py:140
  16.8 11.7 %collective-permute-start.7 = (f32[64,8,128]{2,1,0:T(8,128)S(1)}, f32[64,8,128]{2,1,0:T(8,128)S(1)}, u32[]{:S(2)}, u32[]{:S(2)}) collective-permute-start(f32[64,8,128]{2,1,0:T(8,128)S(1)} %get-tuple-element.42), channel_id=1, source_target_pairs={{0,1},{1,0},{2,3},{3,2},{4,5},{5,4},{6,7},{7,6},{8,9},{9,8},{10,11... | collective-permute-start | bytes 786440 | tf_op jit(solution)/shard_map/ppermute | solution.py:140
  16.9 15.3 %collective-permute-start.8 = (f32[64,8,128]{2,1,0:T(8,128)S(1)}, f32[64,8,128]{2,1,0:T(8,128)S(1)}, u32[]{:S(2)}, u32[]{:S(2)}) collective-permute-start(f32[64,8,128]{2,1,0:T(8,128)S(1)} %get-tuple-element.43), channel_id=1, source_target_pairs={{0,2},{1,3},{2,0},{3,1},{4,6},{5,7},{6,4},{7,5},{8,10},{9,11},{10,... | collective-permute-start | bytes 786440 | tf_op jit(solution)/shard_map/ppermute | solution.py:140
  18.7 18.5 %collective-permute-start.9 = (f32[64,8,128]{2,1,0:T(8,128)S(1)}, f32[64,8,128]{2,1,0:T(8,128)S(1)}, u32[]{:S(2)}, u32[]{:S(2)}) collective-permute-start(f32[64,8,128]{2,1,0:T(8,128)S(1)} %get-tuple-element.44), channel_id=1, source_target_pairs={{0,3},{1,2},{2,1},{3,0},{4,7},{5,6},{6,5},{7,4},{8,11},{9,10},{10,... | collective-permute-start | bytes 786440 | tf_op jit(solution)/shard_map/ppermute | solution.py:140
  37.2 3.2 %copy-start.10 = (f32[5,3,8,32,128]{4,3,2,1,0:T(8,128)S(1)}, f32[5,3,8,32,128]{4,3,2,1,0:T(8,128)}, u32[]{:S(2)}) copy-start(f32[5,3,8,32,128]{4,3,2,1,0:T(8,128)} %state_ref.5) | copy-start | bytes 5898244
  37.2 3.2 %copy-start.12 = (f32[5,3,8,32,128]{4,3,2,1,0:T(8,128)S(1)}, f32[5,3,8,32,128]{4,3,2,1,0:T(8,128)}, u32[]{:S(2)}) copy-start(f32[5,3,8,32,128]{4,3,2,1,0:T(8,128)} %adjoint_ref.5) | copy-start | bytes 5898244
  39.7 0.7 copy-start.1
  40.4 6.2 %collective-permute-start.10 = (f32[37,8,128]{2,1,0:T(8,128)S(1)}, f32[37,8,128]{2,1,0:T(8,128)S(1)}, u32[]{:S(2)}, u32[]{:S(2)}) collective-permute-start(f32[37,8,128]{2,1,0:T(8,128)S(1)} %get-tuple-element.48), channel_id=1, source_target_pairs={{0,1},{1,0},{2,3},{3,2},{4,5},{5,4},{6,7},{7,6},{8,9},{9,8},{10,11... | collective-permute-start | bytes 454664 | tf_op jit(solution)/shard_map/ppermute | solution.py:140
  42.9 20.2 %collective-permute-start.13 = (f32[43,8,128]{2,1,0:T(8,128)S(1)}, f32[43,8,128]{2,1,0:T(8,128)S(1)}, u32[]{:S(2)}, u32[]{:S(2)}) collective-permute-start(f32[43,8,128]{2,1,0:T(8,128)S(1)} %get-tuple-element.52), channel_id=1, source_target_pairs={{0,1},{1,0},{2,3},{3,2},{4,5},{5,4},{6,7},{7,6},{8,9},{9,8},{10,11... | collective-permute-start | bytes 528392 | tf_op jit(solution)/shard_map/ppermute | solution.py:140
  43.3 20.5 %collective-permute-start.14 = (f32[43,8,128]{2,1,0:T(8,128)S(1)}, f32[43,8,128]{2,1,0:T(8,128)S(1)}, u32[]{:S(2)}, u32[]{:S(2)}) collective-permute-start(f32[43,8,128]{2,1,0:T(8,128)S(1)} %get-tuple-element.53), channel_id=1, source_target_pairs={{0,2},{1,3},{2,0},{3,1},{4,6},{5,7},{6,4},{7,5},{8,10},{9,11},{10,... | collective-permute-start | bytes 528392 | tf_op jit(solution)/shard_map/ppermute | solution.py:140
  44.9 23.5 %collective-permute-start.15 = (f32[43,8,128]{2,1,0:T(8,128)S(1)}, f32[43,8,128]{2,1,0:T(8,128)S(1)}, u32[]{:S(2)}, u32[]{:S(2)}) collective-permute-start(f32[43,8,128]{2,1,0:T(8,128)S(1)} %get-tuple-element.54), channel_id=1, source_target_pairs={{0,3},{1,2},{2,1},{3,0},{4,7},{5,6},{6,5},{7,4},{8,11},{9,10},{10,... | collective-permute-start | bytes 528392 | tf_op jit(solution)/shard_map/ppermute | solution.py:140
  44.9 12.8 %collective-permute-start.11 = (f32[37,8,128]{2,1,0:T(8,128)S(1)}, f32[37,8,128]{2,1,0:T(8,128)S(1)}, u32[]{:S(2)}, u32[]{:S(2)}) collective-permute-start(f32[37,8,128]{2,1,0:T(8,128)S(1)} %get-tuple-element.49), channel_id=1, source_target_pairs={{0,2},{1,3},{2,0},{3,1},{4,6},{5,7},{6,4},{7,5},{8,10},{9,11},{10,... | collective-permute-start | bytes 454664 | tf_op jit(solution)/shard_map/ppermute | solution.py:140
  46.6 14.7 %copy-start.3 = (f32[37,8,128]{2,1,0:T(8,128)}, f32[37,8,128]{2,1,0:T(8,128)S(1)}, u32[]{:S(2)}) copy-start(f32[37,8,128]{2,1,0:T(8,128)S(1)} %collective-permute-done.10.refs_1_.refs_5_) | copy-start | bytes 454660
  46.6 12.8 %collective-permute-start.12 = (f32[37,8,128]{2,1,0:T(8,128)S(1)}, f32[37,8,128]{2,1,0:T(8,128)S(1)}, u32[]{:S(2)}, u32[]{:S(2)}) collective-permute-start(f32[37,8,128]{2,1,0:T(8,128)S(1)} %get-tuple-element.50), channel_id=1, source_target_pairs={{0,3},{1,2},{2,1},{3,0},{4,7},{5,6},{6,5},{7,4},{8,11},{9,10},{10,... | collective-permute-start | bytes 454664 | tf_op jit(solution)/shard_map/ppermute | solution.py:140
  57.7 3.5 %copy-start.5 = (f32[37,8,128]{2,1,0:T(8,128)}, f32[37,8,128]{2,1,0:T(8,128)S(1)}, u32[]{:S(2)}) copy-start(f32[37,8,128]{2,1,0:T(8,128)S(1)} %collective-permute-done.11.refs_2_.refs_6_) | copy-start | bytes 454660
  57.7 12.5 %collective-permute-start.3 = (f32[27,8,128]{2,1,0:T(8,128)S(1)}, f32[27,8,128]{2,1,0:T(8,128)S(1)}, u32[]{:S(2)}, u32[]{:S(2)}) collective-permute-start(f32[27,8,128]{2,1,0:T(8,128)S(1)} %get-tuple-element.38), channel_id=1, source_target_pairs={{0,1},{1,0},{2,3},{3,2},{4,5},{5,4},{6,7},{7,6},{8,9},{9,8},{10,11... | collective-permute-start | bytes 331784 | tf_op jit(solution)/shard_map/ppermute | solution.py:140
  59.4 1.9 %copy-start.7 = (f32[37,8,128]{2,1,0:T(8,128)}, f32[37,8,128]{2,1,0:T(8,128)S(1)}, u32[]{:S(2)}) copy-start(f32[37,8,128]{2,1,0:T(8,128)S(1)} %collective-permute-done.12.refs_3_.refs_7_) | copy-start | bytes 454660
  59.4 12.0 %collective-permute-start.4 = (f32[27,8,128]{2,1,0:T(8,128)S(1)}, f32[27,8,128]{2,1,0:T(8,128)S(1)}, u32[]{:S(2)}, u32[]{:S(2)}) collective-permute-start(f32[27,8,128]{2,1,0:T(8,128)S(1)} %get-tuple-element.39), channel_id=1, source_target_pairs={{0,2},{1,3},{2,0},{3,1},{4,6},{5,7},{6,4},{7,5},{8,10},{9,11},{10,... | collective-permute-start | bytes 331784 | tf_op jit(solution)/shard_map/ppermute | solution.py:140
  63.1 9.5 %collective-permute-start.5 = (f32[27,8,128]{2,1,0:T(8,128)S(1)}, f32[27,8,128]{2,1,0:T(8,128)S(1)}, u32[]{:S(2)}, u32[]{:S(2)}) collective-permute-start(f32[27,8,128]{2,1,0:T(8,128)S(1)} %get-tuple-element.40), channel_id=1, source_target_pairs={{0,3},{1,2},{2,1},{3,0},{4,7},{5,6},{6,5},{7,4},{8,11},{9,10},{10,... | collective-permute-start | bytes 331784 | tf_op jit(solution)/shard_map/ppermute | solution.py:140
  63.8 13.7 %collective-permute-start.19 = (f32[5,2,32,128]{3,2,1,0:T(8,128)}, f32[5,2,32,128]{3,2,1,0:T(8,128)S(1)}, u32[]{:S(2)}, u32[]{:S(2)}) collective-permute-start(f32[5,2,32,128]{3,2,1,0:T(8,128)} %last_plane.1), channel_id=1, source_target_pairs={{0,4},{4,8},{8,12},{12,16},{16,20},{20,24},{24,28},{1,5},{5,9},{9,... | collective-permute-start | bytes 491528 | tf_op jit(solution)/shard_map/ppermute | solution.py:23
  68.4 9.2 %copy-start = (f32[5,3,8,32,128]{4,3,2,1,0:T(8,128)S(1)}, f32[5,3,8,32,128]{4,3,2,1,0:T(8,128)}, u32[]{:S(2)}) copy-start(f32[5,3,8,32,128]{4,3,2,1,0:T(8,128)} %refs_13_.1) | copy-start | bytes 5898244
  68.4 9.1 %copy-start.2 = (f32[37,8,128]{2,1,0:T(8,128)S(1)}, f32[37,8,128]{2,1,0:T(8,128)}, u32[]{:S(2)}) copy-start(f32[37,8,128]{2,1,0:T(8,128)} %copy-done.1) | copy-start | bytes 454660
  68.4 9.1 %copy-start.4 = (f32[37,8,128]{2,1,0:T(8,128)S(1)}, f32[37,8,128]{2,1,0:T(8,128)}, u32[]{:S(2)}) copy-start(f32[37,8,128]{2,1,0:T(8,128)} %copy-done.3) | copy-start | bytes 454660
  68.4 9.1 %copy-start.6 = (f32[37,8,128]{2,1,0:T(8,128)S(1)}, f32[37,8,128]{2,1,0:T(8,128)}, u32[]{:S(2)}) copy-start(f32[37,8,128]{2,1,0:T(8,128)} %copy-done.5) | copy-start | bytes 454660
  68.4 9.1 %copy-start.8 = (f32[37,8,128]{2,1,0:T(8,128)S(1)}, f32[37,8,128]{2,1,0:T(8,128)}, u32[]{:S(2)}) copy-start(f32[37,8,128]{2,1,0:T(8,128)} %copy-done.7) | copy-start | bytes 454660
  70.1 2.6 %collective-permute-start.16 = (f32[27,8,128]{2,1,0:T(8,128)S(1)}, f32[27,8,128]{2,1,0:T(8,128)S(1)}, u32[]{:S(2)}, u32[]{:S(2)}) collective-permute-start(f32[27,8,128]{2,1,0:T(8,128)S(1)} %get-tuple-element.58), channel_id=1, source_target_pairs={{0,1},{1,0},{2,3},{3,2},{4,5},{5,4},{6,7},{7,6},{8,9},{9,8},{10,11... | collective-permute-start | bytes 331784 | tf_op jit(solution)/shard_map/ppermute | solution.py:140
  70.2 5.9 %collective-permute-start.17 = (f32[27,8,128]{2,1,0:T(8,128)S(1)}, f32[27,8,128]{2,1,0:T(8,128)S(1)}, u32[]{:S(2)}, u32[]{:S(2)}) collective-permute-start(f32[27,8,128]{2,1,0:T(8,128)S(1)} %get-tuple-element.59), channel_id=1, source_target_pairs={{0,2},{1,3},{2,0},{3,1},{4,6},{5,7},{6,4},{7,5},{8,10},{9,11},{10,... | collective-permute-start | bytes 331784 | tf_op jit(solution)/shard_map/ppermute | solution.py:140
  71.3 6.2 %collective-permute-start.18 = (f32[27,8,128]{2,1,0:T(8,128)S(1)}, f32[27,8,128]{2,1,0:T(8,128)S(1)}, u32[]{:S(2)}, u32[]{:S(2)}) collective-permute-start(f32[27,8,128]{2,1,0:T(8,128)S(1)} %get-tuple-element.60), channel_id=1, source_target_pairs={{0,3},{1,2},{2,1},{3,0},{4,7},{5,6},{6,5},{7,4},{8,11},{9,10},{10,... | collective-permute-start | bytes 331784 | tf_op jit(solution)/shard_map/ppermute | solution.py:140

commit v3 on v2

--- a/solution.py
+++ b/solution.py
@@ -13,6 +13,7 @@
 iron_floor = 0.05
 saturation = 1.0
 GAUGE_LIMIT = 16 * 1024 * 1024
+FIRST_LIMIT = 62 * 1024 * 1024
 SAMPLE_LIMIT = 16 * 1024 * 1024
 RESIDUAL_LIMIT = 16 * 1024 * 1024
 
@@ -148,10 +149,13 @@
 VMEM = pl.BlockSpec(memory_space=pltpu.VMEM)
 SMEM = pl.BlockSpec(memory_space=pltpu.SMEM)
 HBM = pl.BlockSpec(memory_space=pltpu.HBM)
+ANY = pl.BlockSpec(memory_space=pl.ANY)
+LITTLE = pl.CostEstimate(flops=1000, bytes_accessed=1000, transcendentals=0)
 
 
 class Chunk:
-    def __init__(self, kind, lo, hi):
+    def __init__(self, kind, lo, hi, at=0):
+        self.at = at
         self.kind, self.lo, self.hi, self.n = kind, lo, hi, hi - lo
         self.q_from = 1 if kind == 1 else 0
         self.q_to = self.n if kind == 2 else self.n + 1
@@ -167,74 +171,113 @@
         return coefs * (self.nh + self.n) + tiles_for(coefs * self.n, quarter)
 
 
-def gauge_kernel(chunk, groups, me_ref, state_ref, adjoint_ref, halo_ref, *rest):
-    out_refs, (held, p_held, q_held, sems) = rest[:groups], rest[groups:]
+def gauge_kernel(chunks, groups, has_halo, me_ref, state_ref, adjoint_ref, *rest):
+    if has_halo:
+        halo_ref, rest = rest[0], rest[1:]
+    out_refs, rest = rest[:groups], rest[groups:]
+    if not has_halo:
+        first_ref, first_sems = rest[0], rest[-1]
+        rest = rest[1:-1]
     coefs, parts, planes, rows, width = state_ref.shape
     quarter = rows // groups
-    n, nq = chunk.n, chunk.nq
-    own = held.shape[3]
     me = me_ref[0]
-    copies = []
-    for c in range(coefs):
-        for which, ref in enumerate((state_ref, adjoint_ref)):
-            copy = pltpu.make_async_copy(ref.at[c, :, pl.ds(chunk.lo, own)], held.at[which, c], sems.at[which, c])
-            copy.start()
-            copies.append((c, which, copy))
-    zero_rows = jnp.zeros((n, quarter, width), jnp.float32)
-    last_row = lax.broadcasted_iota(jnp.int32, (n + 1, rows, width), 1) == rows - 1
-    for c, which, copy in copies:
+    sources = (state_ref, adjoint_ref)
+    copies = {}
+    for which in range(2):
+        for at, chunk in enumerate(chunks):
+            held, sems = rest[5 * at], rest[5 * at + 4]
+            planes_here = pl.ds(chunk.lo, held.shape[3])
+            for c in range(coefs):
+                copy = pltpu.make_async_copy(sources[which].at[c, :, planes_here], held.at[which, c], sems.at[which, c])
+                copy.start()
+                copies[which, at, c] = copy
+    firsts = []
+    if not has_halo:
+        for which in range(2):
+            for c in range(coefs):
+                source = sources[which].at[c, pl.ds(1, 2), 0]
+                firsts.append(pltpu.make_async_copy(source, first_ref.at[which, c], first_sems.at[which, c]))
+                firsts[-1].start()
+    for which in range(2):
+        for at, chunk in enumerate(chunks):
+            held, phi_held, p_held, q_held, _ = rest[5 * at : 5 * at + 5]
+            n, nq = chunk.n, chunk.nq
+            own = held.shape[3]
+            last_row = lax.broadcasted_iota(jnp.int32, (n + 1, rows, width), 1) == rows - 1
+            zero_rows = jnp.zeros((n, quarter, width), jnp.float32)
+            for c in range(coefs):
+                copies[which, at, c].wait()
+            third = held[which, :, 2]
+            if own == n:
+                third = jnp.concatenate([third, halo_ref[which, :, 1][:, None]], axis=1)
+            phi_all = lane_sum(third.reshape(coefs * (n + 1) * rows, width), True)
+            phi_held[...] = phi_all.reshape(coefs, n + 1, rows, width)
+            for c in range(coefs):
+                second = held[which, c, 1]
+                if own == n:
+                    second = jnp.concatenate([second, halo_ref[which, c, 0][None]], axis=0)
+                phi = phi_held[c]
+                phi_up = jnp.where(last_row, 0.0, pltpu.roll(phi, rows - 1, 1))
+                p_held[which, c, :, 0:rows] = held[which, c, 0, 0:n] + phi[1:] - phi[:-1]
+                p_held[which, c, :, rows : rows + quarter] = zero_rows
+                q_held[which, c] = (second + (phi_up - phi))[chunk.q_from : chunk.q_to]
+            for c in range(coefs):
+                base = chunk.at + (which * coefs + c) * (n + nq)
+                for r in range(groups):
+                    start = pl.multiple_of(partner(me, r, groups) * quarter, quarter)
+                    out_refs[r][base : base + n] = p_held[which, c, :, pl.ds(start, quarter)]
+                    out_refs[r][base + n : base + n + nq] = q_held[which, c, :, pl.ds(start, quarter)]
+                    for i in range(n):
+                        spot = (which * coefs + c) * n + i
+                        edge = p_held[which, c, i, pl.ds(pl.multiple_of(start + quarter, quarter), quarter)]
+                        tile = chunk.at + 2 * coefs * (n + nq) + spot // quarter
+                        out_refs[r][tile, spot % quarter : spot % quarter + 1] = edge[0:1]
+    for copy in firsts:
         copy.wait()
-        third = held[which, c, 2]
-        second = held[which, c, 1]
-        if own == n:
-            third = jnp.concatenate([third, halo_ref[which, c, 1][None]], axis=0)
-            second = jnp.concatenate([second, halo_ref[which, c, 0][None]], axis=0)
-        phi = lane_sum(third.reshape((n + 1) * rows, width), True).reshape(n + 1, rows, width)
-        phi_up = jnp.where(last_row, 0.0, pltpu.roll(phi, rows - 1, 1))
-        p_held[which, c, :, 0:rows] = held[which, c, 0, 0:n] + phi[1:] - phi[:-1]
-        p_held[which, c, :, rows : rows + quarter] = zero_rows
-        q_held[which, c] = (second + (phi_up - phi))[chunk.q_from : chunk.q_to]
-        base = (which * coefs + c) * (n + nq)
-        for r in range(groups):
-            start = pl.multiple_of(partner(me, r, groups) * quarter, quarter)
-            out_refs[r][base : base + n] = p_held[which, c, :, pl.ds(start, quarter)]
-            out_refs[r][base + n : base + n + nq] = q_held[which, c, :, pl.ds(start, quarter)]
-            for i in range(n):
-                spot = (which * coefs + c) * n + i
-                edge = p_held[which, c, i, pl.ds(pl.multiple_of(start + quarter, quarter), quarter)]
-                tile = 2 * coefs * (n + nq) + spot // quarter
-                out_refs[r][tile, spot % quarter : spot % quarter + 1] = edge[0:1]
-
-
-def gauge(chunk, groups, me, state_hat, adjoint_hat, halo):
+
+
+def gauge(chunks, groups, me, state_hat, adjoint_hat, halo=None):
     coefs, parts, planes, rows, width = state_hat.shape
     quarter = rows // groups
-    own = min(chunk.n + 1, planes - chunk.lo)
-    shape = jax.ShapeDtypeStruct((chunk.sent(coefs, quarter), quarter, width), jnp.float32)
-    return pl.pallas_call(
-        functools.partial(gauge_kernel, chunk, groups),
-        in_specs=[SMEM, HBM, HBM, VMEM],
-        out_specs=[VMEM] * groups,
-        out_shape=[shape] * groups,
-        scratch_shapes=[
+    tiles = sum(chunk.sent(coefs, quarter) for chunk in chunks)
+    shapes = [jax.ShapeDtypeStruct((tiles, quarter, width), jnp.float32)] * groups
+    scratch = []
+    for chunk in chunks:
+        own = min(chunk.n + 1, planes - chunk.lo)
+        scratch += [
             pltpu.VMEM((2, coefs, parts, own, rows, width), jnp.float32),
+            pltpu.VMEM((coefs, chunk.n + 1, rows, width), jnp.float32),
             pltpu.VMEM((2, coefs, chunk.n, rows + quarter, width), jnp.float32),
             pltpu.VMEM((2, coefs, chunk.nq, rows, width), jnp.float32),
             pltpu.SemaphoreType.DMA((2, coefs)),
-        ],
-        compiler_params=pltpu.CompilerParams(vmem_limit_bytes=GAUGE_LIMIT),
-        cost_estimate=pl.CostEstimate(flops=2 * 10**9, bytes_accessed=4 * 10**6, transcendentals=0),
-        name="gauge%d" % chunk.kind,
-    )(me, state_hat, adjoint_hat, halo)
-
-
-def sample_kernel(chunk, groups, coefs, *refs):
+        ]
+    operands, specs = [me, state_hat, adjoint_hat], [SMEM, HBM, HBM]
+    if halo is None:
+        shapes.append(jax.ShapeDtypeStruct((2, coefs, 2, rows, width), jnp.float32))
+        scratch.append(pltpu.SemaphoreType.DMA((2, coefs)))
+    else:
+        operands.append(halo)
+        specs.append(VMEM)
+    return pl.pallas_call(
+        functools.partial(gauge_kernel, chunks, groups, halo is not None),
+        in_specs=specs,
+        out_specs=[VMEM] * len(shapes),
+        out_shape=shapes,
+        scratch_shapes=scratch,
+        compiler_params=pltpu.CompilerParams(vmem_limit_bytes=FIRST_LIMIT if halo is None else GAUGE_LIMIT),
+        cost_estimate=LITTLE,
+        name="gauge_middle" if halo is None else "gauge_ends",
+    )(*operands)
+
+
+def sample_kernel(chunk, groups, coefs, later, *refs):
     n, nq, kind = chunk.n, chunk.nq, chunk.kind
     me_ref, message_refs, refs = refs[0], refs[1 : 1 + groups], refs[1 + groups :]
     density_ref, region_ref, refs = refs[0], refs[1], refs[2:]
     edge_q_ref = edge_h_ref = None
     if kind:
         edge_q_ref, edge_h_ref, refs = refs[0], refs[1], refs[2:]
+    refs = refs[later:]
     out_refs, grad_ref, refs = refs[:groups], refs[groups], refs[groups + 1 :]
     if kind == 0:
         first_q_ref, last_q_ref, pending_ref, last_psi_ref = refs[:4]
@@ -257,11 +300,11 @@
         g = origin(me, r, groups)
         for which in range(2):
             for c in range(coefs):
-                base = (which * coefs + c) * (n + nq)
+                base = chunk.at + (which * coefs + c) * (n + nq)
                 p_ref[which, g, c] = message_refs[r][base : base + n]
                 q_ref[which, g, c, chunk.q_from : chunk.q_to] = message_refs[r][base + n : base + n + nq]
         for t in range(tiles_for(2 * coefs * n, quarter)):
-            edge_ref[g, t * quarter : (t + 1) * quarter] = message_refs[r][2 * coefs * (n + nq) + t]
+            edge_ref[g, t * quarter : (t + 1) * quarter] = message_refs[r][chunk.at + 2 * coefs * (n + nq) + t]
     for which in range(2):
         for g in range(groups):
             for c in range(coefs):
@@ -362,7 +405,7 @@
             out_refs[r][coefs * step + t] = tail_ref[g, t * quarter : (t + 1) * quarter]
 
 
-def sample_fields(chunk, me, messages, density, region, coefs, edges):
+def sample_fields(chunk, me, messages, density, region, coefs, edges, after):
     groups = len(messages)
     _, quarter, width = messages[0].shape
     n = chunk.n
@@ -372,10 +415,10 @@
     if chunk.kind == 0:
         shapes += [jax.ShapeDtypeStruct((2, groups, coefs, quarter, width), f32)] * 2
         shapes += [jax.ShapeDtypeStruct((groups, coefs, quarter, width), f32)] * 2
-    operands = [me, *messages, density, region, *edges]
+    operands = [me, *messages, density, region, *edges, *after]
     return pl.pallas_call(
-        functools.partial(sample_kernel, chunk, groups, coefs),
-        in_specs=[SMEM] + [VMEM] * (len(operands) - 1),
+        functools.partial(sample_kernel, chunk, groups, coefs, len(after)),
+        in_specs=[SMEM] + [VMEM] * (len(operands) - 1 - len(after)) + [ANY] * len(after),
         out_specs=[VMEM] * len(shapes),
         out_shape=shapes,
         scratch_shapes=[
@@ -390,14 +433,14 @@
             pltpu.VMEM((groups, tiles_for(coefs * n, quarter) * quarter, width), f32),
         ],
         compiler_params=pltpu.CompilerParams(vmem_limit_bytes=SAMPLE_LIMIT),
-        cost_estimate=pl.CostEstimate(flops=3 * 10**9, bytes_accessed=8 * 10**6, transcendentals=0),
+        cost_estimate=LITTLE,
         name="samples%d" % chunk.kind,
     )(*operands)
 
 
 def last_plane_kernel(chunk, coefs, me_ref, *refs):
-    groups = len(refs) - 2
-    message_refs, out_ref, row_ref = refs[:groups], refs[groups], refs[groups + 1]
+    groups = len(refs) - 3
+    message_refs, out_ref, row_ref = refs[:groups], refs[groups + 1], refs[groups + 2]
     quarter, width = message_refs[0].shape[1:]
     rows = quarter * groups
     step = chunk.nh + chunk.n
@@ -419,81 +462,114 @@
     target[here] = target[here] + message_ref[tile, spot % quarter : spot % quarter + 1]
 
 
-def last_plane(chunk, me, messages, coefs):
+def last_plane(chunk, me, messages, coefs, after):
     groups = len(messages)
     _, quarter, width = messages[0].shape
     rows = groups * quarter
     return pl.pallas_call(
         functools.partial(last_plane_kernel, chunk, coefs),
-        in_specs=[SMEM] + [VMEM] * groups,
+        in_specs=[SMEM] + [VMEM] * groups + [ANY],
         out_specs=VMEM,
         out_shape=jax.ShapeDtypeStruct((coefs, 2, rows, width), jnp.float32),
         scratch_shapes=[pltpu.VMEM((coefs, rows + quarter, width), jnp.float32)],
+        cost_estimate=LITTLE,
         name="last_plane",
-    )(me, *messages)
-
-
-def residual_kernel(chunks, groups, coefs, me_ref, *refs):
+    )(me, *messages, after)
+
+
+def residual_kernel(chunks, groups, coefs, lo, hi, me_ref, *refs):
     message_refs = [refs[k * groups : (k + 1) * groups] for k in range(len(chunks))]
-    halo_ref, objective_ref, out_ref, h0_ref, h1_ref = refs[len(chunks) * groups :]
+    refs = refs[len(chunks) * groups :]
+    if lo == 0:
+        halo_ref, objective_ref, _, out_ref, *refs = refs
+    else:
+        objective_ref, out_ref, *refs = refs
+    h0_ref, h1_ref, taken, given, take_sems, give_sems = refs
     parts, planes, rows, width = objective_ref.shape[1:]
     quarter = rows // groups
     me = me_ref[0]
     row = lax.broadcasted_iota(jnp.int32, (rows, width), 0)
     lane = lax.broadcasted_iota(jnp.int32, (rows, width), 1)
+    below = max(lo - 1, 0)
+    wanted = pl.ds(lo, hi - lo)
+    takes = [pltpu.make_async_copy(objective_ref.at[c, :, wanted], taken.at[c], take_sems.at[c]) for c in range(coefs)]
+    gives = [pltpu.make_async_copy(given.at[c], out_ref.at[c, :, wanted], give_sems.at[c]) for c in range(coefs)]
+    for copy in takes:
+        copy.start()
 
     def lower_lane(v):
         return jnp.where(lane == 0, 0.0, pltpu.roll(v, 1, 1))
 
-    def one_coef(c):
+    for c in range(coefs):
         for chunk, messages in zip(chunks, message_refs):
-            n = chunk.n
-            step = chunk.nh + n
+            step = chunk.nh + chunk.n
+            from_h0, to_h0 = max(chunk.lo + chunk.h_from, lo), min(chunk.lo + chunk.h_to, hi)
+            from_h1, to_h1 = max(chunk.lo, below), min(chunk.hi, hi)
             for r in range(groups):
-                g = origin(me, r, groups)
-                here = pl.ds(pl.multiple_of(g * quarter, quarter), quarter)
-                count = chunk.h_to - chunk.h_from
-                h0_ref[chunk.lo + chunk.h_from : chunk.lo + chunk.h_to, here] = messages[r][c * step : c * step + count]
-                h1_ref[chunk.lo : chunk.hi, here] = messages[r][c * step + chunk.nh : (c + 1) * step]
+                here = pl.ds(pl.multiple_of(origin(me, r, groups) * quarter, quarter), quarter)
+                if to_h0 > from_h0:
+                    at = c * step - chunk.lo - chunk.h_from
+                    h0_ref[c, from_h0 - below : to_h0 - below, here] = messages[r][at + from_h0 : at + to_h0]
+                if to_h1 > from_h1:
+                    at = c * step + chunk.nh - chunk.lo
+                    h1_ref[c, from_h1 - below : to_h1 - below, here] = messages[r][at + from_h1 : at + to_h1]
             for r in range(groups):
-                g = origin(me, r, groups)
-                for i in range(n):
-                    add_edge(h1_ref.at[chunk.lo + i], messages[r], chunk, coefs, c * n + i, g * quarter + quarter)
-        before = halo_ref[c, 0]
-        for i in range(planes):
-            h0 = h0_ref[i]
+                above = origin(me, r, groups) * quarter + quarter
+                for i in range(from_h1, to_h1):
+                    add_edge(h1_ref.at[c, i - below], messages[r], chunk, coefs, c * chunk.n + i - chunk.lo, above)
+    for c in range(coefs):
+        takes[c].wait()
+        before = halo_ref[c, 0] if lo == 0 else h1_ref[c, 0, 0:rows]
+        for i in range(lo, hi):
+            h0 = h0_ref[c, i - below]
             if i == 0:
                 h0 = h0 + halo_ref[c, 1]
-            h1 = h1_ref[i, 0:rows]
-            out_ref[0, 0, i] = objective_ref[0, 0, i] - (2.0 / NT) * (lower_lane(h1) - h1)
-            out_ref[0, 1, i] = objective_ref[0, 1, i] - (2.0 / NT) * (h0 - lower_lane(h0))
+            h1 = h1_ref[c, i - below, 0:rows]
+            given[c, 0, i - lo] = taken[c, 0, i - lo] - (2.0 / NT) * (lower_lane(h1) - h1)
+            given[c, 1, i - lo] = taken[c, 1, i - lo] - (2.0 / NT) * (h0 - lower_lane(h0))
             lower_row = jnp.where(row == 0, 0.0, pltpu.roll(h0, 1, 0))
-            out_ref[0, 2, i] = objective_ref[0, 2, i] - (2.0 / NT) * ((lower_row - h0) - (before - h1))
+            given[c, 2, i - lo] = taken[c, 2, i - lo] - (2.0 / NT) * ((lower_row - h0) - (before - h1))
             before = h1
-
-    for c in range(coefs):
-        pl.when(pl.program_id(0) == c)(functools.partial(one_coef, c))
-
-
-def residual(chunks, me, returned, halo, objective_hat):
+        gives[c].start()
+    for copy in gives:
+        copy.wait()
+
+
+def residual(chunks, me, returned, objective_hat, lo, hi, halo=None, begun=None):
     coefs, parts, planes, rows, width = objective_hat.shape
     groups = len(returned[0])
     quarter = rows // groups
-    block = pl.BlockSpec((1, parts, planes, rows, width), lambda c: (c, 0, 0, 0, 0))
-    operands = [m for messages in returned for m in messages]
+    held = hi - max(lo - 1, 0)
+    operands = [me] + [m for messages in returned for m in messages]
+    specs = [SMEM] + [VMEM] * (len(operands) - 1)
+    if lo == 0:
+        operands.append(halo)
+        specs.append(VMEM)
+    operands.append(objective_hat)
+    specs.append(HBM)
+    aliases = {}
+    if lo == 0:
+        aliases = {len(operands): 0}
+        operands.append(begun)
+        specs.append(HBM)
     return pl.pallas_call(
-        functools.partial(residual_kernel, chunks, groups, coefs),
-        grid=(coefs,),
-        in_specs=[SMEM] + [VMEM] * (len(operands) + 1) + [block],
-        out_specs=block,
+        functools.partial(residual_kernel, chunks, groups, coefs, lo, hi),
+        in_specs=specs,
+        out_specs=HBM,
         out_shape=jax.ShapeDtypeStruct(objective_hat.shape, jnp.float32),
+        input_output_aliases=aliases,
         scratch_shapes=[
-            pltpu.VMEM((planes, rows, width), jnp.float32),
-            pltpu.VMEM((planes, rows + quarter, width), jnp.float32),
+            pltpu.VMEM((coefs, held, rows, width), jnp.float32),
+            pltpu.VMEM((coefs, held, rows + quarter, width), jnp.float32),
+            pltpu.VMEM((coefs, parts, hi - lo, rows, width), jnp.float32),
+            pltpu.VMEM((coefs, parts, hi - lo, rows, width), jnp.float32),
+            pltpu.SemaphoreType.DMA((coefs,)),
+            pltpu.SemaphoreType.DMA((coefs,)),
         ],
         compiler_params=pltpu.CompilerParams(vmem_limit_bytes=RESIDUAL_LIMIT),
-        name="residual",
-    )(me, *operands, halo, objective_hat)
+        cost_estimate=LITTLE,
+        name="residual_first" if lo == 0 else "residual_rest",
+    )(*operands)
 
 
 def local(state_hat, adjoint_hat, objective_hat, density, region):
@@ -501,23 +577,23 @@
     coefs, parts, planes, rows, width = state_hat.shape
     me = lax.axis_index("sample").astype(jnp.int32).reshape(1)
     first = planes // 4
-    last = first + (planes - first) // 2
-    middle_chunk, last_chunk, first_chunk = Chunk(0, first, last), Chunk(1, last, planes), Chunk(2, 0, first)
-    upper = passed_along(jnp.stack([state_hat[:, 1:3, 0], adjoint_hat[:, 1:3, 0]], axis=0), "space", -1)
-    sent0 = gauge(middle_chunk, groups, me, state_hat, adjoint_hat, jnp.zeros((8, 128), jnp.float32))
+    last = planes - first
+    middle_chunk, last_chunk = Chunk(0, first, last), Chunk(1, last, planes)
+    first_chunk = Chunk(2, 0, first, last_chunk.sent(coefs, rows // groups))
+    *sent0, first_planes = gauge((middle_chunk,), groups, me, state_hat, adjoint_hat)
     cells0 = exchange(sent0)
-    sent1 = gauge(last_chunk, groups, me, state_hat, adjoint_hat, upper)
+    upper = passed_along(first_planes, "space", -1)
+    sent1 = gauge((last_chunk, first_chunk), groups, me, state_hat, adjoint_hat, upper)
     cells1 = exchange(sent1)
-    sent2 = gauge(first_chunk, groups, me, state_hat, adjoint_hat, upper)
-    cells2 = exchange(sent2)
-    *out0, grad0, first_q, last_q, pending, last_psi = sample_fields(middle_chunk, me, cells0, density, region, coefs, ())
+    *out0, grad0, first_q, last_q, pending, last_psi = sample_fields(middle_chunk, me, cells0, density, region, coefs, (), sent1[:1])
     back0 = exchange(out0)
-    *out1, grad1 = sample_fields(last_chunk, me, cells1, density, region, coefs, (last_q, last_psi))
+    *out1, grad1 = sample_fields(last_chunk, me, cells1, density, region, coefs, (last_q, last_psi), ())
     back1 = exchange(out1)
-    *out2, grad2 = sample_fields(first_chunk, me, cells2, density, region, coefs, (first_q, pending))
+    *out2, grad2 = sample_fields(first_chunk, me, cells1, density, region, coefs, (first_q, pending), out1[:1])
     back2 = exchange(out2)
-    lower = passed_along(last_plane(last_chunk, me, back1, coefs), "space", 1)
-    adjoint_residual = residual((middle_chunk, last_chunk, first_chunk), me, (back0, back1, back2), lower, objective_hat)
+    lower = passed_along(last_plane(last_chunk, me, back1, coefs, out2[0]), "space", 1)
+    begun = residual((middle_chunk, last_chunk), me, (back0, back1), objective_hat, first + 1, planes)
+    adjoint_residual = residual((middle_chunk, first_chunk), me, (back0, back2), objective_hat, 0, first + 1, lower, begun)
     return adjoint_residual, jnp.concatenate([grad2, grad0, grad1], axis=0)
 
 

time: 80.8 us -> 72.7 us (0.90)
  waiting for transfers between devices: 35.6 us -> 26.9 us
  local copies, waits for them, and re-layouts: 4.82 us -> 6.44 us
  starting transfers between devices: 19.6 us -> 18.4 us
    ppermute x18 -> x15, waiting for transfers between devices: 33.4 us -> 18 us  [exchange(): taken[r] = lax.ppermute(messages[r], 'sample', pairs)]
    ppermute x2, waiting for transfers between devices: 2.17 us -> 8.91 us  [passed_along(): return lax.ppermute(array, axis, pairs)]
    unnamed x30 -> x36, local copies, waits for them, and re-layouts: 3.79 us -> 6.44 us
    another operation x1 -> x0, local copies, waits for them, and re-layouts: 1.03 us -> none  [local(): jnp.stack([state_hat[:, 1:3, 0], adjoint_hat[:, 1:3, 0]], axis=0)]
    ppermute x18 -> x15, starting transfers between devices: 13.7 us -> 12.8 us  [exchange(): taken[r] = lax.ppermute(messages[r], 'sample', pairs)]
  transfers between devices with their start and end apart: 20 -> 17, of which waited for: 9 -> 6; matrix products, arithmetic and copies ran while one was open for 1% -> 1% of each run, Pallas kernels for 17% -> 16%
where the time goes in v3:
time: 72.7 us; the launch traced here: 71.7 us
  waiting for transfers between devices  26.9 us (37%)
  Pallas kernels  18.5 us (25%)
  starting transfers between devices  18.4 us (25%)
  local copies, waits for them, and re-layouts  6.44 us (9%)
  between operations  0.84 us (1%)
    ppermute x15, waiting for transfers between devices, exchange(): taken[r] = lax.ppermute(messages[r], 'sample', pairs)  18 us
    ppermute x15, starting transfers between devices, exchange(): taken[r] = lax.ppermute(messages[r], 'sample', pairs)  12.8 us
    ppermute x2, waiting for transfers between devices, passed_along(): return lax.ppermute(array, axis, pairs)  8.91 us
    pallas_call x3, Pallas kernels, sample_fields(): pl.pallas_call(functools.partial(sample_kernel, chunk, groups, coefs, len...  6.51 us
    unnamed x36, local copies, waits for them, and re-layouts  6.44 us
    pallas_call x2, Pallas kernels, gauge(): pl.pallas_call(functools.partial(gauge_kernel, chunks, groups, halo is no...  6.43 us
    ppermute x2, starting transfers between devices, passed_along(): return lax.ppermute(array, axis, pairs)  5.58 us
    pallas_call x2, Pallas kernels, residual(): pl.pallas_call(functools.partial(residual_kernel, chunks, groups, coefs,...  3.8 us
  transfers between devices with their start and end apart: 17, of which 6 were waited for; matrix products, arithmetic and copies ran while one was open for 1% of the time, Pallas kernels for 16%

profile of v3, /device:TPU:0, one launch (start us, length us, event | category | flops | bytes accessed | tf_op | source)
XLA Modules:
  0.0 71.7 jit_solution(13051144770380608383)
XLA Ops:
  0.6 3.9 %gauge_middle.1 = (f32[95,8,128]{2,1,0:T(8,128)}, f32[95,8,128]{2,1,0:T(8,128)}, f32[95,8,128]{2,1,0:T(8,128)}, f32[95,8,128]{2,1,0:T(8,128)}, f32[2,5,2,32,128]{4,3,2,1,0:T(8,128)}) custom-call(s32[1]{0:T(128)} %bitcast.me_ref.refs_0_, f32[5,3,8,32,128]{4,3,2,1,0:T(8,128)} %state_ref.3, f32[5,3,8,32,128]{4,3,2,1,0:T(8,128)} %adjoint_ref.3), custom_call_target="tpu_custom_call" | custom-call | flops 1000 | bytes 1000 | tf_op jit(solution)/shard_map/gauge_middle/pallas_call | solution.py:261
  4.5 0.5 collective-permute-start
  5.1 1.3 %collective-permute-start.3 = (f32[2,5,2,32,128]{4,3,2,1,0:T(8,128)}, f32[2,5,2,32,128]{4,3,2,1,0:T(8,128)S(1)}, u32[]{:S(2)}, u32[]{:S(2)}) collective-permute-start(f32[2,5,2,32,128]{4,3,2,1,0:T(8,128)} %get-tuple-element.34), channel_id=1, source_target_pairs={{4,0},{8,4},{12,8},{16,12},{20,16},{24,20},{28,24},{5,1},{9,5},{13... | collective-permute-start | bytes 983048 | tf_op jit(solution)/shard_map/ppermute | solution.py:24
  6.3 2.6 %collective-permute-start.1 = (f32[95,8,128]{2,1,0:T(8,128)}, f32[95,8,128]{2,1,0:T(8,128)S(1)}, u32[]{:S(2)}, u32[]{:S(2)}) collective-permute-start(f32[95,8,128]{2,1,0:T(8,128)} %get-tuple-element.32), channel_id=1, source_target_pairs={{0,2},{1,3},{2,0},{3,1},{4,6},{5,7},{6,4},{7,5},{8,10},{9,11},{10,... | collective-permute-start | bytes 1167368 | tf_op jit(solution)/shard_map/ppermute | solution.py:141
  8.9 0.2 collective-permute-start.2
  9.1 8.9 %collective-permute-done.3.rest_0_ = f32[2,5,2,32,128]{4,3,2,1,0:T(8,128)S(1)} collective-permute-done((f32[2,5,2,32,128]{4,3,2,1,0:T(8,128)}, f32[2,5,2,32,128]{4,3,2,1,0:T(8,128)S(1)}, u32[]{:S(2)}, u32[]{:S(2)}) %collective-permute-start.3) | collective-permute-done | bytes 327712 | tf_op jit(solution)/shard_map/ppermute | solution.py:24
  18.0 1.5 %copy-done.2 = f32[5,3,8,32,128]{4,3,2,1,0:T(8,128)S(1)} copy-done((f32[5,3,8,32,128]{4,3,2,1,0:T(8,128)S(1)}, f32[5,3,8,32,128]{4,3,2,1,0:T(8,128)}, u32[]{:S(2)}) %copy-start.2) | copy-done | bytes 1966104
  19.6 2.5 %gauge_ends.1 = (f32[86,8,128]{2,1,0:T(8,128)S(1)}, f32[86,8,128]{2,1,0:T(8,128)S(1)}, f32[86,8,128]{2,1,0:T(8,128)S(1)}, f32[86,8,128]{2,1,0:T(8,128)S(1)}) custom-call(s32[1]{0:T(128)} %bitcast.me_ref.refs_0_, f32[5,3,8,32,128]{4,3,2,1,0:T(8,128)S(1)} %copy-done.1, f32[5,3,8,32,128]{4,3,2,1,0:T(8,128)S(1)} %copy-done.2, ...), custom_call_target="tpu_custom_call" | custom-call | flops 1000 | bytes 1000 | tf_op jit(solution)/shard_map/gauge_ends/pallas_call | solution.py:261
  22.1 0.1 collective-permute-start.7
  22.2 1.8 %collective-permute-start.8 = (f32[86,8,128]{2,1,0:T(8,128)S(1)}, f32[86,8,128]{2,1,0:T(8,128)S(1)}, u32[]{:S(2)}, u32[]{:S(2)}) collective-permute-start(f32[86,8,128]{2,1,0:T(8,128)S(1)} %get-tuple-element.41), channel_id=1, source_target_pairs={{0,2},{1,3},{2,0},{3,1},{4,6},{5,7},{6,4},{7,5},{8,10},{9,11},{10,... | collective-permute-start | bytes 1056776 | tf_op jit(solution)/shard_map/ppermute | solution.py:141
  24.0 0.0 collective-permute-done.refs_2_
  24.0 0.1 collective-permute-start.9
  24.1 0.0 collective-permute-done.1.refs_3_
  24.1 2.9 %collective-permute-done.2.refs_4_ = f32[95,8,128]{2,1,0:T(8,128)S(1)} collective-permute-done((f32[95,8,128]{2,1,0:T(8,128)}, f32[95,8,128]{2,1,0:T(8,128)S(1)}, u32[]{:S(2)}, u32[]{:S(2)}) %collective-permute-start.2) | collective-permute-done | bytes 389152 | tf_op jit(solution)/shard_map/ppermute | solution.py:141
  27.0 3.3 %samples0.1 = (f32[38,8,128]{2,1,0:T(8,128)S(1)}, f32[38,8,128]{2,1,0:T(8,128)S(1)}, f32[38,8,128]{2,1,0:T(8,128)S(1)}, f32[38,8,128]{2,1,0:T(8,128)S(1)}, f32[4...) custom-call(s32[1]{0:T(128)} %bitcast.me_ref.refs_0_, ...), custom_call_target="tpu_custom_call" | custom-call | flops 1000 | bytes 1000 | tf_op jit(solution)/shard_map/samples0/pallas_call | solution.py:419
  30.2 0.0 collective-permute-done.7.refs_2_
  30.3 4.7 %collective-permute-done.8.refs_3_ = f32[86,8,128]{2,1,0:T(8,128)S(1)} collective-permute-done((f32[86,8,128]{2,1,0:T(8,128)S(1)}, f32[86,8,128]{2,1,0:T(8,128)S(1)}, u32[]{:S(2)}, u32[]{:S(2)}) %collective-permute-start.8) | collective-permute-done | bytes 352288 | tf_op jit(solution)/shard_map/ppermute | solution.py:141
  34.9 7.1 %collective-permute-done.9.refs_4_ = f32[86,8,128]{2,1,0:T(8,128)S(1)} collective-permute-done((f32[86,8,128]{2,1,0:T(8,128)S(1)}, f32[86,8,128]{2,1,0:T(8,128)S(1)}, u32[]{:S(2)}, u32[]{:S(2)}) %collective-permute-start.9) | collective-permute-done | bytes 352288 | tf_op jit(solution)/shard_map/ppermute | solution.py:141
  42.1 1.6 %samples1.1 = (f32[27,8,128]{2,1,0:T(8,128)S(1)}, f32[27,8,128]{2,1,0:T(8,128)S(1)}, f32[27,8,128]{2,1,0:T(8,128)S(1)}, f32[27,8,128]{2,1,0:T(8,128)S(1)}, f32[2,8,128]{2,1,0:T(8,128)S(1)}) custom-call(s32[1]{0:T(128)} %bitcast.me_ref.refs_0_, f32[86,8,128]{2,1,0:T(8,128)S(1)} %get-tuple-element.35.refs_7_.refs_1_, ...), custom_call_target="tpu_custom_call" | custom-call | flops 1000 | bytes 1000 | tf_op jit(solution)/shard_map/samples1/pallas_call | solution.py:419
  43.7 0.0 copy-start.5
  43.7 0.2 collective-permute-start.13
  43.9 1.7 %collective-permute-start.14 = (f32[27,8,128]{2,1,0:T(8,128)S(1)}, f32[27,8,128]{2,1,0:T(8,128)S(1)}, u32[]{:S(2)}, u32[]{:S(2)}) collective-permute-start(f32[27,8,128]{2,1,0:T(8,128)S(1)} %get-tuple-element.53), channel_id=1, source_target_pairs={{0,2},{1,3},{2,0},{3,1},{4,6},{5,7},{6,4},{7,5},{8,10},{9,11},{10,... | collective-permute-start | bytes 331784 | tf_op jit(solution)/shard_map/ppermute | solution.py:141
  45.6 0.1 collective-permute-start.15
  45.7 0.4 collective-permute-start.4
  46.0 1.7 %collective-permute-start.5 = (f32[38,8,128]{2,1,0:T(8,128)S(1)}, f32[38,8,128]{2,1,0:T(8,128)S(1)}, u32[]{:S(2)}, u32[]{:S(2)}) collective-permute-start(f32[38,8,128]{2,1,0:T(8,128)S(1)} %get-tuple-element.38), channel_id=1, source_target_pairs={{0,2},{1,3},{2,0},{3,1},{4,6},{5,7},{6,4},{7,5},{8,10},{9,11},{10,... | collective-permute-start | bytes 466952 | tf_op jit(solution)/shard_map/ppermute | solution.py:141
  47.7 1.6 %samples2.1 = (f32[27,8,128]{2,1,0:T(8,128)S(1)}, f32[27,8,128]{2,1,0:T(8,128)S(1)}, f32[27,8,128]{2,1,0:T(8,128)S(1)}, f32[27,8,128]{2,1,0:T(8,128)S(1)}, f32[2,8,128]{2,1,0:T(8,128)S(1)}) custom-call(s32[1]{0:T(128)} %bitcast.me_ref.refs_0_, f32[86,8,128]{2,1,0:T(8,128)S(1)} %get-tuple-element.35.refs_7_.refs_1_, ...), custom_call_target="tpu_custom_call" | custom-call | flops 1000 | bytes 1000 | tf_op jit(solution)/shard_map/samples2/pallas_call | solution.py:419
  49.3 0.6 copy-done.7
  50.0 0.0 collective-permute-done.13.refs_1_.refs_5_
  50.0 0.0 collective-permute-done.14.refs_2_.refs_6_
  50.0 1.3 %collective-permute-done.15.refs_3_.refs_7_ = f32[27,8,128]{2,1,0:T(8,128)S(1)} collective-permute-done((f32[27,8,128]{2,1,0:T(8,128)S(1)}, f32[27,8,128]{2,1,0:T(8,128)S(1)}, u32[]{:S(2)}, u32[]{:S(2)}) %collective-permute-start.15) | collective-permute-done | bytes 110624 | tf_op jit(solution)/shard_map/ppermute | solution.py:141
  51.4 0.6 copy-done.13
  52.0 1.8 %last_plane.1 = f32[5,2,32,128]{3,2,1,0:T(8,128)} custom-call(s32[1]{0:T(128)} %bitcast.me_ref.refs_0_, f32[27,8,128]{2,1,0:T(8,128)} %copy-done.5, f32[27,8,128]{2,1,0:T(8,128)} %copy-done.9, f32[27,8,128]{2,1,0:T(8,128)} %copy-done.11, f32[27,8,128]{2,1,0:T(8,128)} %copy-done.13, f32[27,8,128]{2,1,0:T(8,128)} %copy-done.7), custom_call_target="tpu_custom_call" | custom-call | flops 1000 | bytes 1000 | tf_op jit(solution)/shard_map/last_plane/pallas_call | solution.py:469
  53.8 4.3 %collective-permute-start.16 = (f32[5,2,32,128]{3,2,1,0:T(8,128)}, f32[5,2,32,128]{3,2,1,0:T(8,128)S(1)}, u32[]{:S(2)}, u32[]{:S(2)}) collective-permute-start(f32[5,2,32,128]{3,2,1,0:T(8,128)} %last_plane.1), channel_id=1, source_target_pairs={{0,4},{4,8},{8,12},{12,16},{16,20},{20,24},{24,28},{1,5},{5,9},{9,... | collective-permute-start | bytes 491528 | tf_op jit(solution)/shard_map/ppermute | solution.py:24
  58.1 1.7 %collective-permute-start.6 = (f32[38,8,128]{2,1,0:T(8,128)S(1)}, f32[38,8,128]{2,1,0:T(8,128)S(1)}, u32[]{:S(2)}, u32[]{:S(2)}) collective-permute-start(f32[38,8,128]{2,1,0:T(8,128)S(1)} %get-tuple-element.39), channel_id=1, source_target_pairs={{0,3},{1,2},{2,1},{3,0},{4,7},{5,6},{6,5},{7,4},{8,11},{9,10},{10,... | collective-permute-start | bytes 466952 | tf_op jit(solution)/shard_map/ppermute | solution.py:141
  59.8 0.0 collective-permute-start.10
  59.8 0.0 collective-permute-done.4.refs_1_
  59.8 0.5 collective-permute-start.11
  60.3 1.3 %collective-permute-start.12 = (f32[27,8,128]{2,1,0:T(8,128)S(1)}, f32[27,8,128]{2,1,0:T(8,128)S(1)}, u32[]{:S(2)}, u32[]{:S(2)}) collective-permute-start(f32[27,8,128]{2,1,0:T(8,128)S(1)} %get-tuple-element.51), channel_id=1, source_target_pairs={{0,3},{1,2},{2,1},{3,0},{4,7},{5,6},{6,5},{7,4},{8,11},{9,10},{10,... | collective-permute-start | bytes 331784 | tf_op jit(solution)/shard_map/ppermute | solution.py:141
  61.6 0.6 pad_maximum_fusion
  62.3 2.0 %collective-permute-done.6.refs_3_ = f32[38,8,128]{2,1,0:T(8,128)S(1)} collective-permute-done((f32[38,8,128]{2,1,0:T(8,128)S(1)}, f32[38,8,128]{2,1,0:T(8,128)S(1)}, u32[]{:S(2)}, u32[]{:S(2)}) %collective-permute-start.6) | collective-permute-done | bytes 155680 | tf_op jit(solution)/shard_map/ppermute | solution.py:141
  64.2 0.9 %copy-done.6 = f32[27,8,128]{2,1,0:T(8,128)S(1)} copy-done((f32[27,8,128]{2,1,0:T(8,128)S(1)}, f32[27,8,128]{2,1,0:T(8,128)}, u32[]{:S(2)}) %copy-start.6) | copy-done | bytes 110616
  65.1 0.9 %copy-done.10 = f32[27,8,128]{2,1,0:T(8,128)S(1)} copy-done((f32[27,8,128]{2,1,0:T(8,128)S(1)}, f32[27,8,128]{2,1,0:T(8,128)}, u32[]{:S(2)}) %copy-start.10) | copy-done | bytes 110616
  66.0 0.9 %copy-done.12 = f32[27,8,128]{2,1,0:T(8,128)S(1)} copy-done((f32[27,8,128]{2,1,0:T(8,128)S(1)}, f32[27,8,128]{2,1,0:T(8,128)}, u32[]{:S(2)}) %copy-start.12) | copy-done | bytes 110616
  66.9 0.9 %copy-done.14 = f32[27,8,128]{2,1,0:T(8,128)S(1)} copy-done((f32[27,8,128]{2,1,0:T(8,128)S(1)}, f32[27,8,128]{2,1,0:T(8,128)}, u32[]{:S(2)}) %copy-start.14) | copy-done | bytes 110616
  67.8 2.1 %residual_rest.1.refs_10_ = f32[5,3,8,32,128]{4,3,2,1,0:T(8,128)} custom-call(s32[1]{0:T(128)} %bitcast.me_ref.refs_0_, f32[38,8,128]{2,1,0:T(8,128)S(1)} %get-tuple-element.36.refs_0_, f32[38,8,128]{2,1,0:T(8,128)S(1)} %collective-permute-done.4.refs_1_, f32[38,8,128]{2,1,0:T(8,128)S(1)} %collective-permute-done.5.refs_2_, ...), custom_call_target="tpu_custom_call" | custom-call | flops 1000 | bytes 1000 | tf_op jit(solution)/shard_map/residual_rest/pallas_call | solution.py:555
  69.9 0.0 collective-permute-done.11.refs_6_
  69.9 0.0 collective-permute-done.12.refs_7_
  70.0 1.7 %residual_first.1 = f32[5,3,8,32,128]{4,3,2,1,0:T(8,128)} custom-call(s32[1]{0:T(128)} %bitcast.me_ref.refs_0_, f32[38,8,128]{2,1,0:T(8,128)S(1)} %get-tuple-element.36.refs_0_, f32[38,8,128]{2,1,0:T(8,128)S(1)} %collective-permute-done.4.refs_1_, f32[38,8,128]{2,1,0:T(8,128)S(1)} %collective-permute-done.5.refs_2_, ...), custom_call_target="tpu_custom_call", output_to_operand_aliasing={{}: (11, {})} | custom-call | flops 1000 | bytes 1000 | tf_op jit(solution)/shard_map/residual_first/pallas_call | solution.py:555
  (31 shorter events, 0.1 us)
Async XLA Ops:
  0.6 17.4 %copy-start.1 = (f32[5,3,8,32,128]{4,3,2,1,0:T(8,128)S(1)}, f32[5,3,8,32,128]{4,3,2,1,0:T(8,128)}, u32[]{:S(2)}) copy-start(f32[5,3,8,32,128]{4,3,2,1,0:T(8,128)} %state_ref.3) | copy-start | bytes 5898244
  4.5 19.5 %collective-permute-start = (f32[95,8,128]{2,1,0:T(8,128)}, f32[95,8,128]{2,1,0:T(8,128)S(1)}, u32[]{:S(2)}, u32[]{:S(2)}) collective-permute-start(f32[95,8,128]{2,1,0:T(8,128)} %get-tuple-element.31), channel_id=1, source_target_pairs={{0,1},{1,0},{2,3},{3,2},{4,5},{5,4},{6,7},{7,6},{8,9},{9,8},{10,11... | collective-permute-start | bytes 1167368 | tf_op jit(solution)/shard_map/ppermute | solution.py:141
  5.1 13.0 %collective-permute-start.3 = (f32[2,5,2,32,128]{4,3,2,1,0:T(8,128)}, f32[2,5,2,32,128]{4,3,2,1,0:T(8,128)S(1)}, u32[]{:S(2)}, u32[]{:S(2)}) collective-permute-start(f32[2,5,2,32,128]{4,3,2,1,0:T(8,128)} %get-tuple-element.34), channel_id=1, source_target_pairs={{4,0},{8,4},{12,8},{16,12},{20,16},{24,20},{28,24},{5,1},{9,5},{13... | collective-permute-start | bytes 983048 | tf_op jit(solution)/shard_map/ppermute | solution.py:24
  6.3 17.8 %collective-permute-start.1 = (f32[95,8,128]{2,1,0:T(8,128)}, f32[95,8,128]{2,1,0:T(8,128)S(1)}, u32[]{:S(2)}, u32[]{:S(2)}) collective-permute-start(f32[95,8,128]{2,1,0:T(8,128)} %get-tuple-element.32), channel_id=1, source_target_pairs={{0,2},{1,3},{2,0},{3,1},{4,6},{5,7},{6,4},{7,5},{8,10},{9,11},{10,... | collective-permute-start | bytes 1167368 | tf_op jit(solution)/shard_map/ppermute | solution.py:141
  8.9 18.0 %collective-permute-start.2 = (f32[95,8,128]{2,1,0:T(8,128)}, f32[95,8,128]{2,1,0:T(8,128)S(1)}, u32[]{:S(2)}, u32[]{:S(2)}) collective-permute-start(f32[95,8,128]{2,1,0:T(8,128)} %get-tuple-element.33), channel_id=1, source_target_pairs={{0,3},{1,2},{2,1},{3,0},{4,7},{5,6},{6,5},{7,4},{8,11},{9,10},{10,... | collective-permute-start | bytes 1167368 | tf_op jit(solution)/shard_map/ppermute | solution.py:141
  18.0 1.5 %copy-start.2 = (f32[5,3,8,32,128]{4,3,2,1,0:T(8,128)S(1)}, f32[5,3,8,32,128]{4,3,2,1,0:T(8,128)}, u32[]{:S(2)}) copy-start(f32[5,3,8,32,128]{4,3,2,1,0:T(8,128)} %adjoint_ref.3) | copy-start | bytes 5898244
  19.6 7.4 %copy-start.3 = (f32[8,32,128]{2,1,0:T(8,128)S(1)}, f32[8,32,128]{2,1,0:T(8,128)}, u32[]{:S(2)}) copy-start(f32[8,32,128]{2,1,0:T(8,128)} %refs_5_.5) | copy-start | bytes 393220
  19.6 7.4 %copy-start.4 = (s32[8,32,128]{2,1,0:T(8,128)S(1)}, s32[8,32,128]{2,1,0:T(8,128)}, u32[]{:S(2)}) copy-start(s32[8,32,128]{2,1,0:T(8,128)} %refs_6_.5) | copy-start | bytes 393220
  19.6 7.4 %copy-start.15 = (f32[95,8,128]{2,1,0:T(8,128)S(1)}, f32[95,8,128]{2,1,0:T(8,128)}, u32[]{:S(2)}) copy-start(f32[95,8,128]{2,1,0:T(8,128)} %get-tuple-element.30.refs_1_) | copy-start | bytes 1167364
  22.1 8.1 %collective-permute-start.7 = (f32[86,8,128]{2,1,0:T(8,128)S(1)}, f32[86,8,128]{2,1,0:T(8,128)S(1)}, u32[]{:S(2)}, u32[]{:S(2)}) collective-permute-start(f32[86,8,128]{2,1,0:T(8,128)S(1)} %get-tuple-element.40), channel_id=1, source_target_pairs={{0,1},{1,0},{2,3},{3,2},{4,5},{5,4},{6,7},{7,6},{8,9},{9,8},{10,11... | collective-permute-start | bytes 1056776 | tf_op jit(solution)/shard_map/ppermute | solution.py:141
  22.2 12.7 %collective-permute-start.8 = (f32[86,8,128]{2,1,0:T(8,128)S(1)}, f32[86,8,128]{2,1,0:T(8,128)S(1)}, u32[]{:S(2)}, u32[]{:S(2)}) collective-permute-start(f32[86,8,128]{2,1,0:T(8,128)S(1)} %get-tuple-element.41), channel_id=1, source_target_pairs={{0,2},{1,3},{2,0},{3,1},{4,6},{5,7},{6,4},{7,5},{8,10},{9,11},{10,... | collective-permute-start | bytes 1056776 | tf_op jit(solution)/shard_map/ppermute | solution.py:141
  24.0 18.0 %collective-permute-start.9 = (f32[86,8,128]{2,1,0:T(8,128)S(1)}, f32[86,8,128]{2,1,0:T(8,128)S(1)}, u32[]{:S(2)}, u32[]{:S(2)}) collective-permute-start(f32[86,8,128]{2,1,0:T(8,128)S(1)} %get-tuple-element.42), channel_id=1, source_target_pairs={{0,3},{1,2},{2,1},{3,0},{4,7},{5,6},{6,5},{7,4},{8,11},{9,10},{10,... | collective-permute-start | bytes 1056776 | tf_op jit(solution)/shard_map/ppermute | solution.py:141
  42.1 22.2 %copy-start = (f32[5,3,8,32,128]{4,3,2,1,0:T(8,128)S(1)}, f32[5,3,8,32,128]{4,3,2,1,0:T(8,128)}, u32[]{:S(2)}) copy-start(f32[5,3,8,32,128]{4,3,2,1,0:T(8,128)} %refs_9_.1) | copy-start | bytes 5898244
  43.7 7.7 %copy-start.5 = (f32[27,8,128]{2,1,0:T(8,128)}, f32[27,8,128]{2,1,0:T(8,128)S(1)}, u32[]{:S(2)}) copy-start(f32[27,8,128]{2,1,0:T(8,128)S(1)} %get-tuple-element.47.refs_9_.refs_0_.refs_4_) | copy-start | bytes 331780
  43.7 6.3 %collective-permute-start.13 = (f32[27,8,128]{2,1,0:T(8,128)S(1)}, f32[27,8,128]{2,1,0:T(8,128)S(1)}, u32[]{:S(2)}, u32[]{:S(2)}) collective-permute-start(f32[27,8,128]{2,1,0:T(8,128)S(1)} %get-tuple-element.52), channel_id=1, source_target_pairs={{0,1},{1,0},{2,3},{3,2},{4,5},{5,4},{6,7},{7,6},{8,9},{9,8},{10,11... | collective-permute-start | bytes 331784 | tf_op jit(solution)/shard_map/ppermute | solution.py:141
  43.9 6.1 %collective-permute-start.14 = (f32[27,8,128]{2,1,0:T(8,128)S(1)}, f32[27,8,128]{2,1,0:T(8,128)S(1)}, u32[]{:S(2)}, u32[]{:S(2)}) collective-permute-start(f32[27,8,128]{2,1,0:T(8,128)S(1)} %get-tuple-element.53), channel_id=1, source_target_pairs={{0,2},{1,3},{2,0},{3,1},{4,6},{5,7},{6,4},{7,5},{8,10},{9,11},{10,... | collective-permute-start | bytes 331784 | tf_op jit(solution)/shard_map/ppermute | solution.py:141
  45.6 5.8 %collective-permute-start.15 = (f32[27,8,128]{2,1,0:T(8,128)S(1)}, f32[27,8,128]{2,1,0:T(8,128)S(1)}, u32[]{:S(2)}, u32[]{:S(2)}) collective-permute-start(f32[27,8,128]{2,1,0:T(8,128)S(1)} %get-tuple-element.54), channel_id=1, source_target_pairs={{0,3},{1,2},{2,1},{3,0},{4,7},{5,6},{6,5},{7,4},{8,11},{9,10},{10,... | collective-permute-start | bytes 331784 | tf_op jit(solution)/shard_map/ppermute | solution.py:141
  45.7 14.1 %collective-permute-start.4 = (f32[38,8,128]{2,1,0:T(8,128)S(1)}, f32[38,8,128]{2,1,0:T(8,128)S(1)}, u32[]{:S(2)}, u32[]{:S(2)}) collective-permute-start(f32[38,8,128]{2,1,0:T(8,128)S(1)} %get-tuple-element.37), channel_id=1, source_target_pairs={{0,1},{1,0},{2,3},{3,2},{4,5},{5,4},{6,7},{7,6},{8,9},{9,8},{10,11... | collective-permute-start | bytes 466952 | tf_op jit(solution)/shard_map/ppermute | solution.py:141
  46.0 14.3 %collective-permute-start.5 = (f32[38,8,128]{2,1,0:T(8,128)S(1)}, f32[38,8,128]{2,1,0:T(8,128)S(1)}, u32[]{:S(2)}, u32[]{:S(2)}) collective-permute-start(f32[38,8,128]{2,1,0:T(8,128)S(1)} %get-tuple-element.38), channel_id=1, source_target_pairs={{0,2},{1,3},{2,0},{3,1},{4,6},{5,7},{6,4},{7,5},{8,10},{9,11},{10,... | collective-permute-start | bytes 466952 | tf_op jit(solution)/shard_map/ppermute | solution.py:141
  49.3 0.6 copy-start.7
  50.0 1.4 %copy-start.16 = (f32[27,8,128]{2,1,0:T(8,128)}, f32[27,8,128]{2,1,0:T(8,128)S(1)}, u32[]{:S(2)}) copy-start(f32[27,8,128]{2,1,0:T(8,128)S(1)} %get-tuple-element.50) | copy-start | bytes 331780
  50.0 1.4 %copy-start.17 = (f32[27,8,128]{2,1,0:T(8,128)}, f32[27,8,128]{2,1,0:T(8,128)S(1)}, u32[]{:S(2)}) copy-start(f32[27,8,128]{2,1,0:T(8,128)S(1)} %get-tuple-element.49) | copy-start | bytes 331780
  50.0 1.4 %copy-start.9 = (f32[27,8,128]{2,1,0:T(8,128)}, f32[27,8,128]{2,1,0:T(8,128)S(1)}, u32[]{:S(2)}) copy-start(f32[27,8,128]{2,1,0:T(8,128)S(1)} %collective-permute-done.13.refs_1_.refs_5_) | copy-start | bytes 331780
  50.0 1.4 %copy-start.11 = (f32[27,8,128]{2,1,0:T(8,128)}, f32[27,8,128]{2,1,0:T(8,128)S(1)}, u32[]{:S(2)}) copy-start(f32[27,8,128]{2,1,0:T(8,128)S(1)} %collective-permute-done.14.refs_2_.refs_6_) | copy-start | bytes 331780
  51.3 0.6 copy-start.13
  53.8 16.2 %collective-permute-start.16 = (f32[5,2,32,128]{3,2,1,0:T(8,128)}, f32[5,2,32,128]{3,2,1,0:T(8,128)S(1)}, u32[]{:S(2)}, u32[]{:S(2)}) collective-permute-start(f32[5,2,32,128]{3,2,1,0:T(8,128)} %last_plane.1), channel_id=1, source_target_pairs={{0,4},{4,8},{8,12},{12,16},{16,20},{20,24},{24,28},{1,5},{5,9},{9,... | collective-permute-start | bytes 491528 | tf_op jit(solution)/shard_map/ppermute | solution.py:24
  58.1 6.1 %collective-permute-start.6 = (f32[38,8,128]{2,1,0:T(8,128)S(1)}, f32[38,8,128]{2,1,0:T(8,128)S(1)}, u32[]{:S(2)}, u32[]{:S(2)}) collective-permute-start(f32[38,8,128]{2,1,0:T(8,128)S(1)} %get-tuple-element.39), channel_id=1, source_target_pairs={{0,3},{1,2},{2,1},{3,0},{4,7},{5,6},{6,5},{7,4},{8,11},{9,10},{10,... | collective-permute-start | bytes 466952 | tf_op jit(solution)/shard_map/ppermute | solution.py:141
  59.8 10.2 %collective-permute-start.10 = (f32[27,8,128]{2,1,0:T(8,128)}, f32[27,8,128]{2,1,0:T(8,128)S(1)}, u32[]{:S(2)}, u32[]{:S(2)}) collective-permute-start(f32[27,8,128]{2,1,0:T(8,128)} %copy-done.17), channel_id=1, source_target_pairs={{0,1},{1,0},{2,3},{3,2},{4,5},{5,4},{6,7},{7,6},{8,9},{9,8},{10,11... | collective-permute-start | bytes 331784 | tf_op jit(solution)/shard_map/ppermute | solution.py:141
  59.8 10.2 %collective-permute-start.11 = (f32[27,8,128]{2,1,0:T(8,128)}, f32[27,8,128]{2,1,0:T(8,128)S(1)}, u32[]{:S(2)}, u32[]{:S(2)}) collective-permute-start(f32[27,8,128]{2,1,0:T(8,128)} %copy-done.16), channel_id=1, source_target_pairs={{0,2},{1,3},{2,0},{3,1},{4,6},{5,7},{6,4},{7,5},{8,10},{9,11},{10,... | collective-permute-start | bytes 331784 | tf_op jit(solution)/shard_map/ppermute | solution.py:141
  60.3 9.6 %collective-permute-start.12 = (f32[27,8,128]{2,1,0:T(8,128)S(1)}, f32[27,8,128]{2,1,0:T(8,128)S(1)}, u32[]{:S(2)}, u32[]{:S(2)}) collective-permute-start(f32[27,8,128]{2,1,0:T(8,128)S(1)} %get-tuple-element.51), channel_id=1, source_target_pairs={{0,3},{1,2},{2,1},{3,0},{4,7},{5,6},{6,5},{7,4},{8,11},{9,10},{10,... | collective-permute-start | bytes 331784 | tf_op jit(solution)/shard_map/ppermute | solution.py:141
  64.2 0.9 %copy-start.6 = (f32[27,8,128]{2,1,0:T(8,128)S(1)}, f32[27,8,128]{2,1,0:T(8,128)}, u32[]{:S(2)}) copy-start(f32[27,8,128]{2,1,0:T(8,128)} %copy-done.5) | copy-start | bytes 331780
  65.1 0.9 %copy-start.10 = (f32[27,8,128]{2,1,0:T(8,128)S(1)}, f32[27,8,128]{2,1,0:T(8,128)}, u32[]{:S(2)}) copy-start(f32[27,8,128]{2,1,0:T(8,128)} %copy-done.9) | copy-start | bytes 331780
  66.0 0.9 %copy-start.12 = (f32[27,8,128]{2,1,0:T(8,128)S(1)}, f32[27,8,128]{2,1,0:T(8,128)}, u32[]{:S(2)}) copy-start(f32[27,8,128]{2,1,0:T(8,128)} %copy-done.11) | copy-start | bytes 331780
  66.9 0.9 %copy-start.14 = (f32[27,8,128]{2,1,0:T(8,128)S(1)}, f32[27,8,128]{2,1,0:T(8,128)}, u32[]{:S(2)}) copy-start(f32[27,8,128]{2,1,0:T(8,128)} %copy-done.13) | copy-start | bytes 331780
  67.8 2.1 %copy-start.8 = (f32[27,8,128]{2,1,0:T(8,128)S(1)}, f32[27,8,128]{2,1,0:T(8,128)}, u32[]{:S(2)}) copy-start(f32[27,8,128]{2,1,0:T(8,128)} %copy-done.7) | copy-start | bytes 331780

commit v4 on v3

--- a/solution.py
+++ b/solution.py
@@ -16,6 +16,7 @@
 FIRST_LIMIT = 62 * 1024 * 1024
 SAMPLE_LIMIT = 16 * 1024 * 1024
 RESIDUAL_LIMIT = 16 * 1024 * 1024
+LAST_LIMIT = 4 * 1024 * 1024
 
 
 def passed_along(array, axis, by):
@@ -150,6 +151,7 @@
 SMEM = pl.BlockSpec(memory_space=pltpu.SMEM)
 HBM = pl.BlockSpec(memory_space=pltpu.HBM)
 ANY = pl.BlockSpec(memory_space=pl.ANY)
+MUCH = pl.CostEstimate(flops=10**6, bytes_accessed=6 * 10**7, transcendentals=0)
 LITTLE = pl.CostEstimate(flops=1000, bytes_accessed=1000, transcendentals=0)
 
 
@@ -277,6 +279,9 @@
     edge_q_ref = edge_h_ref = None
     if kind:
         edge_q_ref, edge_h_ref, refs = refs[0], refs[1], refs[2:]
+    carried_refs = ()
+    if kind == 2:
+        carried_refs, refs = refs[: groups - 1], refs[groups - 1 :]
     refs = refs[later:]
     out_refs, grad_ref, refs = refs[:groups], refs[groups], refs[groups + 1 :]
     if kind == 0:
@@ -403,6 +408,8 @@
             out_refs[r][c * step + chunk.nh : (c + 1) * step] = h1_ref[g, c]
         for t in range(tiles_for(coefs * n, quarter)):
             out_refs[r][coefs * step + t] = tail_ref[g, t * quarter : (t + 1) * quarter]
+    for r, carried_ref in enumerate(carried_refs, 1):
+        out_refs[r][chunk.back(coefs, quarter) :] = carried_ref[...]
 
 
 def sample_fields(chunk, me, messages, density, region, coefs, edges, after):
@@ -411,6 +418,9 @@
     n = chunk.n
     f32 = jnp.float32
     shapes = [jax.ShapeDtypeStruct((chunk.back(coefs, quarter), quarter, width), f32)] * groups
+    if chunk.kind == 2:
+        both = chunk.back(coefs, quarter) + edges[2].shape[0]
+        shapes[1:] = [jax.ShapeDtypeStruct((both, quarter, width), f32)] * (groups - 1)
     shapes.append(jax.ShapeDtypeStruct((n, quarter, width), f32))
     if chunk.kind == 0:
         shapes += [jax.ShapeDtypeStruct((2, groups, coefs, quarter, width), f32)] * 2
@@ -455,9 +465,9 @@
         out_ref[c, 0] = row_ref[c, 0:rows]
 
 
-def add_edge(target, message_ref, chunk, coefs, spot, row):
+def add_edge(target, message_ref, chunk, coefs, spot, row, shift=0):
     quarter = message_ref.shape[1]
-    tile = coefs * (chunk.nh + chunk.n) + spot // quarter
+    tile = shift + coefs * (chunk.nh + chunk.n) + spot // quarter
     here = pl.ds(pl.multiple_of(row, quarter), 1)
     target[here] = target[here] + message_ref[tile, spot % quarter : spot % quarter + 1]
 
@@ -472,12 +482,13 @@
         out_specs=VMEM,
         out_shape=jax.ShapeDtypeStruct((coefs, 2, rows, width), jnp.float32),
         scratch_shapes=[pltpu.VMEM((coefs, rows + quarter, width), jnp.float32)],
+        compiler_params=pltpu.CompilerParams(vmem_limit_bytes=LAST_LIMIT),
         cost_estimate=LITTLE,
         name="last_plane",
     )(me, *messages, after)
 
 
-def residual_kernel(chunks, groups, coefs, lo, hi, me_ref, *refs):
+def residual_kernel(chunks, shifts, groups, coefs, lo, hi, me_ref, *refs):
     message_refs = [refs[k * groups : (k + 1) * groups] for k in range(len(chunks))]
     refs = refs[len(chunks) * groups :]
     if lo == 0:
@@ -501,22 +512,22 @@
         return jnp.where(lane == 0, 0.0, pltpu.roll(v, 1, 1))
 
     for c in range(coefs):
-        for chunk, messages in zip(chunks, message_refs):
+        for chunk, shift, messages in zip(chunks, shifts, message_refs):
             step = chunk.nh + chunk.n
             from_h0, to_h0 = max(chunk.lo + chunk.h_from, lo), min(chunk.lo + chunk.h_to, hi)
             from_h1, to_h1 = max(chunk.lo, below), min(chunk.hi, hi)
             for r in range(groups):
                 here = pl.ds(pl.multiple_of(origin(me, r, groups) * quarter, quarter), quarter)
                 if to_h0 > from_h0:
-                    at = c * step - chunk.lo - chunk.h_from
+                    at = shift[r] + c * step - chunk.lo - chunk.h_from
                     h0_ref[c, from_h0 - below : to_h0 - below, here] = messages[r][at + from_h0 : at + to_h0]
                 if to_h1 > from_h1:
-                    at = c * step + chunk.nh - chunk.lo
+                    at = shift[r] + c * step + chunk.nh - chunk.lo
                     h1_ref[c, from_h1 - below : to_h1 - below, here] = messages[r][at + from_h1 : at + to_h1]
             for r in range(groups):
                 above = origin(me, r, groups) * quarter + quarter
                 for i in range(from_h1, to_h1):
-                    add_edge(h1_ref.at[c, i - below], messages[r], chunk, coefs, c * chunk.n + i - chunk.lo, above)
+                    add_edge(h1_ref.at[c, i - below], messages[r], chunk, coefs, c * chunk.n + i - chunk.lo, above, shift[r])
     for c in range(coefs):
         takes[c].wait()
         before = halo_ref[c, 0] if lo == 0 else h1_ref[c, 0, 0:rows]
@@ -535,7 +546,7 @@
         copy.wait()
 
 
-def residual(chunks, me, returned, objective_hat, lo, hi, halo=None, begun=None):
+def residual(chunks, shifts, me, returned, objective_hat, lo, hi, halo=None, begun=None):
     coefs, parts, planes, rows, width = objective_hat.shape
     groups = len(returned[0])
     quarter = rows // groups
@@ -553,7 +564,7 @@
         operands.append(begun)
         specs.append(HBM)
     return pl.pallas_call(
-        functools.partial(residual_kernel, chunks, groups, coefs, lo, hi),
+        functools.partial(residual_kernel, chunks, shifts, groups, coefs, lo, hi),
         in_specs=specs,
         out_specs=HBM,
         out_shape=jax.ShapeDtypeStruct(objective_hat.shape, jnp.float32),
@@ -567,7 +578,7 @@
             pltpu.SemaphoreType.DMA((coefs,)),
         ],
         compiler_params=pltpu.CompilerParams(vmem_limit_bytes=RESIDUAL_LIMIT),
-        cost_estimate=LITTLE,
+        cost_estimate=LITTLE if lo == 0 else MUCH,
         name="residual_first" if lo == 0 else "residual_rest",
     )(*operands)
 
@@ -586,14 +597,17 @@
     sent1 = gauge((last_chunk, first_chunk), groups, me, state_hat, adjoint_hat, upper)
     cells1 = exchange(sent1)
     *out0, grad0, first_q, last_q, pending, last_psi = sample_fields(middle_chunk, me, cells0, density, region, coefs, (), sent1[:1])
-    back0 = exchange(out0)
     *out1, grad1 = sample_fields(last_chunk, me, cells1, density, region, coefs, (last_q, last_psi), ())
     back1 = exchange(out1)
-    *out2, grad2 = sample_fields(first_chunk, me, cells1, density, region, coefs, (first_q, pending), out1[:1])
+    *out2, grad2 = sample_fields(first_chunk, me, cells1, density, region, coefs, (first_q, pending, *out0[1:]), out1[:1])
     back2 = exchange(out2)
+    back0 = [out0[0], *back2[1:]]
+    none = [0] * groups
+    carried = [0] + [first_chunk.back(coefs, rows // groups)] * (groups - 1)
     lower = passed_along(last_plane(last_chunk, me, back1, coefs, out2[0]), "space", 1)
-    begun = residual((middle_chunk, last_chunk), me, (back0, back1), objective_hat, first + 1, planes)
-    adjoint_residual = residual((middle_chunk, first_chunk), me, (back0, back2), objective_hat, 0, first + 1, lower, begun)
+    chunks = (middle_chunk, last_chunk, first_chunk)
+    begun = residual(chunks, (carried, none, none), me, (back0, back1, back2), objective_hat, 1, planes)
+    adjoint_residual = residual((first_chunk,), (none,), me, (back2,), objective_hat, 0, 1, lower, begun)
     return adjoint_residual, jnp.concatenate([grad2, grad0, grad1], axis=0)
 
 

time: 72.7 us -> 66.6 us (0.916)
  waiting for transfers between devices: 26.9 us -> 31.8 us
  local copies, waits for them, and re-layouts: 6.44 us -> 1.57 us
  starting transfers between devices: 18.4 us -> 14.8 us
  Pallas kernels: 18.5 us -> 16.3 us
    ppermute x15 -> x12, waiting for transfers between devices: 18 us -> 22.9 us  [exchange(): taken[r] = lax.ppermute(messages[r], 'sample', pairs)]
    unnamed x36 -> x12, local copies, waits for them, and re-layouts: 6.44 us -> 1.57 us
    ppermute x15 -> x12, starting transfers between devices: 12.8 us -> 9.32 us  [exchange(): taken[r] = lax.ppermute(messages[r], 'sample', pairs)]
    pallas_call x1, Pallas kernels: 1.8 us -> 0.09 us  [last_plane(): pl.pallas_call(functools.partial(last_plane_kernel, chunk, coefs), in_spe...]
  transfers between devices with their start and end apart: 17 -> 14, of which waited for: 6 -> 8; matrix products, arithmetic and copies ran while one was open for 1% -> 1% of each run, Pallas kernels for 16% -> 14%
where the time goes in v4:
time: 66.6 us; the launch traced here: 65.9 us
  waiting for transfers between devices  31.8 us (48%)
  Pallas kernels  16.3 us (24%)
  starting transfers between devices  14.8 us (22%)
  local copies, waits for them, and re-layouts  1.57 us (2%)
  between operations  0.75 us (1%)
    ppermute x12, waiting for transfers between devices, exchange(): taken[r] = lax.ppermute(messages[r], 'sample', pairs)  22.9 us
    ppermute x12, starting transfers between devices, exchange(): taken[r] = lax.ppermute(messages[r], 'sample', pairs)  9.32 us
    ppermute x2, waiting for transfers between devices, passed_along(): return lax.ppermute(array, axis, pairs)  8.91 us
    pallas_call x3, Pallas kernels, sample_fields(): pl.pallas_call(functools.partial(sample_kernel, chunk, groups, coefs, len...  6.54 us
    pallas_call x2, Pallas kernels, gauge(): pl.pallas_call(functools.partial(gauge_kernel, chunks, groups, halo is no...  6.42 us
    ppermute x2, starting transfers between devices, passed_along(): return lax.ppermute(array, axis, pairs)  5.49 us
    pallas_call x2, Pallas kernels, residual(): pl.pallas_call(functools.partial(residual_kernel, chunks, shifts, groups,...  3.26 us
    unnamed x12, local copies, waits for them, and re-layouts  1.57 us
  transfers between devices with their start and end apart: 14, of which 8 were waited for; matrix products, arithmetic and copies ran while one was open for 1% of the time, Pallas kernels for 14%

profile of v4, /device:TPU:0, one launch (start us, length us, event | category | flops | bytes accessed | tf_op | source)
XLA Modules:
  0.0 65.9 jit_solution(14558461166133497600)
XLA Ops:
  0.6 0.0 copy-start
  0.6 3.9 %gauge_middle.1 = (f32[95,8,128]{2,1,0:T(8,128)}, f32[95,8,128]{2,1,0:T(8,128)}, f32[95,8,128]{2,1,0:T(8,128)}, f32[95,8,128]{2,1,0:T(8,128)}, f32[2,5,2,32,128]{4,3,2,1,0:T(8,128)}) custom-call(s32[1]{0:T(128)} %bitcast.me_ref.refs_0_, f32[5,3,8,32,128]{4,3,2,1,0:T(8,128)} %state_ref.3, f32[5,3,8,32,128]{4,3,2,1,0:T(8,128)} %adjoint_ref.3), custom_call_target="tpu_custom_call" | custom-call | flops 1000 | bytes 1000 | tf_op jit(solution)/shard_map/gauge_middle/pallas_call | solution.py:263
  4.5 0.5 collective-permute-start.4
  5.0 1.3 %collective-permute-start = (f32[2,5,2,32,128]{4,3,2,1,0:T(8,128)}, f32[2,5,2,32,128]{4,3,2,1,0:T(8,128)S(1)}, u32[]{:S(2)}, u32[]{:S(2)}) collective-permute-start(f32[2,5,2,32,128]{4,3,2,1,0:T(8,128)} %get-tuple-element.30), channel_id=1, source_target_pairs={{4,0},{8,4},{12,8},{16,12},{20,16},{24,20},{28,24},{5,1},{9,5},{13... | collective-permute-start | bytes 983048 | tf_op jit(solution)/shard_map/ppermute | solution.py:25
  6.3 2.6 %collective-permute-start.5 = (f32[95,8,128]{2,1,0:T(8,128)}, f32[95,8,128]{2,1,0:T(8,128)S(1)}, u32[]{:S(2)}, u32[]{:S(2)}) collective-permute-start(f32[95,8,128]{2,1,0:T(8,128)} %get-tuple-element.37), channel_id=1, source_target_pairs={{0,2},{1,3},{2,0},{3,1},{4,6},{5,7},{6,4},{7,5},{8,10},{9,11},{10,... | collective-permute-start | bytes 1167368 | tf_op jit(solution)/shard_map/ppermute | solution.py:142
  8.9 0.2 collective-permute-start.6
  9.1 8.9 %collective-permute-done.rest_0_ = f32[2,5,2,32,128]{4,3,2,1,0:T(8,128)S(1)} collective-permute-done((f32[2,5,2,32,128]{4,3,2,1,0:T(8,128)}, f32[2,5,2,32,128]{4,3,2,1,0:T(8,128)S(1)}, u32[]{:S(2)}, u32[]{:S(2)}) %collective-permute-start) | collective-permute-done | bytes 327712 | tf_op jit(solution)/shard_map/ppermute | solution.py:25
  18.0 0.0 copy-done
  18.0 0.0 copy-start.1
  18.0 1.5 %copy-done.1 = f32[5,3,8,32,128]{4,3,2,1,0:T(8,128)S(1)} copy-done((f32[5,3,8,32,128]{4,3,2,1,0:T(8,128)S(1)}, f32[5,3,8,32,128]{4,3,2,1,0:T(8,128)}, u32[]{:S(2)}) %copy-start.1) | copy-done | bytes 1966104
  19.6 0.0 copy-start.3
  19.6 0.0 copy-start.4
  19.6 2.5 %gauge_ends.1 = (f32[86,8,128]{2,1,0:T(8,128)S(1)}, f32[86,8,128]{2,1,0:T(8,128)S(1)}, f32[86,8,128]{2,1,0:T(8,128)S(1)}, f32[86,8,128]{2,1,0:T(8,128)S(1)}) custom-call(s32[1]{0:T(128)} %bitcast.me_ref.refs_0_, f32[5,3,8,32,128]{4,3,2,1,0:T(8,128)S(1)} %copy-done, f32[5,3,8,32,128]{4,3,2,1,0:T(8,128)S(1)} %copy-done.1, ...), custom_call_target="tpu_custom_call" | custom-call | flops 1000 | bytes 1000 | tf_op jit(solution)/shard_map/gauge_ends/pallas_call | solution.py:263
  22.1 0.1 collective-permute-start.1
  22.2 1.8 %collective-permute-start.2 = (f32[86,8,128]{2,1,0:T(8,128)S(1)}, f32[86,8,128]{2,1,0:T(8,128)S(1)}, u32[]{:S(2)}, u32[]{:S(2)}) collective-permute-start(f32[86,8,128]{2,1,0:T(8,128)S(1)} %get-tuple-element.33), channel_id=1, source_target_pairs={{0,2},{1,3},{2,0},{3,1},{4,6},{5,7},{6,4},{7,5},{8,10},{9,11},{10,... | collective-permute-start | bytes 1056776 | tf_op jit(solution)/shard_map/ppermute | solution.py:142
  24.0 0.0 collective-permute-done.4.refs_2_
  24.0 0.1 collective-permute-start.3
  24.1 0.0 collective-permute-done.5.refs_3_
  24.1 2.9 %collective-permute-done.6.refs_4_ = f32[95,8,128]{2,1,0:T(8,128)S(1)} collective-permute-done((f32[95,8,128]{2,1,0:T(8,128)}, f32[95,8,128]{2,1,0:T(8,128)S(1)}, u32[]{:S(2)}, u32[]{:S(2)}) %collective-permute-start.6) | collective-permute-done | bytes 389152 | tf_op jit(solution)/shard_map/ppermute | solution.py:142
  27.0 0.0 copy-done.3
  27.0 0.0 copy-done.4
  27.0 0.0 copy-done.5
  27.0 3.3 %samples0.1 = (f32[38,8,128]{2,1,0:T(8,128)S(1)}, f32[38,8,128]{2,1,0:T(8,128)S(1)}, f32[38,8,128]{2,1,0:T(8,128)S(1)}, f32[38,8,128]{2,1,0:T(8,128)S(1)}, f32[4...) custom-call(s32[1]{0:T(128)} %bitcast.me_ref.refs_0_, ...), custom_call_target="tpu_custom_call" | custom-call | flops 1000 | bytes 1000 | tf_op jit(solution)/shard_map/samples0/pallas_call | solution.py:429
  30.2 0.0 collective-permute-done.1.refs_2_
  30.2 4.7 %collective-permute-done.2.refs_3_ = f32[86,8,128]{2,1,0:T(8,128)S(1)} collective-permute-done((f32[86,8,128]{2,1,0:T(8,128)S(1)}, f32[86,8,128]{2,1,0:T(8,128)S(1)}, u32[]{:S(2)}, u32[]{:S(2)}) %collective-permute-start.2) | collective-permute-done | bytes 352288 | tf_op jit(solution)/shard_map/ppermute | solution.py:142
  34.9 7.1 %collective-permute-done.3.refs_4_ = f32[86,8,128]{2,1,0:T(8,128)S(1)} collective-permute-done((f32[86,8,128]{2,1,0:T(8,128)S(1)}, f32[86,8,128]{2,1,0:T(8,128)S(1)}, u32[]{:S(2)}, u32[]{:S(2)}) %collective-permute-start.3) | collective-permute-done | bytes 352288 | tf_op jit(solution)/shard_map/ppermute | solution.py:142
  42.1 1.6 %samples1.1 = (f32[27,8,128]{2,1,0:T(8,128)S(1)}, f32[27,8,128]{2,1,0:T(8,128)S(1)}, f32[27,8,128]{2,1,0:T(8,128)S(1)}, f32[27,8,128]{2,1,0:T(8,128)S(1)}, f32[2,8,128]{2,1,0:T(8,128)S(1)}) custom-call(s32[1]{0:T(128)} %bitcast.me_ref.refs_0_, f32[86,8,128]{2,1,0:T(8,128)S(1)} %get-tuple-element.31.refs_7_.refs_1_, ...), custom_call_target="tpu_custom_call" | custom-call | flops 1000 | bytes 1000 | tf_op jit(solution)/shard_map/samples1/pallas_call | solution.py:429
  43.7 0.0 copy-start.2
  43.7 0.2 collective-permute-start.10
  43.9 1.7 %collective-permute-start.11 = (f32[27,8,128]{2,1,0:T(8,128)S(1)}, f32[27,8,128]{2,1,0:T(8,128)S(1)}, u32[]{:S(2)}, u32[]{:S(2)}) collective-permute-start(f32[27,8,128]{2,1,0:T(8,128)S(1)} %get-tuple-element.52), channel_id=1, source_target_pairs={{0,2},{1,3},{2,0},{3,1},{4,6},{5,7},{6,4},{7,5},{8,10},{9,11},{10,... | collective-permute-start | bytes 331784 | tf_op jit(solution)/shard_map/ppermute | solution.py:142
  45.6 0.1 collective-permute-start.12
  45.7 1.7 %samples2.1 = (f32[27,8,128]{2,1,0:T(8,128)S(1)}, f32[65,8,128]{2,1,0:T(8,128)S(1)}, f32[65,8,128]{2,1,0:T(8,128)S(1)}, f32[65,8,128]{2,1,0:T(8,128)S(1)}, f32[2,8,128]{2,1,0:T(8,128)S(1)}) custom-call(s32[1]{0:T(128)} %bitcast.me_ref.refs_0_, f32[86,8,128]{2,1,0:T(8,128)S(1)} %get-tuple-element.31.refs_7_.refs_1_, ...), custom_call_target="tpu_custom_call" | custom-call | flops 1000 | bytes 1000 | tf_op jit(solution)/shard_map/samples2/pallas_call | solution.py:429
  47.3 0.4 collective-permute-start.7
  47.8 1.7 %collective-permute-start.8 = (f32[65,8,128]{2,1,0:T(8,128)S(1)}, f32[65,8,128]{2,1,0:T(8,128)S(1)}, u32[]{:S(2)}, u32[]{:S(2)}) collective-permute-start(f32[65,8,128]{2,1,0:T(8,128)S(1)} %get-tuple-element.49), channel_id=1, source_target_pairs={{0,2},{1,3},{2,0},{3,1},{4,6},{5,7},{6,4},{7,5},{8,10},{9,11},{10,... | collective-permute-start | bytes 798728 | tf_op jit(solution)/shard_map/ppermute | solution.py:142
  49.4 0.0 collective-permute-done.10.refs_1_.refs_5_
  49.4 0.0 collective-permute-start.9
  49.4 0.3 collective-permute-done.11.refs_2_.refs_6_
  49.7 1.6 %collective-permute-done.12.refs_3_.refs_7_ = f32[27,8,128]{2,1,0:T(8,128)S(1)} collective-permute-done((f32[27,8,128]{2,1,0:T(8,128)S(1)}, f32[27,8,128]{2,1,0:T(8,128)S(1)}, u32[]{:S(2)}, u32[]{:S(2)}) %collective-permute-start.12) | collective-permute-done | bytes 110624 | tf_op jit(solution)/shard_map/ppermute | solution.py:142
  51.3 0.1 last_plane.1
  51.4 4.2 %collective-permute-start.13 = (f32[5,2,32,128]{3,2,1,0:T(8,128)S(1)}, f32[5,2,32,128]{3,2,1,0:T(8,128)S(1)}, u32[]{:S(2)}, u32[]{:S(2)}) collective-permute-start(f32[5,2,32,128]{3,2,1,0:T(8,128)S(1)} %last_plane.1), channel_id=1, source_target_pairs={{0,4},{4,8},{8,12},{12,16},{16,20},{20,24},{24,28},{1,5},{5,9},{9,... | collective-permute-start | bytes 491528 | tf_op jit(solution)/shard_map/ppermute | solution.py:25
  55.6 0.6 pad_maximum_fusion
  56.3 0.0 collective-permute-done.7.refs_1_.refs_9_
  56.3 1.6 %collective-permute-done.8.refs_2_.refs_10_ = f32[65,8,128]{2,1,0:T(8,128)S(1)} collective-permute-done((f32[65,8,128]{2,1,0:T(8,128)S(1)}, f32[65,8,128]{2,1,0:T(8,128)S(1)}, u32[]{:S(2)}, u32[]{:S(2)}) %collective-permute-start.8) | collective-permute-done | bytes 266272 | tf_op jit(solution)/shard_map/ppermute | solution.py:142
  57.8 4.8 %collective-permute-done.9.refs_3_.refs_11_ = f32[65,8,128]{2,1,0:T(8,128)S(1)} collective-permute-done((f32[65,8,128]{2,1,0:T(8,128)S(1)}, f32[65,8,128]{2,1,0:T(8,128)S(1)}, u32[]{:S(2)}, u32[]{:S(2)}) %collective-permute-start.9) | collective-permute-done | bytes 266272 | tf_op jit(solution)/shard_map/ppermute | solution.py:142
  62.6 0.0 copy-done.2
  62.6 1.9 %residual_rest.1.refs_6_ = f32[5,3,8,32,128]{4,3,2,1,0:T(8,128)} custom-call(s32[1]{0:T(128)} %bitcast.me_ref.refs_0_, f32[38,8,128]{2,1,0:T(8,128)S(1)} %get-tuple-element.54.refs_0_, f32[65,8,128]{2,1,0:T(8,128)S(1)} %collective-permute-done.7.refs_1_.refs_9_, f32[65,8,128]{2,1,0:T(8,128)S(1)} %collective-permute-done.8.refs_2_.refs_10_, ...), custom_call_target="tpu_custom_call" | custom-call | flops 1000000 | bytes 60000000 | tf_op jit(solution)/shard_map/residual_rest/pallas_call | solution.py:566
  64.5 0.0 collective-permute-done.13.refs_4_
  64.5 1.3 %residual_first.1 = f32[5,3,8,32,128]{4,3,2,1,0:T(8,128)} custom-call(s32[1]{0:T(128)} %bitcast.me_ref.refs_0_, f32[27,8,128]{2,1,0:T(8,128)S(1)} %get-tuple-element.47.refs_4_.refs_8_.refs_0_, f32[65,8,128]{2,1,0:T(8,128)S(1)} %collective-permute-done.7.refs_1_.refs_9_, ...), custom_call_target="tpu_custom_call", output_to_operand_aliasing={{}: (7, {})} | custom-call | flops 1000 | bytes 1000 | tf_op jit(solution)/shard_map/residual_first/pallas_call | solution.py:566
  (1 shorter events, 0.0 us)
Async XLA Ops:
  0.6 17.4 %copy-start = (f32[5,3,8,32,128]{4,3,2,1,0:T(8,128)S(1)}, f32[5,3,8,32,128]{4,3,2,1,0:T(8,128)}, u32[]{:S(2)}) copy-start(f32[5,3,8,32,128]{4,3,2,1,0:T(8,128)} %state_ref.3) | copy-start | bytes 5898244
  4.5 19.5 %collective-permute-start.4 = (f32[95,8,128]{2,1,0:T(8,128)}, f32[95,8,128]{2,1,0:T(8,128)S(1)}, u32[]{:S(2)}, u32[]{:S(2)}) collective-permute-start(f32[95,8,128]{2,1,0:T(8,128)} %get-tuple-element.36), channel_id=1, source_target_pairs={{0,1},{1,0},{2,3},{3,2},{4,5},{5,4},{6,7},{7,6},{8,9},{9,8},{10,11... | collective-permute-start | bytes 1167368 | tf_op jit(solution)/shard_map/ppermute | solution.py:142
  5.0 13.0 %collective-permute-start = (f32[2,5,2,32,128]{4,3,2,1,0:T(8,128)}, f32[2,5,2,32,128]{4,3,2,1,0:T(8,128)S(1)}, u32[]{:S(2)}, u32[]{:S(2)}) collective-permute-start(f32[2,5,2,32,128]{4,3,2,1,0:T(8,128)} %get-tuple-element.30), channel_id=1, source_target_pairs={{4,0},{8,4},{12,8},{16,12},{20,16},{24,20},{28,24},{5,1},{9,5},{13... | collective-permute-start | bytes 983048 | tf_op jit(solution)/shard_map/ppermute | solution.py:25
  6.3 17.8 %collective-permute-start.5 = (f32[95,8,128]{2,1,0:T(8,128)}, f32[95,8,128]{2,1,0:T(8,128)S(1)}, u32[]{:S(2)}, u32[]{:S(2)}) collective-permute-start(f32[95,8,128]{2,1,0:T(8,128)} %get-tuple-element.37), channel_id=1, source_target_pairs={{0,2},{1,3},{2,0},{3,1},{4,6},{5,7},{6,4},{7,5},{8,10},{9,11},{10,... | collective-permute-start | bytes 1167368 | tf_op jit(solution)/shard_map/ppermute | solution.py:142
  8.9 18.0 %collective-permute-start.6 = (f32[95,8,128]{2,1,0:T(8,128)}, f32[95,8,128]{2,1,0:T(8,128)S(1)}, u32[]{:S(2)}, u32[]{:S(2)}) collective-permute-start(f32[95,8,128]{2,1,0:T(8,128)} %get-tuple-element.38), channel_id=1, source_target_pairs={{0,3},{1,2},{2,1},{3,0},{4,7},{5,6},{6,5},{7,4},{8,11},{9,10},{10,... | collective-permute-start | bytes 1167368 | tf_op jit(solution)/shard_map/ppermute | solution.py:142
  18.0 1.5 %copy-start.1 = (f32[5,3,8,32,128]{4,3,2,1,0:T(8,128)S(1)}, f32[5,3,8,32,128]{4,3,2,1,0:T(8,128)}, u32[]{:S(2)}) copy-start(f32[5,3,8,32,128]{4,3,2,1,0:T(8,128)} %adjoint_ref.3) | copy-start | bytes 5898244
  19.6 7.4 %copy-start.3 = (f32[8,32,128]{2,1,0:T(8,128)S(1)}, f32[8,32,128]{2,1,0:T(8,128)}, u32[]{:S(2)}) copy-start(f32[8,32,128]{2,1,0:T(8,128)} %refs_5_.6) | copy-start | bytes 393220
  19.6 7.4 %copy-start.4 = (s32[8,32,128]{2,1,0:T(8,128)S(1)}, s32[8,32,128]{2,1,0:T(8,128)}, u32[]{:S(2)}) copy-start(s32[8,32,128]{2,1,0:T(8,128)} %refs_6_.5) | copy-start | bytes 393220
  19.6 7.4 %copy-start.5 = (f32[95,8,128]{2,1,0:T(8,128)S(1)}, f32[95,8,128]{2,1,0:T(8,128)}, u32[]{:S(2)}) copy-start(f32[95,8,128]{2,1,0:T(8,128)} %get-tuple-element.35.refs_1_) | copy-start | bytes 1167364
  22.1 8.1 %collective-permute-start.1 = (f32[86,8,128]{2,1,0:T(8,128)S(1)}, f32[86,8,128]{2,1,0:T(8,128)S(1)}, u32[]{:S(2)}, u32[]{:S(2)}) collective-permute-start(f32[86,8,128]{2,1,0:T(8,128)S(1)} %get-tuple-element.32), channel_id=1, source_target_pairs={{0,1},{1,0},{2,3},{3,2},{4,5},{5,4},{6,7},{7,6},{8,9},{9,8},{10,11... | collective-permute-start | bytes 1056776 | tf_op jit(solution)/shard_map/ppermute | solution.py:142
  22.2 12.7 %collective-permute-start.2 = (f32[86,8,128]{2,1,0:T(8,128)S(1)}, f32[86,8,128]{2,1,0:T(8,128)S(1)}, u32[]{:S(2)}, u32[]{:S(2)}) collective-permute-start(f32[86,8,128]{2,1,0:T(8,128)S(1)} %get-tuple-element.33), channel_id=1, source_target_pairs={{0,2},{1,3},{2,0},{3,1},{4,6},{5,7},{6,4},{7,5},{8,10},{9,11},{10,... | collective-permute-start | bytes 1056776 | tf_op jit(solution)/shard_map/ppermute | solution.py:142
  24.0 18.0 %collective-permute-start.3 = (f32[86,8,128]{2,1,0:T(8,128)S(1)}, f32[86,8,128]{2,1,0:T(8,128)S(1)}, u32[]{:S(2)}, u32[]{:S(2)}) collective-permute-start(f32[86,8,128]{2,1,0:T(8,128)S(1)} %get-tuple-element.34), channel_id=1, source_target_pairs={{0,3},{1,2},{2,1},{3,0},{4,7},{5,6},{6,5},{7,4},{8,11},{9,10},{10,... | collective-permute-start | bytes 1056776 | tf_op jit(solution)/shard_map/ppermute | solution.py:142
  43.7 18.9 %copy-start.2 = (f32[5,3,8,32,128]{4,3,2,1,0:T(8,128)S(1)}, f32[5,3,8,32,128]{4,3,2,1,0:T(8,128)}, u32[]{:S(2)}) copy-start(f32[5,3,8,32,128]{4,3,2,1,0:T(8,128)} %refs_5_.7) | copy-start | bytes 5898244
  43.7 5.7 %collective-permute-start.10 = (f32[27,8,128]{2,1,0:T(8,128)S(1)}, f32[27,8,128]{2,1,0:T(8,128)S(1)}, u32[]{:S(2)}, u32[]{:S(2)}) collective-permute-start(f32[27,8,128]{2,1,0:T(8,128)S(1)} %get-tuple-element.51), channel_id=1, source_target_pairs={{0,1},{1,0},{2,3},{3,2},{4,5},{5,4},{6,7},{7,6},{8,9},{9,8},{10,11... | collective-permute-start | bytes 331784 | tf_op jit(solution)/shard_map/ppermute | solution.py:142
  43.9 5.9 %collective-permute-start.11 = (f32[27,8,128]{2,1,0:T(8,128)S(1)}, f32[27,8,128]{2,1,0:T(8,128)S(1)}, u32[]{:S(2)}, u32[]{:S(2)}) collective-permute-start(f32[27,8,128]{2,1,0:T(8,128)S(1)} %get-tuple-element.52), channel_id=1, source_target_pairs={{0,2},{1,3},{2,0},{3,1},{4,6},{5,7},{6,4},{7,5},{8,10},{9,11},{10,... | collective-permute-start | bytes 331784 | tf_op jit(solution)/shard_map/ppermute | solution.py:142
  45.6 5.8 %collective-permute-start.12 = (f32[27,8,128]{2,1,0:T(8,128)S(1)}, f32[27,8,128]{2,1,0:T(8,128)S(1)}, u32[]{:S(2)}, u32[]{:S(2)}) collective-permute-start(f32[27,8,128]{2,1,0:T(8,128)S(1)} %get-tuple-element.53), channel_id=1, source_target_pairs={{0,3},{1,2},{2,1},{3,0},{4,7},{5,6},{6,5},{7,4},{8,11},{9,10},{10,... | collective-permute-start | bytes 331784 | tf_op jit(solution)/shard_map/ppermute | solution.py:142
  47.3 8.9 %collective-permute-start.7 = (f32[65,8,128]{2,1,0:T(8,128)S(1)}, f32[65,8,128]{2,1,0:T(8,128)S(1)}, u32[]{:S(2)}, u32[]{:S(2)}) collective-permute-start(f32[65,8,128]{2,1,0:T(8,128)S(1)} %get-tuple-element.48), channel_id=1, source_target_pairs={{0,1},{1,0},{2,3},{3,2},{4,5},{5,4},{6,7},{7,6},{8,9},{9,8},{10,11... | collective-permute-start | bytes 798728 | tf_op jit(solution)/shard_map/ppermute | solution.py:142
  47.8 10.1 %collective-permute-start.8 = (f32[65,8,128]{2,1,0:T(8,128)S(1)}, f32[65,8,128]{2,1,0:T(8,128)S(1)}, u32[]{:S(2)}, u32[]{:S(2)}) collective-permute-start(f32[65,8,128]{2,1,0:T(8,128)S(1)} %get-tuple-element.49), channel_id=1, source_target_pairs={{0,2},{1,3},{2,0},{3,1},{4,6},{5,7},{6,4},{7,5},{8,10},{9,11},{10,... | collective-permute-start | bytes 798728 | tf_op jit(solution)/shard_map/ppermute | solution.py:142
  49.4 13.1 %collective-permute-start.9 = (f32[65,8,128]{2,1,0:T(8,128)S(1)}, f32[65,8,128]{2,1,0:T(8,128)S(1)}, u32[]{:S(2)}, u32[]{:S(2)}) collective-permute-start(f32[65,8,128]{2,1,0:T(8,128)S(1)} %get-tuple-element.50), channel_id=1, source_target_pairs={{0,3},{1,2},{2,1},{3,0},{4,7},{5,6},{6,5},{7,4},{8,11},{9,10},{10,... | collective-permute-start | bytes 798728 | tf_op jit(solution)/shard_map/ppermute | solution.py:142
  51.4 13.1 %collective-permute-start.13 = (f32[5,2,32,128]{3,2,1,0:T(8,128)S(1)}, f32[5,2,32,128]{3,2,1,0:T(8,128)S(1)}, u32[]{:S(2)}, u32[]{:S(2)}) collective-permute-start(f32[5,2,32,128]{3,2,1,0:T(8,128)S(1)} %last_plane.1), channel_id=1, source_target_pairs={{0,4},{4,8},{8,12},{12,16},{16,20},{20,24},{24,28},{1,5},{5,9},{9,... | collective-permute-start | bytes 491528 | tf_op jit(solution)/shard_map/ppermute | solution.py:25

commit v5 on v4

--- a/solution.py
+++ b/solution.py
@@ -131,10 +131,10 @@
     return lax.rem(me + groups - r, groups)
 
 
-def exchange(messages):
+def exchange(messages, only_cross=False):
     groups = len(messages)
     taken = [messages[0]] + [None] * (groups - 1)
-    for r in list(range(2, groups)) + [1]:
+    for r in list(range(2, groups)) + ([] if only_cross else [1]):
         if groups & (groups - 1) == 0:
             pairs = [(i, i ^ r) for i in range(groups)]
         else:
@@ -151,7 +151,6 @@
 SMEM = pl.BlockSpec(memory_space=pltpu.SMEM)
 HBM = pl.BlockSpec(memory_space=pltpu.HBM)
 ANY = pl.BlockSpec(memory_space=pl.ANY)
-MUCH = pl.CostEstimate(flops=10**6, bytes_accessed=6 * 10**7, transcendentals=0)
 LITTLE = pl.CostEstimate(flops=1000, bytes_accessed=1000, transcendentals=0)
 
 
@@ -176,7 +175,11 @@
 def gauge_kernel(chunks, groups, has_halo, me_ref, state_ref, adjoint_ref, *rest):
     if has_halo:
         halo_ref, rest = rest[0], rest[1:]
-    out_refs, rest = rest[:groups], rest[groups:]
+    outs = [rest[:groups]]
+    rest = rest[groups:]
+    for _ in chunks[1:]:
+        outs.append((*outs[0][:2], *rest[: groups - 2]))
+        rest = rest[groups - 2 :]
     if not has_halo:
         first_ref, first_sems = rest[0], rest[-1]
         rest = rest[1:-1]
@@ -224,16 +227,18 @@
                 p_held[which, c, :, rows : rows + quarter] = zero_rows
                 q_held[which, c] = (second + (phi_up - phi))[chunk.q_from : chunk.q_to]
             for c in range(coefs):
-                base = chunk.at + (which * coefs + c) * (n + nq)
                 for r in range(groups):
+                    out_ref = outs[at][r]
+                    top = chunk.at if r < 2 else 0
+                    base = top + (which * coefs + c) * (n + nq)
                     start = pl.multiple_of(partner(me, r, groups) * quarter, quarter)
-                    out_refs[r][base : base + n] = p_held[which, c, :, pl.ds(start, quarter)]
-                    out_refs[r][base + n : base + n + nq] = q_held[which, c, :, pl.ds(start, quarter)]
+                    out_ref[base : base + n] = p_held[which, c, :, pl.ds(start, quarter)]
+                    out_ref[base + n : base + n + nq] = q_held[which, c, :, pl.ds(start, quarter)]
                     for i in range(n):
                         spot = (which * coefs + c) * n + i
                         edge = p_held[which, c, i, pl.ds(pl.multiple_of(start + quarter, quarter), quarter)]
-                        tile = chunk.at + 2 * coefs * (n + nq) + spot // quarter
-                        out_refs[r][tile, spot % quarter : spot % quarter + 1] = edge[0:1]
+                        tile = top + 2 * coefs * (n + nq) + spot // quarter
+                        out_ref[tile, spot % quarter : spot % quarter + 1] = edge[0:1]
     for copy in firsts:
         copy.wait()
 
@@ -241,8 +246,9 @@
 def gauge(chunks, groups, me, state_hat, adjoint_hat, halo=None):
     coefs, parts, planes, rows, width = state_hat.shape
     quarter = rows // groups
-    tiles = sum(chunk.sent(coefs, quarter) for chunk in chunks)
-    shapes = [jax.ShapeDtypeStruct((tiles, quarter, width), jnp.float32)] * groups
+    tiles = [chunk.sent(coefs, quarter) for chunk in chunks]
+    counts = [sum(tiles)] * 2 + [t for t in tiles for _ in range(groups - 2)]
+    shapes = [jax.ShapeDtypeStruct((t, quarter, width), jnp.float32) for t in counts]
     scratch = []
     for chunk in chunks:
         own = min(chunk.n + 1, planes - chunk.lo)
@@ -303,13 +309,14 @@
 
     for r in range(groups):
         g = origin(me, r, groups)
+        top = chunk.at if r < 2 else 0
         for which in range(2):
             for c in range(coefs):
-                base = chunk.at + (which * coefs + c) * (n + nq)
+                base = top + (which * coefs + c) * (n + nq)
                 p_ref[which, g, c] = message_refs[r][base : base + n]
                 q_ref[which, g, c, chunk.q_from : chunk.q_to] = message_refs[r][base + n : base + n + nq]
         for t in range(tiles_for(2 * coefs * n, quarter)):
-            edge_ref[g, t * quarter : (t + 1) * quarter] = message_refs[r][chunk.at + 2 * coefs * (n + nq) + t]
+            edge_ref[g, t * quarter : (t + 1) * quarter] = message_refs[r][top + 2 * coefs * (n + nq) + t]
     for which in range(2):
         for g in range(groups):
             for c in range(coefs):
@@ -488,25 +495,16 @@
     )(me, *messages, after)
 
 
-def residual_kernel(chunks, shifts, groups, coefs, lo, hi, me_ref, *refs):
+def residual_kernel(chunks, shifts, groups, coefs, me_ref, *refs):
     message_refs = [refs[k * groups : (k + 1) * groups] for k in range(len(chunks))]
     refs = refs[len(chunks) * groups :]
-    if lo == 0:
-        halo_ref, objective_ref, _, out_ref, *refs = refs
-    else:
-        objective_ref, out_ref, *refs = refs
-    h0_ref, h1_ref, taken, given, take_sems, give_sems = refs
+    halo_ref, objective_ref, out_ref, h0_ref, h1_ref, given, give_sems = refs
     parts, planes, rows, width = objective_ref.shape[1:]
     quarter = rows // groups
     me = me_ref[0]
     row = lax.broadcasted_iota(jnp.int32, (rows, width), 0)
     lane = lax.broadcasted_iota(jnp.int32, (rows, width), 1)
-    below = max(lo - 1, 0)
-    wanted = pl.ds(lo, hi - lo)
-    takes = [pltpu.make_async_copy(objective_ref.at[c, :, wanted], taken.at[c], take_sems.at[c]) for c in range(coefs)]
-    gives = [pltpu.make_async_copy(given.at[c], out_ref.at[c, :, wanted], give_sems.at[c]) for c in range(coefs)]
-    for copy in takes:
-        copy.start()
+    gives = [pltpu.make_async_copy(given.at[c], out_ref.at[c], give_sems.at[c]) for c in range(coefs)]
 
     def lower_lane(v):
         return jnp.where(lane == 0, 0.0, pltpu.roll(v, 1, 1))
@@ -514,72 +512,51 @@
     for c in range(coefs):
         for chunk, shift, messages in zip(chunks, shifts, message_refs):
             step = chunk.nh + chunk.n
-            from_h0, to_h0 = max(chunk.lo + chunk.h_from, lo), min(chunk.lo + chunk.h_to, hi)
-            from_h1, to_h1 = max(chunk.lo, below), min(chunk.hi, hi)
+            from_h0, to_h0 = chunk.lo + chunk.h_from, chunk.lo + chunk.h_to
             for r in range(groups):
                 here = pl.ds(pl.multiple_of(origin(me, r, groups) * quarter, quarter), quarter)
-                if to_h0 > from_h0:
-                    at = shift[r] + c * step - chunk.lo - chunk.h_from
-                    h0_ref[c, from_h0 - below : to_h0 - below, here] = messages[r][at + from_h0 : at + to_h0]
-                if to_h1 > from_h1:
-                    at = shift[r] + c * step + chunk.nh - chunk.lo
-                    h1_ref[c, from_h1 - below : to_h1 - below, here] = messages[r][at + from_h1 : at + to_h1]
+                at = shift[r] + c * step
+                h0_ref[c, from_h0:to_h0, here] = messages[r][at : at + to_h0 - from_h0]
+                h1_ref[c, chunk.lo : chunk.hi, here] = messages[r][at + chunk.nh : at + step]
             for r in range(groups):
                 above = origin(me, r, groups) * quarter + quarter
-                for i in range(from_h1, to_h1):
-                    add_edge(h1_ref.at[c, i - below], messages[r], chunk, coefs, c * chunk.n + i - chunk.lo, above, shift[r])
-    for c in range(coefs):
-        takes[c].wait()
-        before = halo_ref[c, 0] if lo == 0 else h1_ref[c, 0, 0:rows]
-        for i in range(lo, hi):
-            h0 = h0_ref[c, i - below]
+                for i in range(chunk.n):
+                    add_edge(h1_ref.at[c, chunk.lo + i], messages[r], chunk, coefs, c * chunk.n + i, above, shift[r])
+        before = halo_ref[c, 0]
+        for i in range(planes):
+            h0 = h0_ref[c, i]
             if i == 0:
                 h0 = h0 + halo_ref[c, 1]
-            h1 = h1_ref[c, i - below, 0:rows]
-            given[c, 0, i - lo] = taken[c, 0, i - lo] - (2.0 / NT) * (lower_lane(h1) - h1)
-            given[c, 1, i - lo] = taken[c, 1, i - lo] - (2.0 / NT) * (h0 - lower_lane(h0))
+            h1 = h1_ref[c, i, 0:rows]
+            given[c, 0, i] = objective_ref[c, 0, i] - (2.0 / NT) * (lower_lane(h1) - h1)
+            given[c, 1, i] = objective_ref[c, 1, i] - (2.0 / NT) * (h0 - lower_lane(h0))
             lower_row = jnp.where(row == 0, 0.0, pltpu.roll(h0, 1, 0))
-            given[c, 2, i - lo] = taken[c, 2, i - lo] - (2.0 / NT) * ((lower_row - h0) - (before - h1))
+            given[c, 2, i] = objective_ref[c, 2, i] - (2.0 / NT) * ((lower_row - h0) - (before - h1))
             before = h1
         gives[c].start()
     for copy in gives:
         copy.wait()
 
 
-def residual(chunks, shifts, me, returned, objective_hat, lo, hi, halo=None, begun=None):
+def residual(chunks, shifts, me, returned, objective_hat, halo):
     coefs, parts, planes, rows, width = objective_hat.shape
     groups = len(returned[0])
     quarter = rows // groups
-    held = hi - max(lo - 1, 0)
-    operands = [me] + [m for messages in returned for m in messages]
-    specs = [SMEM] + [VMEM] * (len(operands) - 1)
-    if lo == 0:
-        operands.append(halo)
-        specs.append(VMEM)
-    operands.append(objective_hat)
-    specs.append(HBM)
-    aliases = {}
-    if lo == 0:
-        aliases = {len(operands): 0}
-        operands.append(begun)
-        specs.append(HBM)
+    operands = [me] + [m for messages in returned for m in messages] + [halo, objective_hat]
     return pl.pallas_call(
-        functools.partial(residual_kernel, chunks, shifts, groups, coefs, lo, hi),
-        in_specs=specs,
+        functools.partial(residual_kernel, chunks, shifts, groups, coefs),
+        in_specs=[SMEM] + [VMEM] * (len(operands) - 1),
         out_specs=HBM,
         out_shape=jax.ShapeDtypeStruct(objective_hat.shape, jnp.float32),
-        input_output_aliases=aliases,
         scratch_shapes=[
-            pltpu.VMEM((coefs, held, rows, width), jnp.float32),
-            pltpu.VMEM((coefs, held, rows + quarter, width), jnp.float32),
-            pltpu.VMEM((coefs, parts, hi - lo, rows, width), jnp.float32),
-            pltpu.VMEM((coefs, parts, hi - lo, rows, width), jnp.float32),
-            pltpu.SemaphoreType.DMA((coefs,)),
+            pltpu.VMEM((coefs, planes, rows, width), jnp.float32),
+            pltpu.VMEM((coefs, planes, rows + quarter, width), jnp.float32),
+            pltpu.VMEM((coefs, parts, planes, rows, width), jnp.float32),
             pltpu.SemaphoreType.DMA((coefs,)),
         ],
         compiler_params=pltpu.CompilerParams(vmem_limit_bytes=RESIDUAL_LIMIT),
-        cost_estimate=LITTLE if lo == 0 else MUCH,
-        name="residual_first" if lo == 0 else "residual_rest",
+        cost_estimate=LITTLE,
+        name="residual",
     )(*operands)
 
 
@@ -595,19 +572,19 @@
     cells0 = exchange(sent0)
     upper = passed_along(first_planes, "space", -1)
     sent1 = gauge((last_chunk, first_chunk), groups, me, state_hat, adjoint_hat, upper)
-    cells1 = exchange(sent1)
+    cells1 = exchange(sent1[:groups])
+    cells2 = cells1[:2] + exchange([None, None, *sent1[groups:]], only_cross=True)[2:]
     *out0, grad0, first_q, last_q, pending, last_psi = sample_fields(middle_chunk, me, cells0, density, region, coefs, (), sent1[:1])
     *out1, grad1 = sample_fields(last_chunk, me, cells1, density, region, coefs, (last_q, last_psi), ())
     back1 = exchange(out1)
-    *out2, grad2 = sample_fields(first_chunk, me, cells1, density, region, coefs, (first_q, pending, *out0[1:]), out1[:1])
+    *out2, grad2 = sample_fields(first_chunk, me, cells2, density, region, coefs, (first_q, pending, *out0[1:]), out1[:1])
     back2 = exchange(out2)
     back0 = [out0[0], *back2[1:]]
     none = [0] * groups
     carried = [0] + [first_chunk.back(coefs, rows // groups)] * (groups - 1)
     lower = passed_along(last_plane(last_chunk, me, back1, coefs, out2[0]), "space", 1)
     chunks = (middle_chunk, last_chunk, first_chunk)
-    begun = residual(chunks, (carried, none, none), me, (back0, back1, back2), objective_hat, 1, planes)
-    adjoint_residual = residual((first_chunk,), (none,), me, (back2,), objective_hat, 0, 1, lower, begun)
+    adjoint_residual = residual(chunks, (carried, none, none), me, (back0, back1, back2), objective_hat, lower)
     return adjoint_residual, jnp.concatenate([grad2, grad0, grad1], axis=0)
 
 

time: 66.6 us -> 60.9 us (0.914)
  the two profiles are of different devices: /device:TPU:0 before, /device:TPU:17 now
where the time goes in v5:
time: 60.9 us; the launch traced here: 60.7 us
  waiting for transfers between devices  25.3 us (42%)
  starting transfers between devices  17.9 us (29%)
  Pallas kernels  14.6 us (24%)
  local copies, waits for them, and re-layouts  1.56 us (3%)
  between operations  0.74 us (1%)
  other arithmetic  0.62 us (1%)
    ppermute x14, waiting for transfers between devices, exchange(): taken[r] = lax.ppermute(messages[r], 'sample', pairs)  20.3 us
    ppermute x14, starting transfers between devices, exchange(): taken[r] = lax.ppermute(messages[r], 'sample', pairs)  12.6 us
    pallas_call x3, Pallas kernels, sample_fields(): pl.pallas_call(functools.partial(sample_kernel, chunk, groups, coefs, len...  6.53 us
    pallas_call x2, Pallas kernels, gauge(): pl.pallas_call(functools.partial(gauge_kernel, chunks, groups, halo is no...  6.4 us
    ppermute x2, starting transfers between devices, passed_along(): return lax.ppermute(array, axis, pairs)  5.27 us
    ppermute x2, waiting for transfers between devices, passed_along(): return lax.ppermute(array, axis, pairs)  4.93 us
    pallas_call x1, Pallas kernels, residual(): pl.pallas_call(functools.partial(residual_kernel, chunks, shifts, groups,...  1.59 us
    unnamed x12, local copies, waits for them, and re-layouts  1.56 us
  transfers between devices with their start and end apart: 16, of which 7 were waited for; matrix products, arithmetic and copies ran while one was open for 1% of the time, Pallas kernels for 15%

profile of v5, /device:TPU:17, one launch (start us, length us, event | category | flops | bytes accessed | tf_op | source)
XLA Modules:
  0.0 60.7 jit_solution(8154513365593886445)
XLA Ops:
  0.6 0.0 copy-start
  0.6 3.9 %gauge_middle.1 = (f32[95,8,128]{2,1,0:T(8,128)}, f32[95,8,128]{2,1,0:T(8,128)}, f32[95,8,128]{2,1,0:T(8,128)}, f32[95,8,128]{2,1,0:T(8,128)}, f32[2,5,2,32,128]{4,3,2,1,0:T(8,128)}) custom-call(s32[1]{0:T(128)} %bitcast.me_ref.refs_0_, f32[5,3,8,32,128]{4,3,2,1,0:T(8,128)} %state_ref.3, f32[5,3,8,32,128]{4,3,2,1,0:T(8,128)} %adjoint_ref.3), custom_call_target="tpu_custom_call" | custom-call | flops 1000 | bytes 1000 | tf_op jit(solution)/shard_map/gauge_middle/pallas_call | solution.py:269
  4.5 3.0 %collective-permute-start.3 = (f32[2,5,2,32,128]{4,3,2,1,0:T(8,128)}, f32[2,5,2,32,128]{4,3,2,1,0:T(8,128)S(1)}, u32[]{:S(2)}, u32[]{:S(2)}) collective-permute-start(f32[2,5,2,32,128]{4,3,2,1,0:T(8,128)} %get-tuple-element.36), channel_id=1, source_target_pairs={{4,0},{8,4},{12,8},{16,12},{20,16},{24,20},{28,24},{5,1},{9,5},{13... | collective-permute-start | bytes 983048 | tf_op jit(solution)/shard_map/ppermute | solution.py:25
  7.5 1.0 %collective-permute-start = (f32[95,8,128]{2,1,0:T(8,128)}, f32[95,8,128]{2,1,0:T(8,128)S(1)}, u32[]{:S(2)}, u32[]{:S(2)}) collective-permute-start(f32[95,8,128]{2,1,0:T(8,128)} %get-tuple-element.33), channel_id=1, source_target_pairs={{0,1},{1,0},{2,3},{3,2},{4,5},{5,4},{6,7},{7,6},{8,9},{9,8},{10,11... | collective-permute-start | bytes 1167368 | tf_op jit(solution)/shard_map/ppermute | solution.py:142
  8.6 1.3 %collective-permute-start.1 = (f32[95,8,128]{2,1,0:T(8,128)}, f32[95,8,128]{2,1,0:T(8,128)S(1)}, u32[]{:S(2)}, u32[]{:S(2)}) collective-permute-start(f32[95,8,128]{2,1,0:T(8,128)} %get-tuple-element.34), channel_id=1, source_target_pairs={{0,2},{1,3},{2,0},{3,1},{4,6},{5,7},{6,4},{7,5},{8,10},{9,11},{10,... | collective-permute-start | bytes 1167368 | tf_op jit(solution)/shard_map/ppermute | solution.py:142
  9.8 0.5 collective-permute-start.2
  10.3 4.9 %collective-permute-done.3.rest_0_ = f32[2,5,2,32,128]{4,3,2,1,0:T(8,128)S(1)} collective-permute-done((f32[2,5,2,32,128]{4,3,2,1,0:T(8,128)}, f32[2,5,2,32,128]{4,3,2,1,0:T(8,128)S(1)}, u32[]{:S(2)}, u32[]{:S(2)}) %collective-permute-start.3) | collective-permute-done | bytes 327712 | tf_op jit(solution)/shard_map/ppermute | solution.py:25
  15.2 0.0 copy-done
  15.2 0.0 copy-start.1
  15.2 1.5 %copy-done.1 = f32[5,3,8,32,128]{4,3,2,1,0:T(8,128)S(1)} copy-done((f32[5,3,8,32,128]{4,3,2,1,0:T(8,128)S(1)}, f32[5,3,8,32,128]{4,3,2,1,0:T(8,128)}, u32[]{:S(2)}) %copy-start.1) | copy-done | bytes 1966104
  16.8 2.5 %gauge_ends.1 = (f32[86,8,128]{2,1,0:T(8,128)S(1)}, f32[86,8,128]{2,1,0:T(8,128)S(1)}, f32[43,8,128]{2,1,0:T(8,128)S(1)}, f32[43,8,128]{2,1,0:T(8,128)S(1)}, f32...) custom-call(s32[1]{0:T(128)} %bitcast.me_ref.refs_0_, f32[5,3,8,32,128]{4,3,2,1,0:T(8,128)S(1)} %copy-done, ...), custom_call_target="tpu_custom_call" | custom-call | flops 1000 | bytes 1000 | tf_op jit(solution)/shard_map/gauge_ends/pallas_call | solution.py:269
  19.3 1.6 %collective-permute-start.4 = (f32[86,8,128]{2,1,0:T(8,128)S(1)}, f32[86,8,128]{2,1,0:T(8,128)S(1)}, u32[]{:S(2)}, u32[]{:S(2)}) collective-permute-start(f32[86,8,128]{2,1,0:T(8,128)S(1)} %get-tuple-element.39), channel_id=1, source_target_pairs={{0,1},{1,0},{2,3},{3,2},{4,5},{5,4},{6,7},{7,6},{8,9},{9,8},{10,11... | collective-permute-start | bytes 1056776 | tf_op jit(solution)/shard_map/ppermute | solution.py:142
  20.9 1.3 %collective-permute-start.7 = (f32[43,8,128]{2,1,0:T(8,128)S(1)}, f32[43,8,128]{2,1,0:T(8,128)S(1)}, u32[]{:S(2)}, u32[]{:S(2)}) collective-permute-start(f32[43,8,128]{2,1,0:T(8,128)S(1)} %get-tuple-element.47), channel_id=1, source_target_pairs={{0,2},{1,3},{2,0},{3,1},{4,6},{5,7},{6,4},{7,5},{8,10},{9,11},{10,... | collective-permute-start | bytes 528392 | tf_op jit(solution)/shard_map/ppermute | solution.py:142
  22.2 0.0 collective-permute-done.refs_2_
  22.2 0.5 collective-permute-start.8
  22.6 0.0 collective-permute-done.1.refs_3_
  22.6 1.2 %collective-permute-start.5 = (f32[43,8,128]{2,1,0:T(8,128)S(1)}, f32[43,8,128]{2,1,0:T(8,128)S(1)}, u32[]{:S(2)}, u32[]{:S(2)}) collective-permute-start(f32[43,8,128]{2,1,0:T(8,128)S(1)} %get-tuple-element.40), channel_id=1, source_target_pairs={{0,2},{1,3},{2,0},{3,1},{4,6},{5,7},{6,4},{7,5},{8,10},{9,11},{10,... | collective-permute-start | bytes 528392 | tf_op jit(solution)/shard_map/ppermute | solution.py:142
  23.9 4.4 %collective-permute-done.2.refs_4_ = f32[95,8,128]{2,1,0:T(8,128)S(1)} collective-permute-done((f32[95,8,128]{2,1,0:T(8,128)}, f32[95,8,128]{2,1,0:T(8,128)S(1)}, u32[]{:S(2)}, u32[]{:S(2)}) %collective-permute-start.2) | collective-permute-done | bytes 389152 | tf_op jit(solution)/shard_map/ppermute | solution.py:142
  28.3 0.9 %collective-permute-start.6 = (f32[43,8,128]{2,1,0:T(8,128)S(1)}, f32[43,8,128]{2,1,0:T(8,128)S(1)}, u32[]{:S(2)}, u32[]{:S(2)}) collective-permute-start(f32[43,8,128]{2,1,0:T(8,128)S(1)} %get-tuple-element.41), channel_id=1, source_target_pairs={{0,3},{1,2},{2,1},{3,0},{4,7},{5,6},{6,5},{7,4},{8,11},{9,10},{10,... | collective-permute-start | bytes 528392 | tf_op jit(solution)/shard_map/ppermute | solution.py:142
  29.2 0.0 copy-done.3
  29.2 0.0 copy-done.4
  29.2 0.0 copy-done.5
  29.2 3.3 %samples0.1 = (f32[38,8,128]{2,1,0:T(8,128)S(1)}, f32[38,8,128]{2,1,0:T(8,128)S(1)}, f32[38,8,128]{2,1,0:T(8,128)S(1)}, f32[38,8,128]{2,1,0:T(8,128)S(1)}, f32[4...) custom-call(s32[1]{0:T(128)} %bitcast.me_ref.refs_0_, ...), custom_call_target="tpu_custom_call" | custom-call | flops 1000 | bytes 1000 | tf_op jit(solution)/shard_map/samples0/pallas_call | solution.py:436
  32.5 0.0 collective-permute-done.7.refs_3_
  32.5 3.4 %collective-permute-done.8.refs_4_ = f32[43,8,128]{2,1,0:T(8,128)S(1)} collective-permute-done((f32[43,8,128]{2,1,0:T(8,128)S(1)}, f32[43,8,128]{2,1,0:T(8,128)S(1)}, u32[]{:S(2)}, u32[]{:S(2)}) %collective-permute-start.8) | collective-permute-done | bytes 176160 | tf_op jit(solution)/shard_map/ppermute | solution.py:142
  35.9 0.0 collective-permute-done.4.refs_2_
  35.9 1.6 %samples1.1 = (f32[27,8,128]{2,1,0:T(8,128)S(1)}, f32[27,8,128]{2,1,0:T(8,128)S(1)}, f32[27,8,128]{2,1,0:T(8,128)S(1)}, f32[27,8,128]{2,1,0:T(8,128)S(1)}, f32[2,8,128]{2,1,0:T(8,128)S(1)}) custom-call(s32[1]{0:T(128)} %bitcast.me_ref.refs_0_, f32[86,8,128]{2,1,0:T(8,128)S(1)} %get-tuple-element.37.refs_7_.refs_1_, ...), custom_call_target="tpu_custom_call" | custom-call | flops 1000 | bytes 1000 | tf_op jit(solution)/shard_map/samples1/pallas_call | solution.py:436
  37.5 0.1 collective-permute-start.12
  37.6 1.3 %collective-permute-start.13 = (f32[27,8,128]{2,1,0:T(8,128)S(1)}, f32[27,8,128]{2,1,0:T(8,128)S(1)}, u32[]{:S(2)}, u32[]{:S(2)}) collective-permute-start(f32[27,8,128]{2,1,0:T(8,128)S(1)} %get-tuple-element.56), channel_id=1, source_target_pairs={{0,2},{1,3},{2,0},{3,1},{4,6},{5,7},{6,4},{7,5},{8,10},{9,11},{10,... | collective-permute-start | bytes 331784 | tf_op jit(solution)/shard_map/ppermute | solution.py:142
  38.9 0.8 %collective-permute-start.14 = (f32[27,8,128]{2,1,0:T(8,128)S(1)}, f32[27,8,128]{2,1,0:T(8,128)S(1)}, u32[]{:S(2)}, u32[]{:S(2)}) collective-permute-start(f32[27,8,128]{2,1,0:T(8,128)S(1)} %get-tuple-element.57), channel_id=1, source_target_pairs={{0,3},{1,2},{2,1},{3,0},{4,7},{5,6},{6,5},{7,4},{8,11},{9,10},{10,... | collective-permute-start | bytes 331784 | tf_op jit(solution)/shard_map/ppermute | solution.py:142
  39.7 0.0 collective-permute-done.5.refs_3_
  39.7 3.7 %collective-permute-done.6.refs_4_ = f32[43,8,128]{2,1,0:T(8,128)S(1)} collective-permute-done((f32[43,8,128]{2,1,0:T(8,128)S(1)}, f32[43,8,128]{2,1,0:T(8,128)S(1)}, u32[]{:S(2)}, u32[]{:S(2)}) %collective-permute-start.6) | collective-permute-done | bytes 176160 | tf_op jit(solution)/shard_map/ppermute | solution.py:142
  43.4 1.7 %samples2.1 = (f32[27,8,128]{2,1,0:T(8,128)S(1)}, f32[65,8,128]{2,1,0:T(8,128)S(1)}, f32[65,8,128]{2,1,0:T(8,128)S(1)}, f32[65,8,128]{2,1,0:T(8,128)S(1)}, f32[2,8,128]{2,1,0:T(8,128)S(1)}) custom-call(s32[1]{0:T(128)} %bitcast.me_ref.refs_0_, f32[86,8,128]{2,1,0:T(8,128)S(1)} %get-tuple-element.37.refs_7_.refs_1_, ...), custom_call_target="tpu_custom_call" | custom-call | flops 1000 | bytes 1000 | tf_op jit(solution)/shard_map/samples2/pallas_call | solution.py:436
  45.1 0.1 collective-permute-start.9
  45.2 1.3 %collective-permute-start.10 = (f32[65,8,128]{2,1,0:T(8,128)S(1)}, f32[65,8,128]{2,1,0:T(8,128)S(1)}, u32[]{:S(2)}, u32[]{:S(2)}) collective-permute-start(f32[65,8,128]{2,1,0:T(8,128)S(1)} %get-tuple-element.53), channel_id=1, source_target_pairs={{0,2},{1,3},{2,0},{3,1},{4,6},{5,7},{6,4},{7,5},{8,10},{9,11},{10,... | collective-permute-start | bytes 798728 | tf_op jit(solution)/shard_map/ppermute | solution.py:142
  46.5 0.0 collective-permute-done.12.refs_1_.refs_5_
  46.5 0.8 %collective-permute-start.11 = (f32[65,8,128]{2,1,0:T(8,128)S(1)}, f32[65,8,128]{2,1,0:T(8,128)S(1)}, u32[]{:S(2)}, u32[]{:S(2)}) collective-permute-start(f32[65,8,128]{2,1,0:T(8,128)S(1)} %get-tuple-element.54), channel_id=1, source_target_pairs={{0,3},{1,2},{2,1},{3,0},{4,7},{5,6},{6,5},{7,4},{8,11},{9,10},{10,... | collective-permute-start | bytes 798728 | tf_op jit(solution)/shard_map/ppermute | solution.py:142
  47.3 0.0 collective-permute-done.13.refs_2_.refs_6_
  47.3 0.4 collective-permute-done.14.refs_3_.refs_7_
  47.7 0.1 last_plane.1
  47.8 2.3 %collective-permute-start.15 = (f32[5,2,32,128]{3,2,1,0:T(8,128)S(1)}, f32[5,2,32,128]{3,2,1,0:T(8,128)S(1)}, u32[]{:S(2)}, u32[]{:S(2)}) collective-permute-start(f32[5,2,32,128]{3,2,1,0:T(8,128)S(1)} %last_plane.1), channel_id=1, source_target_pairs={{0,4},{4,8},{8,12},{12,16},{16,20},{20,24},{24,28},{1,5},{5,9},{9,... | collective-permute-start | bytes 491528 | tf_op jit(solution)/shard_map/ppermute | solution.py:25
  50.1 0.6 %pad_maximum_fusion = f32[8,8,128]{2,1,0:T(8,128)} fusion(f32[2,8,128]{2,1,0:T(8,128)S(1)} %get-tuple-element.61, f32[4,8,128]{2,1,0:T(8,128)S(1)} %get-tuple-element.60, f32[2,8,128]{2,1,0:T(8,128)S(1)} %get-tuple-element.59), kind=kLoop, calls=%fused_computation | loop fusion | flops 16384 | bytes 65536 | tf_op jit(solution)/shard_map/concatenate | solution.py:588
  50.7 0.0 collective-permute-done.9.refs_1_.refs_9_
  50.7 2.2 %collective-permute-done.10.refs_2_.refs_10_ = f32[65,8,128]{2,1,0:T(8,128)S(1)} collective-permute-done((f32[65,8,128]{2,1,0:T(8,128)S(1)}, f32[65,8,128]{2,1,0:T(8,128)S(1)}, u32[]{:S(2)}, u32[]{:S(2)}) %collective-permute-start.10) | collective-permute-done | bytes 266272 | tf_op jit(solution)/shard_map/ppermute | solution.py:142
  52.9 6.2 %collective-permute-done.11.refs_3_.refs_11_ = f32[65,8,128]{2,1,0:T(8,128)S(1)} collective-permute-done((f32[65,8,128]{2,1,0:T(8,128)S(1)}, f32[65,8,128]{2,1,0:T(8,128)S(1)}, u32[]{:S(2)}, u32[]{:S(2)}) %collective-permute-start.11) | collective-permute-done | bytes 266272 | tf_op jit(solution)/shard_map/ppermute | solution.py:142
  59.1 0.0 collective-permute-done.15.refs_12_
  59.1 0.0 copy-done.2
  59.1 1.6 %residual.1 = f32[5,3,8,32,128]{4,3,2,1,0:T(8,128)} custom-call(s32[1]{0:T(128)} %bitcast.me_ref.refs_0_, f32[38,8,128]{2,1,0:T(8,128)S(1)} %get-tuple-element.38.refs_0_, f32[65,8,128]{2,1,0:T(8,128)S(1)} %collective-permute-done.9.refs_1_.refs_9_, f32[65,8,128]{2,1,0:T(8,128)S(1)} %collective-permute-done.10.refs_2_.refs_10_, ...), custom_call_target="tpu_custom_call" | custom-call | flops 1000 | bytes 1000 | tf_op jit(solution)/shard_map/residual/pallas_call | solution.py:546
  (4 shorter events, 0.0 us)
Async XLA Ops:
  0.6 14.6 %copy-start = (f32[5,3,8,32,128]{4,3,2,1,0:T(8,128)S(1)}, f32[5,3,8,32,128]{4,3,2,1,0:T(8,128)}, u32[]{:S(2)}) copy-start(f32[5,3,8,32,128]{4,3,2,1,0:T(8,128)} %state_ref.3) | copy-start | bytes 5898244
  4.5 10.7 %collective-permute-start.3 = (f32[2,5,2,32,128]{4,3,2,1,0:T(8,128)}, f32[2,5,2,32,128]{4,3,2,1,0:T(8,128)S(1)}, u32[]{:S(2)}, u32[]{:S(2)}) collective-permute-start(f32[2,5,2,32,128]{4,3,2,1,0:T(8,128)} %get-tuple-element.36), channel_id=1, source_target_pairs={{4,0},{8,4},{12,8},{16,12},{20,16},{24,20},{28,24},{5,1},{9,5},{13... | collective-permute-start | bytes 983048 | tf_op jit(solution)/shard_map/ppermute | solution.py:25
  7.5 14.6 %collective-permute-start = (f32[95,8,128]{2,1,0:T(8,128)}, f32[95,8,128]{2,1,0:T(8,128)S(1)}, u32[]{:S(2)}, u32[]{:S(2)}) collective-permute-start(f32[95,8,128]{2,1,0:T(8,128)} %get-tuple-element.33), channel_id=1, source_target_pairs={{0,1},{1,0},{2,3},{3,2},{4,5},{5,4},{6,7},{7,6},{8,9},{9,8},{10,11... | collective-permute-start | bytes 1167368 | tf_op jit(solution)/shard_map/ppermute | solution.py:142
  8.6 14.1 %collective-permute-start.1 = (f32[95,8,128]{2,1,0:T(8,128)}, f32[95,8,128]{2,1,0:T(8,128)S(1)}, u32[]{:S(2)}, u32[]{:S(2)}) collective-permute-start(f32[95,8,128]{2,1,0:T(8,128)} %get-tuple-element.34), channel_id=1, source_target_pairs={{0,2},{1,3},{2,0},{3,1},{4,6},{5,7},{6,4},{7,5},{8,10},{9,11},{10,... | collective-permute-start | bytes 1167368 | tf_op jit(solution)/shard_map/ppermute | solution.py:142
  9.8 18.5 %collective-permute-start.2 = (f32[95,8,128]{2,1,0:T(8,128)}, f32[95,8,128]{2,1,0:T(8,128)S(1)}, u32[]{:S(2)}, u32[]{:S(2)}) collective-permute-start(f32[95,8,128]{2,1,0:T(8,128)} %get-tuple-element.35), channel_id=1, source_target_pairs={{0,3},{1,2},{2,1},{3,0},{4,7},{5,6},{6,5},{7,4},{8,11},{9,10},{10,... | collective-permute-start | bytes 1167368 | tf_op jit(solution)/shard_map/ppermute | solution.py:142
  15.2 1.5 %copy-start.1 = (f32[5,3,8,32,128]{4,3,2,1,0:T(8,128)S(1)}, f32[5,3,8,32,128]{4,3,2,1,0:T(8,128)}, u32[]{:S(2)}) copy-start(f32[5,3,8,32,128]{4,3,2,1,0:T(8,128)} %adjoint_ref.3) | copy-start | bytes 5898244
  16.7 12.5 %copy-start.3 = (f32[8,32,128]{2,1,0:T(8,128)S(1)}, f32[8,32,128]{2,1,0:T(8,128)}, u32[]{:S(2)}) copy-start(f32[8,32,128]{2,1,0:T(8,128)} %refs_5_.5) | copy-start | bytes 393220
  16.7 12.5 %copy-start.4 = (s32[8,32,128]{2,1,0:T(8,128)S(1)}, s32[8,32,128]{2,1,0:T(8,128)}, u32[]{:S(2)}) copy-start(s32[8,32,128]{2,1,0:T(8,128)} %refs_6_.5) | copy-start | bytes 393220
  16.8 12.5 %copy-start.5 = (f32[95,8,128]{2,1,0:T(8,128)S(1)}, f32[95,8,128]{2,1,0:T(8,128)}, u32[]{:S(2)}) copy-start(f32[95,8,128]{2,1,0:T(8,128)} %get-tuple-element.32.refs_1_) | copy-start | bytes 1167364
  19.3 16.6 %collective-permute-start.4 = (f32[86,8,128]{2,1,0:T(8,128)S(1)}, f32[86,8,128]{2,1,0:T(8,128)S(1)}, u32[]{:S(2)}, u32[]{:S(2)}) collective-permute-start(f32[86,8,128]{2,1,0:T(8,128)S(1)} %get-tuple-element.39), channel_id=1, source_target_pairs={{0,1},{1,0},{2,3},{3,2},{4,5},{5,4},{6,7},{7,6},{8,9},{9,8},{10,11... | collective-permute-start | bytes 1056776 | tf_op jit(solution)/shard_map/ppermute | solution.py:142
  20.9 11.6 %collective-permute-start.7 = (f32[43,8,128]{2,1,0:T(8,128)S(1)}, f32[43,8,128]{2,1,0:T(8,128)S(1)}, u32[]{:S(2)}, u32[]{:S(2)}) collective-permute-start(f32[43,8,128]{2,1,0:T(8,128)S(1)} %get-tuple-element.47), channel_id=1, source_target_pairs={{0,2},{1,3},{2,0},{3,1},{4,6},{5,7},{6,4},{7,5},{8,10},{9,11},{10,... | collective-permute-start | bytes 528392 | tf_op jit(solution)/shard_map/ppermute | solution.py:142
  22.2 13.7 %collective-permute-start.8 = (f32[43,8,128]{2,1,0:T(8,128)S(1)}, f32[43,8,128]{2,1,0:T(8,128)S(1)}, u32[]{:S(2)}, u32[]{:S(2)}) collective-permute-start(f32[43,8,128]{2,1,0:T(8,128)S(1)} %get-tuple-element.48), channel_id=1, source_target_pairs={{0,3},{1,2},{2,1},{3,0},{4,7},{5,6},{6,5},{7,4},{8,11},{9,10},{10,... | collective-permute-start | bytes 528392 | tf_op jit(solution)/shard_map/ppermute | solution.py:142
  22.6 17.1 %collective-permute-start.5 = (f32[43,8,128]{2,1,0:T(8,128)S(1)}, f32[43,8,128]{2,1,0:T(8,128)S(1)}, u32[]{:S(2)}, u32[]{:S(2)}) collective-permute-start(f32[43,8,128]{2,1,0:T(8,128)S(1)} %get-tuple-element.40), channel_id=1, source_target_pairs={{0,2},{1,3},{2,0},{3,1},{4,6},{5,7},{6,4},{7,5},{8,10},{9,11},{10,... | collective-permute-start | bytes 528392 | tf_op jit(solution)/shard_map/ppermute | solution.py:142
  28.3 15.1 %collective-permute-start.6 = (f32[43,8,128]{2,1,0:T(8,128)S(1)}, f32[43,8,128]{2,1,0:T(8,128)S(1)}, u32[]{:S(2)}, u32[]{:S(2)}) collective-permute-start(f32[43,8,128]{2,1,0:T(8,128)S(1)} %get-tuple-element.41), channel_id=1, source_target_pairs={{0,3},{1,2},{2,1},{3,0},{4,7},{5,6},{6,5},{7,4},{8,11},{9,10},{10,... | collective-permute-start | bytes 528392 | tf_op jit(solution)/shard_map/ppermute | solution.py:142
  35.9 23.3 %copy-start.2 = (f32[5,3,8,32,128]{4,3,2,1,0:T(8,128)S(1)}, f32[5,3,8,32,128]{4,3,2,1,0:T(8,128)}, u32[]{:S(2)}) copy-start(f32[5,3,8,32,128]{4,3,2,1,0:T(8,128)} %refs_13_.1) | copy-start | bytes 5898244
  37.5 9.0 %collective-permute-start.12 = (f32[27,8,128]{2,1,0:T(8,128)S(1)}, f32[27,8,128]{2,1,0:T(8,128)S(1)}, u32[]{:S(2)}, u32[]{:S(2)}) collective-permute-start(f32[27,8,128]{2,1,0:T(8,128)S(1)} %get-tuple-element.55), channel_id=1, source_target_pairs={{0,1},{1,0},{2,3},{3,2},{4,5},{5,4},{6,7},{7,6},{8,9},{9,8},{10,11... | collective-permute-start | bytes 331784 | tf_op jit(solution)/shard_map/ppermute | solution.py:142
  37.6 9.7 %collective-permute-start.13 = (f32[27,8,128]{2,1,0:T(8,128)S(1)}, f32[27,8,128]{2,1,0:T(8,128)S(1)}, u32[]{:S(2)}, u32[]{:S(2)}) collective-permute-start(f32[27,8,128]{2,1,0:T(8,128)S(1)} %get-tuple-element.56), channel_id=1, source_target_pairs={{0,2},{1,3},{2,0},{3,1},{4,6},{5,7},{6,4},{7,5},{8,10},{9,11},{10,... | collective-permute-start | bytes 331784 | tf_op jit(solution)/shard_map/ppermute | solution.py:142
  38.9 8.8 %collective-permute-start.14 = (f32[27,8,128]{2,1,0:T(8,128)S(1)}, f32[27,8,128]{2,1,0:T(8,128)S(1)}, u32[]{:S(2)}, u32[]{:S(2)}) collective-permute-start(f32[27,8,128]{2,1,0:T(8,128)S(1)} %get-tuple-element.57), channel_id=1, source_target_pairs={{0,3},{1,2},{2,1},{3,0},{4,7},{5,6},{6,5},{7,4},{8,11},{9,10},{10,... | collective-permute-start | bytes 331784 | tf_op jit(solution)/shard_map/ppermute | solution.py:142
  45.1 5.6 %collective-permute-start.9 = (f32[65,8,128]{2,1,0:T(8,128)S(1)}, f32[65,8,128]{2,1,0:T(8,128)S(1)}, u32[]{:S(2)}, u32[]{:S(2)}) collective-permute-start(f32[65,8,128]{2,1,0:T(8,128)S(1)} %get-tuple-element.52), channel_id=1, source_target_pairs={{0,1},{1,0},{2,3},{3,2},{4,5},{5,4},{6,7},{7,6},{8,9},{9,8},{10,11... | collective-permute-start | bytes 798728 | tf_op jit(solution)/shard_map/ppermute | solution.py:142
  45.2 7.7 %collective-permute-start.10 = (f32[65,8,128]{2,1,0:T(8,128)S(1)}, f32[65,8,128]{2,1,0:T(8,128)S(1)}, u32[]{:S(2)}, u32[]{:S(2)}) collective-permute-start(f32[65,8,128]{2,1,0:T(8,128)S(1)} %get-tuple-element.53), channel_id=1, source_target_pairs={{0,2},{1,3},{2,0},{3,1},{4,6},{5,7},{6,4},{7,5},{8,10},{9,11},{10,... | collective-permute-start | bytes 798728 | tf_op jit(solution)/shard_map/ppermute | solution.py:142
  46.5 12.7 %collective-permute-start.11 = (f32[65,8,128]{2,1,0:T(8,128)S(1)}, f32[65,8,128]{2,1,0:T(8,128)S(1)}, u32[]{:S(2)}, u32[]{:S(2)}) collective-permute-start(f32[65,8,128]{2,1,0:T(8,128)S(1)} %get-tuple-element.54), channel_id=1, source_target_pairs={{0,3},{1,2},{2,1},{3,0},{4,7},{5,6},{6,5},{7,4},{8,11},{9,10},{10,... | collective-permute-start | bytes 798728 | tf_op jit(solution)/shard_map/ppermute | solution.py:142
  47.8 11.3 %collective-permute-start.15 = (f32[5,2,32,128]{3,2,1,0:T(8,128)S(1)}, f32[5,2,32,128]{3,2,1,0:T(8,128)S(1)}, u32[]{:S(2)}, u32[]{:S(2)}) collective-permute-start(f32[5,2,32,128]{3,2,1,0:T(8,128)S(1)} %last_plane.1), channel_id=1, source_target_pairs={{0,4},{4,8},{8,12},{12,16},{16,20},{20,24},{24,28},{1,5},{5,9},{9,... | collective-permute-start | bytes 491528 | tf_op jit(solution)/shard_map/ppermute | solution.py:25
